TPU v7x, 32 devices: a whole 2x2x4 slice. The times are simulated.
32 devices in a mesh: fsdp: 16 (over z, y, x), rep: 2 (over core).
Axes of the slice: x: 2, y: 2, z: 4, core: 2. Of those that a mesh axis runs over, the one named last changes fastest.
Arguments:
- tokens: bfloat16 [32768, 768], P(('fsdp', 'rep')), may hold values from -6 to 6
- doc_ids: int32 [32768], P(('fsdp', 'rep')), may hold values from 0 to 3, as said below
- cotangent: bfloat16 [32768, 768], P(('fsdp', 'rep')), may hold values from -6 to 6
- attn_weights: float32 [768, 3072], P('fsdp'), may hold values from -0.8660254 to 0.8660254, as said below
- mlp_weights: float32 [768, 6144], P('fsdp'), may hold values from -0.21875 to 0.21875
- gains: float32 [2, 768], P(None, 'fsdp'), may hold values from 0.5 to 1.5
- moment_attn: float32 [768, 3072], P('fsdp'), may hold values from -320 to 320
- moment_mlp: float32 [768, 6144], P('fsdp'), may hold values from -320 to 320
- moment_gains: float32 [2, 768], P(None, 'fsdp'), may hold values from -1024 to 1024
- ema_attn: float32 [768, 3072], P('fsdp'), may hold values from -0.21875 to 0.21875
- ema_mlp: float32 [768, 6144], P('fsdp'), may hold values from -0.21875 to 0.21875
- ema_gains: float32 [2, 768], P(None, 'fsdp'), may hold values from 0.5 to 1.5
Outputs:
- block_out: bfloat16 [32768, 768], P(('fsdp', 'rep'))
- input_grad: bfloat16 [32768, 768], P(('fsdp', 'rep'))
- grad_attn: float32 [768, 3072], P('fsdp')
- grad_mlp: float32 [768, 6144], P('fsdp')
- grad_gains: float32 [2, 768], P(None, 'fsdp')
- next_attn: float32 [768, 3072], P('fsdp')
- next_mlp: float32 [768, 6144], P('fsdp')
- next_gains: float32 [2, 768], P(None, 'fsdp')
- velocity_attn: float32 [768, 3072], P('fsdp')
- velocity_mlp: float32 [768, 6144], P('fsdp')
- velocity_gains: float32 [2, 768], P(None, 'fsdp')
- average_attn: float32 [768, 3072], P('fsdp')
- average_mlp: float32 [768, 6144], P('fsdp')
- average_gains: float32 [2, 768], P(None, 'fsdp')
- copy_attn: bfloat16 [768, 3072], P('fsdp')
- copy_mlp: bfloat16 [768, 6144], P('fsdp')
- copy_gains: bfloat16 [2, 768], P(None, 'fsdp')
Inputs may be any that keep to these rules, and one draw needn't show every extreme that they name: `doc_ids`: within each device's 1024 tokens the numbers start at 0 and never fall; a document holds 256, 512 or 1024 tokens; some device holds a single document and another holds four. `attn_weights`: independent entries; the last 768 columns are four times larger than the others.
All inputs are finite; a program needn't handle non-finite values.
Results may differ from a plain program's by a relative error of at most 0.015.
The roundings to bfloat16 on the way count: a program that leaves them out, or rounds other values in their place, can miss the bound.
Values may be sent and summed in bfloat16 or wider, within the bound.
A program may use at most 256 MiB of HBM per device.

v0:
```python
import math

import jax
import jax.numpy as jnp
from jax import lax
from jax.sharding import PartitionSpec as P

HEAD = 64
STEP = 5
WARMUP = 10


EPSILON = 1e-05
MASKED = -1e30
MOMENTUM = 0.5
DECAY = 0.5
PEAK_RATE = 0.1
LANES = 128


def doc_positions(doc_block):
    row_count = doc_block.shape[0]
    places = jnp.arange(row_count, dtype=jnp.int32)
    boundary = jnp.concatenate(
        [jnp.ones((1,), jnp.int32), (doc_block[1:] != doc_block[:-1]).astype(jnp.int32)]
    )
    starts = lax.cummax(places * boundary, axis=0)
    return places - starts


def rotary_tables(positions):
    half_size = HEAD // 2
    frequency = 10000.0 ** (-jnp.arange(half_size, dtype=jnp.float32) / half_size)
    angles = positions.astype(jnp.float32)[:, None] * frequency[None, :]
    return (jnp.cos(angles)[:, None, :], jnp.sin(angles)[:, None, :])


def rotate(tensor, cosine, sine):
    half_size = tensor.shape[-1] // 2
    first_half = tensor[..., :half_size]
    second_half = tensor[..., half_size:]
    return jnp.concatenate(
        [first_half * cosine - second_half * sine, second_half * cosine + first_half * sine],
        axis=-1,
    )


def rms_scale(tensor):
    return lax.rsqrt(jnp.mean(tensor * tensor, axis=-1, keepdims=True) + EPSILON)


def norm_back(grad_normed, unit_rows, scale_rows, gain_row):
    grad_unit = grad_normed * gain_row
    gain_grad = jnp.sum(grad_normed * unit_rows, axis=0)
    grad_field = scale_rows * (
        grad_unit - unit_rows * jnp.mean(grad_unit * unit_rows, axis=-1, keepdims=True)
    )
    return (grad_field, gain_grad)


def over_rows(left, right):
    return lax.dot_general(
        left, right, (((0,), (0,)), ((), ())), preferred_element_type=jnp.float32
    )


def over_columns(left, right):
    return lax.dot_general(
        left, right, (((1,), (1,)), ((), ())), preferred_element_type=jnp.float32
    )


def as_slab(matrix):
    return matrix.reshape(matrix.shape[0] * matrix.shape[1] // LANES, LANES)


def local(
    tokens,
    doc_ids,
    cotangent,
    attn_weights,
    mlp_weights,
    gains,
    moment_attn,
    moment_mlp,
    moment_gains,
    ema_attn,
    ema_mlp,
    ema_gains,
):
    row_count, model_width = tokens.shape
    head_count = model_width // HEAD
    hidden_width = mlp_weights.shape[1] // 3
    shape_heads = (row_count, head_count, HEAD)
    attn_low = attn_weights.astype(jnp.bfloat16)
    mlp_low = mlp_weights.astype(jnp.bfloat16)
    gain_low = gains.astype(jnp.bfloat16)
    attn_full, mlp_full, gain_full = (
        lax.all_gather(attn_low, "fsdp", axis=0, tiled=True),
        lax.all_gather(mlp_low, "fsdp", axis=0, tiled=True),
        lax.all_gather(gain_low, "fsdp", axis=1, tiled=True),
    )
    gain_one = gain_full[0].astype(jnp.float32)
    gain_two = gain_full[1].astype(jnp.float32)
    cosine, sine = rotary_tables(doc_positions(doc_ids))
    stream = tokens.astype(jnp.float32)
    scale_one = rms_scale(stream)
    unit_one = stream * scale_one
    normed_one = (unit_one * gain_one).astype(jnp.bfloat16)
    projected = jnp.dot(
        normed_one, attn_full[:, : 3 * model_width], preferred_element_type=jnp.float32
    )
    queries = rotate(projected[:, :model_width].reshape(shape_heads), cosine, sine).astype(
        jnp.bfloat16
    )
    key_rows = rotate(
        projected[:, model_width : 2 * model_width].reshape(shape_heads), cosine, sine
    ).astype(jnp.bfloat16)
    values = projected[:, 2 * model_width :].reshape(shape_heads).astype(jnp.bfloat16)
    block_rows = min(512, row_count)
    places = jnp.arange(row_count, dtype=jnp.int32)

    def masked_scores(first_row, last_row):
        scores = (
            jnp.einsum(
                "qhe,khe->hqk",
                queries[first_row:last_row],
                key_rows[:last_row],
                preferred_element_type=jnp.float32,
            )
            * 0.125
        )
        allowed = (places[first_row:last_row, None] >= places[None, :last_row]) & (
            doc_ids[first_row:last_row, None] == doc_ids[None, :last_row]
        )
        return jnp.where(allowed[None], scores, MASKED)

    mixed_pieces = []
    log_sums = []
    for first_row in range(0, row_count, block_rows):
        last_row = first_row + block_rows
        scores = masked_scores(first_row, last_row)
        top_score = jnp.max(scores, axis=-1, keepdims=True)
        shifted_exp = jnp.exp(scores - top_score)
        exp_total = jnp.sum(shifted_exp, axis=-1, keepdims=True)
        attn_probs = (shifted_exp / exp_total).astype(jnp.bfloat16)
        mixed_pieces.append(
            jnp.einsum(
                "hqk,khe->qhe", attn_probs, values[:last_row], preferred_element_type=jnp.float32
            )
        )
        log_sums.append(top_score + jnp.log(exp_total))
    mixed = (
        jnp.concatenate(mixed_pieces, axis=0).reshape(row_count, model_width).astype(jnp.bfloat16)
    )
    after_attn = stream + jnp.dot(
        mixed, attn_full[:, 3 * model_width :], preferred_element_type=jnp.float32
    )
    scale_two = rms_scale(after_attn)
    unit_two = after_attn * scale_two
    normed_two = (unit_two * gain_two).astype(jnp.bfloat16)
    gate_up = jnp.dot(
        normed_two, mlp_full[:, : 2 * hidden_width], preferred_element_type=jnp.float32
    )
    gate_pre = gate_up[:, :hidden_width]
    up_pre = gate_up[:, hidden_width:]
    sigmoid_gate = jax.nn.sigmoid(gate_pre)
    silu_gate = gate_pre * sigmoid_gate
    hidden = (silu_gate * up_pre).astype(jnp.bfloat16)
    block_total = after_attn + over_columns(hidden, mlp_full[:, 2 * hidden_width :])
    block_out = block_total.astype(jnp.bfloat16)
    attn_back, mlp_back, gain_back = (
        lax.all_gather(attn_low, "fsdp", axis=0, tiled=True),
        lax.all_gather(mlp_low, "fsdp", axis=0, tiled=True),
        lax.all_gather(gain_low, "fsdp", axis=1, tiled=True),
    )
    grad_stream = cotangent.astype(jnp.float32)
    d_hidden = jnp.dot(
        cotangent, mlp_back[:, 2 * hidden_width :], preferred_element_type=jnp.float32
    )
    grad_down = over_rows(cotangent, hidden)
    d_gate = (d_hidden * up_pre * sigmoid_gate * (1.0 + gate_pre * (1.0 - sigmoid_gate))).astype(
        jnp.bfloat16
    )
    d_up = (d_hidden * silu_gate).astype(jnp.bfloat16)
    d_gate_up = jnp.concatenate([d_gate, d_up], axis=1)
    grad_gate_up = over_rows(normed_two, d_gate_up)
    d_normed_two = over_columns(d_gate_up, mlp_back[:, : 2 * hidden_width])
    grad_field_two, gain_grad_two = norm_back(
        d_normed_two, unit_two, scale_two, gain_back[1].astype(jnp.float32)
    )
    grad_after = grad_stream + grad_field_two
    d_branch = grad_after.astype(jnp.bfloat16)
    grad_out_proj = over_rows(mixed, d_branch)
    d_mixed = (
        over_columns(d_branch, attn_back[:, 3 * model_width :])
        .astype(jnp.bfloat16)
        .reshape(shape_heads)
    )
    query_grads = []
    key_grads = jnp.zeros(shape_heads, jnp.float32)
    value_grads = jnp.zeros(shape_heads, jnp.float32)
    for block_index, first_row in enumerate(range(0, row_count, block_rows)):
        last_row = first_row + block_rows
        scores = masked_scores(first_row, last_row)
        attn_probs = jnp.exp(scores - log_sums[block_index])
        grad_probs = jnp.einsum(
            "qhe,khe->hqk",
            d_mixed[first_row:last_row],
            values[:last_row],
            preferred_element_type=jnp.float32,
        )
        inner_sum = jnp.sum(attn_probs * grad_probs, axis=-1, keepdims=True)
        grad_scores = (attn_probs * (grad_probs - inner_sum)).astype(jnp.bfloat16)
        query_grads.append(
            jnp.einsum(
                "hqk,khe->qhe", grad_scores, key_rows[:last_row], preferred_element_type=jnp.float32
            )
            * 0.125
        )
        key_grads = key_grads.at[:last_row].add(
            jnp.einsum(
                "hqk,qhe->khe",
                grad_scores,
                queries[first_row:last_row],
                preferred_element_type=jnp.float32,
            )
            * 0.125
        )
        value_grads = value_grads.at[:last_row].add(
            jnp.einsum(
                "hqk,qhe->khe",
                attn_probs.astype(jnp.bfloat16),
                d_mixed[first_row:last_row],
                preferred_element_type=jnp.float32,
            )
        )
    query_grad = (
        rotate(jnp.concatenate(query_grads, axis=0), cosine, -sine)
        .reshape(row_count, model_width)
        .astype(jnp.bfloat16)
    )
    key_grad = rotate(key_grads, cosine, -sine).reshape(row_count, model_width).astype(jnp.bfloat16)
    value_grad = value_grads.reshape(row_count, model_width).astype(jnp.bfloat16)
    d_projected = jnp.concatenate([query_grad, key_grad, value_grad], axis=1)
    grad_qkv = over_rows(normed_one, d_projected)
    d_normed_one = over_columns(d_projected, attn_back[:, : 3 * model_width])
    grad_field_one, gain_grad_one = norm_back(
        d_normed_one, unit_one, scale_one, gain_back[0].astype(jnp.float32)
    )
    input_grad = (grad_after + grad_field_one).astype(jnp.bfloat16)
    full_attn = as_slab(jnp.concatenate([grad_qkv, grad_out_proj], axis=1))
    full_mlp = as_slab(jnp.concatenate([grad_gate_up, grad_down], axis=1))
    full_gains = jnp.stack([gain_grad_one, gain_grad_two], axis=0)
    part_attn, part_mlp, part_gains = (
        lax.psum_scatter(full_attn, "fsdp", scatter_dimension=0, tiled=True),
        lax.psum_scatter(full_mlp, "fsdp", scatter_dimension=0, tiled=True),
        lax.psum_scatter(full_gains, "fsdp", scatter_dimension=1, tiled=True),
    )
    slab_attn, slab_mlp, grad_gains = (
        lax.psum(part_attn.astype(jnp.bfloat16), "rep").astype(jnp.float32),
        lax.psum(part_mlp.astype(jnp.bfloat16), "rep").astype(jnp.float32),
        lax.psum(part_gains.astype(jnp.bfloat16), "rep").astype(jnp.float32),
    )
    grad_attn = slab_attn.reshape(attn_weights.shape)
    grad_mlp = slab_mlp.reshape(mlp_weights.shape)
    total_tokens = row_count * lax.axis_size("fsdp") * lax.axis_size("rep")
    rate = PEAK_RATE * STEP / (WARMUP * math.sqrt(total_tokens))

    def update(weight, grad, moment, average):
        velocity = MOMENTUM * moment + grad
        weight_new = weight - rate * (grad + MOMENTUM * velocity)
        average_new = DECAY * average + (1.0 - DECAY) * weight_new
        return (weight_new, velocity, average_new, weight_new.astype(jnp.bfloat16))

    next_attn, velocity_attn, average_attn, copy_attn = update(
        attn_weights, grad_attn, moment_attn, ema_attn
    )
    next_mlp, velocity_mlp, average_mlp, copy_mlp = update(
        mlp_weights, grad_mlp, moment_mlp, ema_mlp
    )
    next_gains, velocity_gains, average_gains, copy_gains = update(
        gains, grad_gains, moment_gains, ema_gains
    )
    return (
        block_out,
        input_grad,
        grad_attn,
        grad_mlp,
        grad_gains,
        next_attn,
        next_mlp,
        next_gains,
        velocity_attn,
        velocity_mlp,
        velocity_gains,
        average_attn,
        average_mlp,
        average_gains,
        copy_attn,
        copy_mlp,
        copy_gains,
    )


def solution(mesh):
    return jax.shard_map(
        local,
        mesh=mesh,
        in_specs=(
            P(("fsdp", "rep"), None),
            P(("fsdp", "rep")),
            P(("fsdp", "rep"), None),
            P("fsdp", None),
            P("fsdp", None),
            P(None, "fsdp"),
            P("fsdp", None),
            P("fsdp", None),
            P(None, "fsdp"),
            P("fsdp", None),
            P("fsdp", None),
            P(None, "fsdp"),
        ),
        out_specs=(
            P(("fsdp", "rep"), None),
            P(("fsdp", "rep"), None),
            P("fsdp", None),
            P("fsdp", None),
            P(None, "fsdp"),
            P("fsdp", None),
            P("fsdp", None),
            P(None, "fsdp"),
            P("fsdp", None),
            P("fsdp", None),
            P(None, "fsdp"),
            P("fsdp", None),
            P("fsdp", None),
            P(None, "fsdp"),
            P("fsdp", None),
            P("fsdp", None),
            P(None, "fsdp"),
        ),
        check_vma=False,
    )
```

profile of v0, /device:TPU:0, one launch (start us, length us, event | category | flops | bytes accessed | tf_op | source)
XLA Modules:
  0.0 1025.7 jit_solution(8497044591032346008)
XLA Ops:
  7.3 1.9 convert_element_type.124
  9.3 2.1 convert_element_type.131
  12.1 42.3 %all-gather = bf16[16,48,2]{1,2,0:T(2,128)(2,1)S(1)} all-gather(bf16[1,48,2]{1,2,0:T(2,128)(2,1)S(1)} %convert_bitcast_fusion), channel_id=1, replica_groups=mesh['fsdp'=16,'rep'=2] {'fsdp'}, dimensions={0}, use_global_device_ids=true | all-gather | bytes 3264 | tf_op jit(solution)/shard_map/all_gather | solution.py:101
  55.3 3.2 copy.80
  59.4 1.2 fusion.65
  61.1 33.5 %all-gather.4.cloned.1.call-done = bf16[768,3072]{1,0:T(8,128)(2,1)} async-done(((bf16[48,3072]{1,0:T(8,128)(2,1)}), bf16[768,3072]{1,0:T(8,128)(2,1)}) %all-gather.4.cloned.1.call-update) | async-done | bytes 4718608 | tf_op jit(solution)/shard_map/all_gather | solution.py:99
  94.6 6.1 fusion.94
  101.7 1.2 slice.262
  102.9 3.1 fusion.91
  106.0 3.7 copy.75
  109.7 2.6 copy.78
  112.3 1.4 copy.74
  113.7 3.6 copy.76
  117.3 3.9 subtract_convert_fusion.3
  121.2 2.1 fusion.23
  123.4 11.4 %fusion.8 = (f32[12,512]{1,0:T(8,128)S(1)}, f32[12,512,1024]{2,1,0:T(8,128)}) fusion(pred[512,1024]{1,0:T(8,128)(4,1)S(1)} %fusion.41, bf16[1024,12,32]{0,2,1:T(8,128)(2,1)S(1)} %get-tuple-element.169, bf16[1024,12,32]{0,2,1:T(8,128)(2,1)S(1)} %get-tuple-element.170, bf16[1024,12,32]{0,2,1:T(8,128)(2,1)S(1)} %get-tuple-element.162, ...), kind=kOutput, calls=%fused_computation.21 | convolution fusion | flops 828893184 | bytes 28860416 | tf_op jit(solution)/shard_map/qhe,khe->hqk/dot_general | solution.py:125
  135.7 2.6 fusion.6
  138.3 13.3 %fusion = f32[12,512]{1,0:T(8,128)S(1)} fusion(f32[12,512]{1,0:T(8,128)S(1)} %get-tuple-element.178, f32[12,512,1024]{2,1,0:T(8,128)} %get-tuple-element.179, pred[512,1024]{1,0:T(8,128)(4,1)S(1)} %fusion.41), kind=kLoop, calls=%fused_computation.6 | loop fusion | flops 25159680 | bytes 25739264 | tf_op jit(solution)/shard_map/reduce_sum | solution.py:145
  151.6 7.7 fusion.54
  160.1 1.2 slice-done.5
  161.7 8.5 fusion.53
  170.2 1.6 pad_maximum_fusion.10
  171.8 5.1 multiply_reduce_fusion.4
  177.0 42.2 %all-gather.6.cloned.1.call-done = bf16[768,6144]{1,0:T(8,128)(2,1)} async-done(((bf16[48,6144]{1,0:T(8,128)(2,1)}), bf16[768,6144]{1,0:T(8,128)(2,1)}) %all-gather.6.cloned.1.call-update) | async-done | bytes 9437200 | tf_op jit(solution)/shard_map/all_gather | solution.py:100
  219.2 25.4 %fusion.16 = f32[1024,4096]{1,0:T(8,128)} fusion(bf16[768,6144]{1,0:T(8,128)(2,1)} %all-gather.6.cloned.1.call-done, f32[1024,768]{0,1:T(8,128)} %get-tuple-element.183, f32[768]{0:T(1024)S(1)} %get-tuple-element.136, f32[1024]{0:T(1024)S(1)} %add_rsqrt_fusion), kind=kOutput, calls=%fused_computation.33 | convolution fusion | flops 6444810240 | bytes 26221568 | tf_op jit(solution)/shard_map/dot_general | solution.py:162
  244.6 13.0 %multiply_convert_fusion.3 = (bf16[1024,2048]{1,0:T(8,128)(2,1)S(1)}, bf16[1024,2048]{1,0:T(8,128)(2,1)}, bf16[1024,2048]{1,0:T(8,128)(2,1)}) fusion(f32[1024,4096]{1,0:T(8,128)} %fusion.16, bf16[1024,768]{1,0:T(8,128)(2,1)S(1)} %copy-done.24, bf16[768,6144]{1,0:T(8,128)(2,1)} %all-gather.6.cloned.1.call-done), kind=kOutput, calls=%fused_computation.24 | convolution fusion | flops 3252682752 | bytes 34078720 | tf_op jit(solution)/shard_map/dot_general | solution.py:178
  257.6 13.2 %multiply_reduce_fusion.2 = (f32[768]{0:T(1024)}, f32[1024]{0:T(1024)S(1)}, f32[1024,768]{0,1:T(8,128)S(1)}) fusion(f32[1024,768]{0,1:T(8,128)S(1)} %copy-done.15, f32[1024]{0:T(1024)S(1)} %add_rsqrt_fusion, f32[768]{0:T(1024)S(1)} %get-tuple-element.136, bf16[768,6144]{1,0:T(8,128)(2,1)} %all-gather.6.cloned.1.call-done, ...), kind=kOutput, calls=%fused_computation.59 | convolution fusion | flops 6463944704 | bytes 20985856 | tf_op jit(solution)/shard_map/dot_general | solution.py:68
  272.2 2.9 fusion.59
  275.1 3.5 convolution_convert_fusion
  279.6 4.0 fusion.48
  283.6 6.8 multiply_reduce_fusion.1
  290.4 7.4 multiply_convert_fusion.1
  297.9 3.2 multiply_bitcast_fusion
  301.1 2.3 multiply_bitcast_fusion.2
  303.5 18.2 %multiply_reduce_fusion = (f32[12,512]{1,0:T(8,128)S(1)}, f32[12,512,1024]{2,1,0:T(8,128)}) fusion(f32[12,512]{1,0:T(8,128)S(1)} %log_add_fusion, f32[12,512,1024]{2,1,0:T(8,128)} %get-tuple-element.179, pred[512,1024]{1,0:T(8,128)(4,1)} %copy-done.11, bf16[512,12,64]{0,2,1:T(8,128)(2,1)} %bitcast.77, bf16[1024,12,64]{0,2,1:T(8,128)(2,1)} %bitcast.71), kind=kOutput, calls=%fused_computation.1 | convolution fusion | flops 836757504 | bytes 53264384 | tf_op jit(solution)/shard_map/qhe,khe->hqk/dot_general | solution.py:207
  321.7 12.5 %fusion.32 = bf16[1024,12,64]{0,2,1:T(8,128)(2,1)S(1)} fusion(f32[512,12,64]{0,2,1:T(8,128)} %fusion.48, bf16[512,12,64]{0,2,1:T(8,128)(2,1)} %bitcast.78, f32[12,512]{1,0:T(8,128)S(1)} %log_add_fusion, f32[12,512,1024]{2,1,0:T(8,128)} %get-tuple-element.179, pred[512,1024]{1,0:T(8,128)(4,1)} %copy-done.11), kind=kOutput, calls=%fused_computation.57 | convolution fusion | flops 832045056 | bytes 29646848 | tf_op jit(solution)/shard_map/hqk,qhe->khe/dot_general | solution.py:231
  334.2 21.9 %multiply_convert_fusion = bf16[12,512,1024]{2,1,0:T(8,128)(2,1)} fusion(f32[12,512,1024]{2,1,0:T(8,128)} %get-tuple-element.186, f32[12,512]{1,0:T(8,128)S(1)} %get-tuple-element.185, f32[12,512]{1,0:T(8,128)S(1)} %log_add_fusion, f32[12,512,1024]{2,1,0:T(8,128)} %get-tuple-element.179, pred[512,1024]{1,0:T(8,128)(4,1)S(1)} %copy-done.12), kind=kLoop, calls=%fused_computation | loop fusion | flops 37748736 | bytes 63488000 | tf_op jit(solution)/shard_map/convert_element_type | solution.py:214
  356.1 8.6 multiply_bitcast_fusion.1
  364.7 7.1 bitcast_add_fusion.1
  373.4 1.1 copy-done.28
  375.1 9.0 fusion.42
  384.0 8.7 pad_maximum_fusion.1
  392.7 10.9 %reshape.452 = f32[18432,128]{1,0:T(8,128)} reshape(f32[768,3072]{1,0:T(8,128)} %pad_maximum_fusion.1) | data formatting | bytes 18874368 | tf_op jit(solution)/shard_map/reshape | solution.py:74
  403.7 1.3 copy-done.25
  405.0 8.0 convolution_bitcast_fusion
  413.0 9.4 fusion.18
  422.5 9.6 pad_maximum_fusion
  432.0 19.5 %reshape.455 = f32[36864,128]{1,0:T(8,128)} reshape(f32[768,6144]{1,0:T(8,128)} %pad_maximum_fusion) | data formatting | bytes 37748736 | tf_op jit(solution)/shard_map/reshape | solution.py:74
  452.9 8.9 fusion.30
  462.8 7.8 add_convert_fusion
  470.6 1.8 copy.90
  472.4 100.5 %reduce-scatter.6.cloned.1.call-done = f32[1152,128]{1,0:T(8,128)} async-done(((f32[18432,128]{1,0:T(8,128)}), f32[1152,128]{1,0:T(8,128)}) %reduce-scatter.6.cloned.1.call-update) | async-done | bytes 589840 | tf_op jit(solution)/shard_map/reduce_scatter | solution.py:256
  573.0 1.1 convert_element_type.148
  574.9 289.0 %reduce-scatter.8.cloned.1.call-done = f32[2304,128]{1,0:T(8,128)} async-done(((f32[36864,128]{1,0:T(8,128)}), f32[2304,128]{1,0:T(8,128)}) %reduce-scatter.8.cloned.1.call-update) | async-done | bytes 1179664 | tf_op jit(solution)/shard_map/reduce_scatter | solution.py:257
  863.9 1.3 convert_element_type.149
  865.2 1.1 reshape.456
  866.3 3.6 fusion.29
  870.0 1.6 copy.91
  871.6 118.6 %reduce-scatter.10.cloned.1.call-done = f32[48,2]{1,0:T(8,128)} async-done(((f32[768,2]{1,0:T(8,128)}), f32[48,2]{1,0:T(8,128)}) %reduce-scatter.10.cloned.1.call-update) | async-done | bytes 400
  991.0 2.5 psum.23
  994.6 16.9 %all-reduce.5.cloned.1.call-done = (bf16[48,3072]{1,0:T(8,128)(2,1)}, bf16[48,6144]{1,0:T(8,128)(2,1)}) async-done(((bf16[48,3072]{1,0:T(8,128)(2,1)}, bf16[48,6144]{1,0:T(8,128)(2,1)}), (bf16[48,3072]{1,0:T(8,128)(2,1)}, bf16[48,6144]{1,0:T(8,128)(2,1)})) %all-reduce.5.cloned.1.call-update) | async-done | bytes 884752 | tf_op jit(solution)/shard_map/psum | solution.py:261
  1011.5 2.6 fusion.90
  1015.2 1.9 fusion.89
  1017.1 1.3 add_multiply_fusion
  (172 shorter events, 17.0 us)
Async XLA Ops:
  7.2 4.3 copy-start.38
  7.2 4.9 copy-start.46
  7.2 47.3 %copy-start.23 = (bf16[1024,768]{1,0:T(8,128)(2,1)S(1)}, bf16[1024,768]{1,0:T(8,128)(2,1)}, u32[]{:S(2)}) copy-start(bf16[1024,768]{1,0:T(8,128)(2,1)} %param.24) | copy-start | bytes 4718596
  7.2 87.4 %all-gather.4.cloned.1.call-start = ((), (), s32[]{:S(2)}) async-start(), calls=%async_computation.3 | async-start | bytes 5013504 | tf_op jit(solution)/shard_map/all_gather | solution.py:99
  9.2 210.0 %all-gather.6.cloned.1.call-start = ((), (), s32[]{:S(2)}) async-start(), calls=%async_computation.4 | async-start | bytes 10027008 | tf_op jit(solution)/shard_map/all_gather | solution.py:100
  11.4 561.5 %reduce-scatter.6.cloned.1.call-start = ((), (), s32[]{:S(2)}) async-start(), calls=%async_computation.5 | async-start | bytes 10027008 | tf_op jit(solution)/shard_map/reduce_scatter | solution.py:256
  55.3 116.5 %copy-start.9 = (bf16[1024,768]{0,1:T(8,128)(2,1)}, bf16[1024,768]{0,1:T(8,128)(2,1)S(1)}, u32[]{:S(2)}) copy-start(bf16[1024,768]{0,1:T(8,128)(2,1)S(1)} %copy.72) | copy-start | bytes 4718596
  58.6 42.1 %copy-start.39 = (f32[768]{0:T(1024)}, f32[768]{0:T(1024)S(1)}, u32[]{:S(2)}) copy-start(f32[768]{0:T(1024)S(1)} %get-tuple-element.137) | copy-start | bytes 9220
  59.0 41.7 %copy-start.41 = (f32[1024]{0:T(1024)}, f32[1024]{0:T(1024)S(1)}, u32[]{:S(2)}) copy-start(f32[1024]{0:T(1024)S(1)} %add_rsqrt_fusion.1) | copy-start | bytes 12292
  60.6 56.7 %copy-start.31 = (f32[1024,32]{0,1:T(8,128)}, f32[1024,32]{0,1:T(8,128)S(1)}, u32[]{:S(2)}) copy-start(f32[1024,32]{0,1:T(8,128)S(1)} %get-tuple-element.173) | copy-start | bytes 393220
  61.1 98.2 %copy-start.11 = (pred[512,1024]{1,0:T(8,128)(4,1)}, pred[512,1024]{1,0:T(8,128)(4,1)S(1)}, u32[]{:S(2)}) copy-start(pred[512,1024]{1,0:T(8,128)(4,1)S(1)} %fusion.41) | copy-start | bytes 1572868
  121.2 2.2 copy-start.1
  121.2 2.2 copy-start.3
  121.2 2.2 copy-start.5
  121.2 2.2 copy-start.7
  123.4 12.3 %copy-start = (f32[12,512,512]{1,2,0:T(8,128)}, f32[12,512,512]{1,2,0:T(8,128)S(1)}, u32[]{:S(2)}) copy-start(f32[12,512,512]{1,2,0:T(8,128)S(1)} %get-tuple-element.181) | copy-start | bytes 37748740
  138.3 21.0 %slice-start = ((s8[25165824]{0:T(1024)(128)(4,1)}), s8[4194304]{0:T(1024)(128)(4,1)S(1)}, s32[]{:S(2)}) async-start(s8[25165824]{0:T(1024)(128)(4,1)} %bitcast.65), calls=%async_computation.9 | async-start | bytes 8388608
  138.3 21.0 %slice-start.1 = ((s8[25165824]{0:T(1024)(128)(4,1)}), s8[4194304]{0:T(1024)(128)(4,1)S(1)}, s32[]{:S(2)}) async-start(s8[25165824]{0:T(1024)(128)(4,1)} %bitcast.65), calls=%async_computation.10 | async-start | bytes 8388608
  151.6 7.7 slice-start.2
  151.6 7.7 slice-start.3
  151.6 8.5 slice-start.4
  151.6 9.7 slice-start.5
  151.6 10.1 copy-start.17
  171.8 5.1 copy-start.26
  219.2 25.4 %copy-start.24 = (bf16[1024,768]{1,0:T(8,128)(2,1)S(1)}, bf16[1024,768]{1,0:T(8,128)(2,1)}, u32[]{:S(2)}) copy-start(bf16[1024,768]{1,0:T(8,128)(2,1)} %param.26) | copy-start | bytes 4718596
  244.6 13.0 %copy-start.15 = (f32[1024,768]{0,1:T(8,128)S(1)}, f32[1024,768]{0,1:T(8,128)}, u32[]{:S(2)}) copy-start(f32[1024,768]{0,1:T(8,128)} %get-tuple-element.183) | copy-start | bytes 9437188
  257.6 13.2 %copy-start.50 = (bf16[1024,2048]{1,0:T(8,128)(2,1)}, bf16[1024,2048]{1,0:T(8,128)(2,1)S(1)}, u32[]{:S(2)}) copy-start(bf16[1024,2048]{1,0:T(8,128)(2,1)S(1)} %get-tuple-element.152) | copy-start | bytes 12582916
  257.6 13.2 %copy-start.19 = (bf16[1024,768]{0,1:T(8,128)(2,1)S(1)}, bf16[1024,768]{0,1:T(8,128)(2,1)}, u32[]{:S(2)}) copy-start(bf16[1024,768]{0,1:T(8,128)(2,1)} %copy.80) | copy-start | bytes 4718596
  270.8 1.4 copy-start.27
  272.2 2.9 copy-start.14
  272.2 7.4 slice-start.6
  272.2 7.4 slice-start.7
  275.1 4.5 slice-start.8
  290.4 7.5 copy-start.2
  290.4 7.5 copy-start.4
  297.9 3.2 copy-start.6
  297.9 3.2 copy-start.8
  321.7 12.5 %copy-start.12 = (pred[512,1024]{1,0:T(8,128)(4,1)S(1)}, pred[512,1024]{1,0:T(8,128)(4,1)}, u32[]{:S(2)}) copy-start(pred[512,1024]{1,0:T(8,128)(4,1)} %copy-done.11) | copy-start | bytes 1572868
  334.2 39.2 %copy-start.49 = (bf16[1024,12,64]{0,2,1:T(8,128)(2,1)}, bf16[1024,12,64]{0,2,1:T(8,128)(2,1)S(1)}, u32[]{:S(2)}) copy-start(bf16[1024,12,64]{0,2,1:T(8,128)(2,1)S(1)} %fusion.32) | copy-start | bytes 4718596
  356.1 8.6 copy-start.18
  364.7 7.1 copy-start.13
  364.7 7.1 copy-start.32
  364.7 7.1 copy-start.37
  372.9 2.2 copy-start.10
  372.9 2.2 copy-start.40
  372.9 2.2 copy-start.42
  373.4 1.7 copy-start.30
  403.6 1.4 copy-start.25
  403.7 460.2 %reduce-scatter.8.cloned.1.call-start = ((), (), s32[]{:S(2)}) async-start(), calls=%async_computation.6 | async-start | bytes 20054016 | tf_op jit(solution)/shard_map/reduce_scatter | solution.py:257
  405.0 8.0 copy-start.16
  451.5 1.5 copy-start.29
  451.5 538.6 %reduce-scatter.10.cloned.1.call-start = ((), (), s32[]{:S(2)}) async-start(), calls=%async_computation.7 | async-start | bytes 417792
  462.8 548.7 %all-reduce.5.cloned.1.call-start = ((), (), s32[]{:S(2)}) async-start(), calls=%async_computation.8 | async-start | bytes 1769472 | tf_op jit(solution)/shard_map/psum | solution.py:261
  869.9 123.5 %copy-start.47 = (f32[2,48]{1,0:T(2,128)S(1)}, f32[2,48]{1,0:T(2,128)}, u32[]{:S(2)}) copy-start(f32[2,48]{1,0:T(2,128)} %param.29) | copy-start | bytes 1156
  870.0 123.5 %copy-start.48 = (f32[2,48]{1,0:T(2,128)S(1)}, f32[2,48]{1,0:T(2,128)}, u32[]{:S(2)}) copy-start(f32[2,48]{1,0:T(2,128)} %param.32) | copy-start | bytes 1156
  870.0 124.0 %copy-start.45 = (f32[2,48]{1,0:T(2,128)S(1)}, f32[2,48]{1,0:T(2,128)}, u32[]{:S(2)}) copy-start(f32[2,48]{1,0:T(2,128)} %param.35) | copy-start | bytes 1156
  871.6 142.6 %copy-start.36 = (f32[48,3072]{1,0:T(8,128)S(1)}, f32[48,3072]{1,0:T(8,128)}, u32[]{:S(2)}) copy-start(f32[48,3072]{1,0:T(8,128)} %param.33) | copy-start | bytes 1769476
  871.6 143.6 %copy-start.21 = (f32[48,6144]{1,0:T(8,128)S(1)}, f32[48,6144]{1,0:T(8,128)}, u32[]{:S(2)}) copy-start(f32[48,6144]{1,0:T(8,128)} %param.28) | copy-start | bytes 3538948
  871.6 143.6 %copy-start.33 = (f32[48,6144]{1,0:T(8,128)S(1)}, f32[48,6144]{1,0:T(8,128)}, u32[]{:S(2)}) copy-start(f32[48,6144]{1,0:T(8,128)} %param.31) | copy-start | bytes 3538948
  994.0 23.1 %copy-start.44 = (f32[2,48]{1,0:T(2,128)}, f32[2,48]{1,0:T(2,128)S(1)}, u32[]{:S(2)}) copy-start(f32[2,48]{1,0:T(2,128)S(1)} %get-tuple-element.141) | copy-start | bytes 1156
  1011.5 3.7 copy-start.35
  1014.1 2.9 copy-start.22
  1015.1 1.9 copy-start.34
  1017.1 1.4 copy-start.20
  (2 other events, 1.9 us)
Sparse Core Ops, SparseCore 0:
  11.4 83.1 all-gather.3
  98.0 121.1 all-gather.5
  403.8 169.1 reduce-scatter.5
  579.6 284.2 reduce-scatter.7
  869.6 120.4 reduce-scatter.9
  993.0 18.4 all-reduce.4
where the time goes:
time: 1040 us; the launch traced here: 1030 us
  waiting for transfers between devices  601 us (58%)
  matrix products  205 us (20%)
  other arithmetic  92.1 us (9%)
  local copies, waits for them, and re-layouts  67.8 us (7%)
  blocking collectives  44.8 us (4%)
  between operations  15.3 us (1%)
    reduce_scatter x1, waiting for transfers between devices, local(): lax.psum_scatter(full_mlp, 'fsdp', scatter_dimension=0, tiled=True)  289 us
    unnamed x7, waiting for transfers between devices  119 us
    reduce_scatter x1, waiting for transfers between devices, local(): lax.psum_scatter(full_attn, 'fsdp', scatter_dimension=0, tiled=True)  101 us
    all_gather x1, blocking collectives, local(): lax.all_gather(gain_low, 'fsdp', axis=1, tiled=True)  42.3 us
    all_gather x1, waiting for transfers between devices, local(): lax.all_gather(mlp_low, 'fsdp', axis=0, tiled=True)  42.2 us
    all_gather x1, waiting for transfers between devices, local(): lax.all_gather(attn_low, 'fsdp', axis=0, tiled=True)  33.5 us
    dot_general x4, matrix products, over_columns(): lax.dot_general(left, right, (((1,), (1,)), ((), ())), preferred_element_...  33.3 us
    reshape x2, local copies, waits for them, and re-layouts, as_slab(): return matrix.reshape(matrix.shape[0] * matrix.shape[1] // LANES, LANES)  30.4 us
  transfers between devices with their start and end apart: 6, of which 6 were waited for; matrix products, arithmetic and copies ran while one was open for 16% of the time, Pallas kernels for 0%

commit v1 on v0

v1 whole, which is shorter than its diff:
```python
import functools
import math

import jax
import jax.numpy as jnp
import numpy as np
from jax import lax
from jax.experimental import pallas as pl
from jax.experimental.pallas import tpu as pltpu
from jax.sharding import PartitionSpec as P

HEAD = 64
STEP = 5
WARMUP = 10
EPSILON = 1e-05
MASKED = -1e30
MOMENTUM = 0.5
DECAY = 0.5
PEAK_RATE = 0.1
LANES = 128
BLOCK = 256

f32 = jnp.float32
bf16 = jnp.bfloat16


def nn(left, right):
    return jnp.dot(left, right, preferred_element_type=f32)


def nt(left, right):
    return lax.dot_general(
        left, right, (((1,), (1,)), ((), ())), preferred_element_type=f32
    )


def rotary_tables(row_count):
    half = HEAD // 2
    frequency = np.float32(10000.0) ** (-np.arange(half, dtype=np.float32) / np.float32(half))
    angles = np.arange(row_count, dtype=np.float32)[None, :] * frequency.astype(np.float32)[:, None]
    angles = angles.astype(np.float64)
    split = lambda t: np.ascontiguousarray(
        t.astype(np.float32).reshape(half, row_count // BLOCK, BLOCK).transpose(1, 0, 2)
    )
    return split(np.cos(angles)), split(np.sin(angles))


def rotate_rows(rows, cosine, sine):
    half = HEAD // 2
    first, second = rows[:half], rows[half:]
    return jnp.concatenate(
        [first * cosine - second * sine, second * cosine + first * sine], axis=0
    )


def rms_scale(rows):
    return lax.rsqrt(jnp.mean(rows * rows, axis=-1, keepdims=True) + EPSILON)


def block_kernel(
    doc_ref,
    x_ref,
    cot_ref,
    cos_ref,
    sin_ref,
    gain_ref,
    w_ref,
    out_ref,
    input_grad_ref,
    gain_grad_ref,
    g_out,
    g_ref,
    g_sem,
    y_ref,
    total_ref,
    dn_ref,
    n1t_ref,
    qt_ref,
    kt_ref,
    vt_ref,
    k_ref,
    v_ref,
    mixt_ref,
    n2_ref,
    n2t_ref,
    cott_ref,
    hid_ref,
    dgu_ref,
    lse_ref,
    cost_ref,
    sint_ref,
    acc_ref,
):
    row_count, width = x_ref.shape
    blocks = row_count // BLOCK
    pairs = width // LANES
    thirds = pairs // 2
    half_width = width // 2
    mlp_chunks = w_ref.shape[0] - thirds - 1
    slots = g_ref.shape[0]

    def load_w(chunk, half):
        return w_ref[chunk, half].reshape(width, half_width)

    def store_g(chunk, half, lanes, value):
        g_ref[chunk % slots, half, :, lanes] = value.astype(bf16)

    def grad_copy(chunk):
        slot = chunk % slots
        return pltpu.make_async_copy(g_ref.at[slot], g_out.at[chunk], g_sem.at[slot])

    def before_chunk(chunk):
        @pl.when(chunk >= slots)
        def _():
            grad_copy(chunk - slots).wait()

    def after_chunk(chunk):
        grad_copy(chunk).start()

    docs = [doc_ref[BLOCK * j] for j in range(blocks)]
    bias = [
        [jnp.where(docs[i] == docs[j], 0.0, MASKED).astype(f32) for j in range(i)] + [0.0]
        for i in range(blocks)
    ]
    causal = lax.broadcasted_iota(jnp.int32, (BLOCK, BLOCK), 0) <= lax.broadcasted_iota(
        jnp.int32, (BLOCK, BLOCK), 1
    )
    gain_one = gain_ref[0:1, :]
    gain_two = gain_ref[1:2, :]

    def rows_of(i):
        return pl.ds(i * BLOCK, BLOCK)

    for i in range(blocks):
        place = sum([(docs[j] == docs[i]).astype(jnp.int32) for j in range(i)], jnp.int32(0))
        cost_ref[:, rows_of(i)] = cos_ref[place]
        sint_ref[:, rows_of(i)] = sin_ref[place]
        stream = x_ref[rows_of(i), :].astype(f32)
        normed = (stream * rms_scale(stream) * gain_one).astype(bf16)
        n1t_ref[:, rows_of(i)] = normed.T
        cott_ref[:, rows_of(i)] = cot_ref[rows_of(i), :].T
        dn_ref[rows_of(i), :] = jnp.zeros((BLOCK, width), f32)

    def masked_pair(rows, h):
        zero = jnp.zeros((HEAD, BLOCK), bf16)
        parts = [rows[:HEAD], zero] if h == 0 else [zero, rows[HEAD:]]
        return jnp.concatenate(parts, axis=0)

    def scores_of(p, i, h):
        span = (i + 1) * BLOCK
        query = masked_pair(qt_ref[p, :, rows_of(i)], h)
        scores = nn(k_ref[p, pl.ds(0, span), :], query)
        parts = [scores[j * BLOCK : (j + 1) * BLOCK] for j in range(i + 1)]
        parts[i] = jnp.where(causal, parts[i], MASKED)
        return parts

    def attention_forward(p, carry):
        weights_t = load_w(p // 2, p % 2).T
        for i in range(blocks):
            cosine, sine = cost_ref[:, rows_of(i)], sint_ref[:, rows_of(i)]
            projected = nn(weights_t, n1t_ref[:, rows_of(i)])
            for h in range(2):
                lo, hi = h * HEAD, (h + 1) * HEAD
                query = rotate_rows(projected[lo:hi], cosine, sine).astype(bf16)
                qt_ref[p, lo:hi, rows_of(i)] = query * bf16(0.125)
                key = rotate_rows(projected[LANES + lo : LANES + hi], cosine, sine)
                kt_ref[p, lo:hi, rows_of(i)] = key.astype(bf16)
            vt_ref[p, :, rows_of(i)] = projected[2 * LANES :].astype(bf16)
            k_ref[p, rows_of(i), :] = kt_ref[p, :, rows_of(i)].T
            v_ref[p, rows_of(i), :] = vt_ref[p, :, rows_of(i)].T
        for i in range(blocks):
            span = (i + 1) * BLOCK
            for h in range(2):
                parts = scores_of(p, i, h)
                tops = [
                    jnp.max(part, axis=0, keepdims=True) + bias[i][j]
                    for j, part in enumerate(parts)
                ]
                top = functools.reduce(jnp.maximum, tops)
                exps = [jnp.exp(part - (top - bias[i][j])) for j, part in enumerate(parts)]
                total = sum([jnp.sum(e, axis=0, keepdims=True) for e in exps])
                exps_low = jnp.concatenate([e.astype(bf16) for e in exps], axis=0)
                heads = pl.ds(h * HEAD, HEAD)
                mixed = nn(vt_ref[p, heads, pl.ds(0, span)], exps_low)
                mixt_ref[p, heads, rows_of(i)] = (mixed * (1.0 / total)).astype(bf16)
                lse_ref[p, h : h + 1, rows_of(i)] = top + jnp.log(total)
        return carry

    lax.fori_loop(0, pairs, attention_forward, 0)

    out_chunk = thirds
    for i in range(blocks):
        mixed = mixt_ref[:, :, rows_of(i)].reshape(width, BLOCK).T
        branch = jnp.concatenate(
            [nn(mixed, load_w(out_chunk, half)) for half in range(2)], axis=1
        )
        after = x_ref[rows_of(i), :].astype(f32) + branch
        y_ref[rows_of(i), :] = after
        total_ref[rows_of(i), :] = after
        normed = (after * rms_scale(after) * gain_two).astype(bf16)
        n2_ref[rows_of(i), :] = normed
        n2t_ref[:, :, rows_of(i)] = normed.T.reshape(pairs, LANES, BLOCK)

    def feed_forward(chunk, carry):
        before_chunk(chunk)
        low = [load_w(thirds + 1 + chunk, half) for half in range(2)]
        w_gu = [w[:, : 2 * LANES] for w in low]
        w_gu_all = jnp.concatenate(w_gu, axis=1)
        w_down = jnp.concatenate([w[:, 2 * LANES :] for w in low], axis=1)
        for i in range(blocks):
            normed = n2_ref[rows_of(i), :]
            d_hidden = nn(cot_ref[rows_of(i), :], w_down)
            for half in range(2):
                gate_up = nn(normed, w_gu[half])
                gate, up = gate_up[:, :LANES], gate_up[:, LANES:]
                back = d_hidden[:, half * LANES : (half + 1) * LANES]
                sig = jax.nn.sigmoid(gate)
                silu = gate * sig
                lanes = pl.ds(half * LANES, LANES)
                hid_ref[rows_of(i), lanes] = (silu * up).astype(bf16)
                dgu_ref[rows_of(i), pl.ds(2 * half * LANES, LANES)] = (
                    back * up * (sig + silu * (1.0 - sig))
                ).astype(bf16)
                dgu_ref[rows_of(i), pl.ds((2 * half + 1) * LANES, LANES)] = (
                    back * silu
                ).astype(bf16)
            total_ref[rows_of(i), :] += nt(hid_ref[rows_of(i), :], w_down)
            dn_ref[rows_of(i), :] += nt(dgu_ref[rows_of(i), :], w_gu_all)
        n2t = n2t_ref[...].reshape(width, row_count)
        for half in range(2):
            store_g(
                chunk,
                half,
                pl.ds(0, 2 * LANES),
                nn(n2t, dgu_ref[:, pl.ds(2 * half * LANES, 2 * LANES)]),
            )
        grad_down = nn(cott_ref[...], hid_ref[...])
        for half in range(2):
            store_g(
                chunk,
                half,
                pl.ds(2 * LANES, LANES),
                grad_down[:, half * LANES : (half + 1) * LANES],
            )
        after_chunk(chunk)
        return carry

    lax.fori_loop(0, mlp_chunks, feed_forward, 0)

    gain_grad_two = jnp.zeros((1, width), f32)
    for i in range(blocks):
        after = y_ref[rows_of(i), :]
        scale = rms_scale(after)
        unit = after * scale
        d_normed = dn_ref[rows_of(i), :]
        d_unit = d_normed * gain_two
        gain_grad_two += jnp.sum(d_normed * unit, axis=0, keepdims=True)
        grad_after = cot_ref[rows_of(i), :].astype(f32) + scale * (
            d_unit - unit * jnp.mean(d_unit * unit, axis=-1, keepdims=True)
        )
        y_ref[rows_of(i), :] = grad_after
        n2_ref[rows_of(i), :] = grad_after.astype(bf16)
        out_ref[rows_of(i), :] = total_ref[rows_of(i), :].astype(bf16)
        dn_ref[rows_of(i), :] = jnp.zeros((BLOCK, width), f32)

    before_chunk(mlp_chunks)
    mixt = mixt_ref[...].reshape(width, row_count)
    for half in range(2):
        store_g(
            mlp_chunks,
            half,
            pl.ds(0, half_width),
            nn(mixt, n2_ref[:, pl.ds(half * half_width, half_width)]),
        )
    after_chunk(mlp_chunks)
    dmt_ref = n2t_ref
    w_out = jnp.concatenate([load_w(out_chunk, half) for half in range(2)], axis=1)
    for i in range(blocks):
        d_mixed = nt(w_out, n2_ref[rows_of(i), :])
        dmt_ref[:, :, rows_of(i)] = d_mixed.astype(bf16).reshape(pairs, LANES, BLOCK)

    def attention_backward(p, carry):
        acc_ref[1] = jnp.zeros((LANES, row_count), f32)
        acc_ref[2] = jnp.zeros((LANES, row_count), f32)
        for i in range(blocks):
            span = (i + 1) * BLOCK
            for h in range(2):
                heads = pl.ds(h * HEAD, HEAD)
                parts = scores_of(p, i, h)
                lse = lse_ref[p, h : h + 1, rows_of(i)]
                probs = [jnp.exp(part - (lse - bias[i][j])) for j, part in enumerate(parts)]
                probs = jnp.concatenate(probs, axis=0)
                back = masked_pair(dmt_ref[p, :, rows_of(i)], h)
                d_probs = nn(v_ref[p, pl.ds(0, span), :], back)
                weighted = probs * d_probs
                inner = jnp.sum(weighted, axis=0, keepdims=True)
                d_scores = (weighted - probs * inner).astype(bf16)
                acc_ref[0, heads, rows_of(i)] = nn(
                    kt_ref[p, heads, pl.ds(0, span)], d_scores
                )
                acc_ref[1, heads, pl.ds(0, span)] += nt(
                    qt_ref[p, heads, rows_of(i)], d_scores
                )
                acc_ref[2, heads, pl.ds(0, span)] += nt(
                    dmt_ref[p, heads, rows_of(i)], probs.astype(bf16)
                )
        dqkv_ref = dgu_ref
        for i in range(blocks):
            cosine, sine = cost_ref[:, rows_of(i)], -sint_ref[:, rows_of(i)]
            pieces = []
            for kind in range(2):
                for h in range(2):
                    piece = acc_ref[kind, pl.ds(h * HEAD, HEAD), rows_of(i)]
                    piece = rotate_rows(piece, cosine, sine)
                    pieces.append((piece * 0.125 if kind == 0 else piece).astype(bf16))
            pieces.append(acc_ref[2, :, rows_of(i)].astype(bf16))
            dqkv_ref[rows_of(i), pl.ds(0, 3 * LANES)] = jnp.concatenate(pieces, axis=0).T
        weights = load_w(p // 2, p % 2)
        chunk = mlp_chunks + 1 + p // 2

        @pl.when(p % 2 == 0)
        def _():
            before_chunk(chunk)

        d_qkv = dqkv_ref[:, pl.ds(0, 3 * LANES)]
        store_g(chunk, p % 2, pl.ds(0, half_width), nn(n1t_ref[...], d_qkv))

        @pl.when(p % 2 == 1)
        def _():
            after_chunk(chunk)

        for i in range(blocks):
            dn_ref[rows_of(i), :] += nt(dqkv_ref[rows_of(i), pl.ds(0, 3 * LANES)], weights)
        return carry

    lax.fori_loop(0, pairs, attention_backward, 0)

    gain_grad_one = jnp.zeros((1, width), f32)
    for i in range(blocks):
        stream = x_ref[rows_of(i), :].astype(f32)
        scale = rms_scale(stream)
        unit = stream * scale
        d_normed = dn_ref[rows_of(i), :]
        d_unit = d_normed * gain_one
        gain_grad_one += jnp.sum(d_normed * unit, axis=0, keepdims=True)
        input_grad_ref[rows_of(i), :] = (
            y_ref[rows_of(i), :]
            + scale * (d_unit - unit * jnp.mean(d_unit * unit, axis=-1, keepdims=True))
        ).astype(bf16)
    gain_grad_ref[...] = jnp.concatenate([gain_grad_one, gain_grad_two], axis=0)
    chunks = w_ref.shape[0]
    for chunk in range(chunks - slots, chunks):
        grad_copy(chunk).wait()


def local(
    tokens,
    doc_ids,
    cotangent,
    attn_weights,
    mlp_weights,
    gains,
    moment_attn,
    moment_mlp,
    moment_gains,
    ema_attn,
    ema_mlp,
    ema_gains,
):
    row_count, width = tokens.shape
    shard_rows = attn_weights.shape[0]
    group = width // shard_rows
    pairs = width // LANES
    hidden = mlp_weights.shape[1] // 3
    half_width = width // 2
    thirds = pairs // 2
    mlp_chunks = hidden // (2 * LANES)
    chunks = thirds + 1 + mlp_chunks

    def pack(attn, mlp):
        qkv = attn[:, : 3 * width].reshape(shard_rows, 3, pairs, LANES).transpose(2, 0, 1, 3)
        out = attn[:, 3 * width :].reshape(shard_rows, 2, half_width).transpose(1, 0, 2)
        ffn = mlp.reshape(shard_rows, 3, 2 * mlp_chunks, LANES).transpose(2, 0, 1, 3)
        return jnp.concatenate(
            [
                qkv.reshape(pairs, shard_rows, half_width),
                out,
                ffn.reshape(2 * mlp_chunks, shard_rows, half_width),
            ],
            axis=0,
        ).reshape(chunks, 2, shard_rows, half_width)

    packed = pack(attn_weights.astype(bf16), mlp_weights.astype(bf16))
    full = lax.all_gather(packed, "fsdp", axis=2, tiled=True)
    gain_rows = lax.all_gather(gains.astype(bf16), "fsdp", axis=1, tiled=True).astype(f32)
    cos_table, sin_table = rotary_tables(row_count)
    vmem = pl.BlockSpec(memory_space=pltpu.VMEM)
    hbm = pl.BlockSpec(memory_space=pl.ANY)
    slots = 3
    block_out, input_grad, gain_grads, grads = pl.pallas_call(
        block_kernel,
        out_shape=(
            jax.ShapeDtypeStruct((row_count, width), bf16),
            jax.ShapeDtypeStruct((row_count, width), bf16),
            jax.ShapeDtypeStruct((2, width), f32),
            jax.ShapeDtypeStruct((chunks, 2, width, half_width), bf16),
        ),
        in_specs=[pl.BlockSpec(memory_space=pltpu.SMEM)] + [vmem] * 6,
        out_specs=(vmem, vmem, vmem, hbm),
        scratch_shapes=[
            pltpu.VMEM((slots, 2, width, half_width), bf16),
            pltpu.SemaphoreType.DMA((slots,)),
            pltpu.VMEM((row_count, width), f32),
            pltpu.VMEM((row_count, width), f32),
            pltpu.VMEM((row_count, width), f32),
            pltpu.VMEM((width, row_count), bf16),
            pltpu.VMEM((pairs, LANES, row_count), bf16),
            pltpu.VMEM((pairs, LANES, row_count), bf16),
            pltpu.VMEM((pairs, LANES, row_count), bf16),
            pltpu.VMEM((pairs, row_count, LANES), bf16),
            pltpu.VMEM((pairs, row_count, LANES), bf16),
            pltpu.VMEM((pairs, LANES, row_count), bf16),
            pltpu.VMEM((row_count, width), bf16),
            pltpu.VMEM((pairs, LANES, row_count), bf16),
            pltpu.VMEM((width, row_count), bf16),
            pltpu.VMEM((row_count, 2 * LANES), bf16),
            pltpu.VMEM((row_count, 4 * LANES), bf16),
            pltpu.VMEM((pairs, 8, row_count), f32),
            pltpu.VMEM((HEAD // 2, row_count), f32),
            pltpu.VMEM((HEAD // 2, row_count), f32),
            pltpu.VMEM((3, LANES, row_count), f32),
        ],
        compiler_params=pltpu.CompilerParams(vmem_limit_bytes=63 * 2**20),
        name="block",
    )(doc_ids, tokens, cotangent, cos_table, sin_table, gain_rows, full)

    part = lax.psum_scatter(grads, "fsdp", scatter_dimension=2, tiled=True)
    part = lax.psum(part.astype(bf16), "rep").astype(f32)
    part = jnp.concatenate([part[mlp_chunks + 1 :], part[mlp_chunks:][:1], part[:mlp_chunks]])
    part = part.reshape(2 * chunks, shard_rows, half_width)
    qkv = part[:pairs].reshape(pairs, shard_rows, 3, LANES).transpose(1, 2, 0, 3)
    out = part[pairs : pairs + 2].transpose(1, 0, 2)
    ffn = part[pairs + 2 :].reshape(2 * mlp_chunks, shard_rows, 3, LANES).transpose(1, 2, 0, 3)
    grad_attn = jnp.concatenate(
        [qkv.reshape(shard_rows, 3 * width), out.reshape(shard_rows, width)], axis=1
    )
    grad_mlp = ffn.reshape(shard_rows, 3 * hidden)
    grad_gains = lax.psum_scatter(gain_grads, "fsdp", scatter_dimension=1, tiled=True)
    grad_gains = lax.psum(grad_gains, "rep")

    total_tokens = row_count * lax.axis_size("fsdp") * lax.axis_size("rep")
    rate = PEAK_RATE * STEP / (WARMUP * math.sqrt(total_tokens))

    def update(weight, grad, moment, average):
        velocity = MOMENTUM * moment + grad
        weight_new = weight - rate * (grad + MOMENTUM * velocity)
        average_new = DECAY * average + (1.0 - DECAY) * weight_new
        return (weight_new, velocity, average_new, weight_new.astype(bf16))

    kinds = [
        update(attn_weights, grad_attn, moment_attn, ema_attn),
        update(mlp_weights, grad_mlp, moment_mlp, ema_mlp),
        update(gains, grad_gains, moment_gains, ema_gains),
    ]
    return (block_out, input_grad, grad_attn, grad_mlp, grad_gains) + tuple(
        kind[what] for what in range(4) for kind in kinds
    )


def solution(mesh):
    rows = P(("fsdp", "rep"), None)
    shard = P("fsdp", None)
    columns = P(None, "fsdp")
    kinds = (shard, shard, columns)
    return jax.shard_map(
        local,
        mesh=mesh,
        in_specs=(rows, P(("fsdp", "rep")), rows) + kinds * 3,
        out_specs=(rows, rows) + kinds * 5,
        check_vma=False,
    )
```

time: 1040 us -> 694 us (0.67); the launches traced: 1030 us -> 693 us
  matrix products: 205 us -> 0 us
  Pallas kernels: 0 us -> 124 us
  waiting for transfers between devices: 601 us -> 488 us
  other arithmetic: 92.1 us -> 8.83 us
  local copies, waits for them, and re-layouts: 67.8 us -> 13.9 us
    dot_general x24 -> x0, matrix products: 205 us -> none  [the longest x4 33.3 us: over_columns(): lax.dot_general(left, right, (((1,), (1,)), ((), ())), preferred_element_...]
    reduce_scatter x2 -> x1, waiting for transfers between devices: 390 us -> 218 us  [local(): part = lax.psum_scatter(grads, 'fsdp', scatter_dimension=2, tiled=True)]
    pallas_call x0 -> x1, Pallas kernels: none -> 124 us  [local(): pl.pallas_call(block_kernel, out_shape=(jax.ShapeDtypeStruct((row_count,...]
    all_gather x2 -> x1, waiting for transfers between devices: 75.7 us -> 127 us  [local(): full = lax.all_gather(packed, 'fsdp', axis=2, tiled=True)]
    convert_element_type x11 -> x6, other arithmetic: 44.6 us -> 5.05 us  [the longest x3 3.79 us: update(): return (weight_new, velocity, average_new, weight_new.astype(bf16))]
    reshape x4 -> x9, local copies, waits for them, and re-layouts: 32.3 us -> 3.77 us  [the longest x1 2.07 us: local(): part[pairs + 2:].reshape(2 * mlp_chunks, shard_rows, 3, LANES)]
    concatenate x4 -> x1, other arithmetic: 20.2 us -> 1.01 us  [pack(): jnp.concatenate([qkv.reshape(pairs, shard_rows, half_width), out, ffn.res...]
    reduce_sum x3 -> x0, other arithmetic: 16.2 us -> none  [the longest x2 15.8 us: local(): exp_total = jnp.sum(shifted_exp, axis=-1, keepdims=True)]
  transfers between devices with their start and end apart: 6 -> 4, of which waited for: 6 -> 4; matrix products, arithmetic and copies ran while one was open for 16% -> 1% of each run, Pallas kernels for 0% -> 0%
where the time goes in v1:
time: 694 us; the launch traced here: 693 us
  waiting for transfers between devices  488 us (70%)
  Pallas kernels  124 us (18%)
  blocking collectives  44.8 us (6%)
  between operations  14.1 us (2%)
  local copies, waits for them, and re-layouts  13.9 us (2%)
  other arithmetic  8.83 us (1%)
    reduce_scatter x1, waiting for transfers between devices, local(): part = lax.psum_scatter(grads, 'fsdp', scatter_dimension=2, tiled=True)  218 us
    unnamed x5, waiting for transfers between devices  127 us
    all_gather x1, waiting for transfers between devices, local(): full = lax.all_gather(packed, 'fsdp', axis=2, tiled=True)  127 us
    pallas_call x1, Pallas kernels, local(): pl.pallas_call(block_kernel, out_shape=(jax.ShapeDtypeStruct((row_count,...  124 us
    all_gather x1, blocking collectives, local(): lax.all_gather(gains.astype(bf16), 'fsdp', axis=1, tiled=True).astype(f32)  42.4 us
    psum x1, waiting for transfers between devices, local(): part = lax.psum(part.astype(bf16), 'rep').astype(f32)  16.3 us
  transfers between devices with their start and end apart: 4, of which 4 were waited for; matrix products, arithmetic and copies ran while one was open for 1% of the time, Pallas kernels for 0%

profile of v1, /device:TPU:0, one launch (start us, length us, event | category | flops | bytes accessed | tf_op | source)
XLA Modules:
  0.0 693.4 jit_solution(32468369556387504)
XLA Ops:
  7.2 0.0 all-gather.3.cloned.1.call-start
  7.2 1.1 convert_element_type.26
  8.3 0.0 copy-start.2
  8.4 0.3 reshape.73
  8.7 0.1 copy.57
  8.8 0.2 reshape.74
  9.0 0.6 copy-done.2
  9.6 0.1 convert_bitcast_fusion
  9.7 0.1 copy.66
  9.8 0.4 copy.72
  10.2 0.5 reshape.77
  10.7 0.0 copy-start.15
  10.7 1.0 pad_maximum_fusion
  11.8 0.0 all-gather.3.cloned.1.call-update
  11.8 0.0 reduce-scatter.5.cloned.1.call-start
  11.8 0.0 copy-done.15
  11.8 42.4 %all-gather = bf16[16,48,2]{1,2,0:T(2,128)(2,1)S(1)} all-gather(bf16[1,48,2]{1,2,0:T(2,128)(2,1)S(1)} %convert_bitcast_fusion.1), channel_id=1, replica_groups=mesh['fsdp'=16,'rep'=2] {'fsdp'}, dimensions={0}, use_global_device_ids=true | all-gather | bytes 3264 | tf_op jit(solution)/shard_map/all_gather | solution.py:395
  54.2 0.7 reshape.86
  54.9 126.6 %all-gather.3.cloned.1.call-done.w_ref = bf16[12,2,768,384]{3,2,1,0:T(8,128)(2,1)} async-done(((bf16[12,2,48,384]{3,2,1,0:T(8,128)(2,1)}), bf16[12,2,768,384]{3,2,1,0:T(8,128)(2,1)}) %all-gather.3.cloned.1.call-update) | async-done | bytes 14155792 | tf_op jit(solution)/shard_map/all_gather | solution.py:394
  181.6 123.8 %block.1 = (bf16[1024,768]{1,0:T(8,128)(2,1)}, bf16[1024,768]{1,0:T(8,128)(2,1)}, f32[2,768]{1,0:T(2,128)}, bf16[12,2,768,384]{3,2,1,0:T(8,128)(2,1)}) custom-call(s32[1024]{0:T(1024)} %doc_ref.1, bf16[1024,768]{1,0:T(8,128)(2,1)} %x_ref.1, bf16[1024,768]{1,0:T(8,128)(2,1)} %cot_ref.1, f32[4,32,256]{2,1,0:T(8,128)} %constant.6.clone.cos_ref, ...), custom_call_target="tpu_custom_call" | custom-call | tf_op jit(solution)/shard_map/block/pallas_call | solution.py:400
  305.4 0.0 copy-start.11
  305.4 0.0 reduce-scatter.5.cloned.1.call-update
  305.4 0.0 copy-start.16
  305.5 0.0 copy-start.14
  305.5 0.0 reduce-scatter.7.cloned.1.call-start
  305.5 0.6 copy-done.11
  306.1 0.9 copy.63
  307.0 0.0 reduce-scatter.7.cloned.1.call-update
  307.1 0.0 all-reduce.2.cloned.1.call-start
  307.1 217.9 %reduce-scatter.5.cloned.1.call-done = bf16[12,2,48,384]{3,2,1,0:T(8,128)(2,1)} async-done(((bf16[12,2,768,384]{3,2,1,0:T(8,128)(2,1)}), bf16[12,2,48,384]{3,2,1,0:T(8,128)(2,1)}) %reduce-scatter.5.cloned.1.call-update) | async-done | bytes 884752 | tf_op jit(solution)/shard_map/reduce_scatter | solution.py:437
  525.0 0.0 all-reduce.2.cloned.1.call-update
  525.1 126.9 %reduce-scatter.7.cloned.1.call-done = f32[48,2]{1,0:T(8,128)} async-done(((f32[768,2]{1,0:T(8,128)}), f32[48,2]{1,0:T(8,128)}) %reduce-scatter.7.cloned.1.call-update) | async-done | bytes 400
  652.0 0.8 copy.64
  652.8 2.5 psum.15
  655.2 0.0 copy-done.16
  655.2 0.6 fusion
  655.8 0.0 copy-done.14
  655.8 0.6 add_multiply_fusion.2
  656.4 16.3 %all-reduce.2.cloned.1.call-done = bf16[12,2,48,384]{3,2,1,0:T(8,128)(2,1)} async-done(((bf16[12,2,48,384]{3,2,1,0:T(8,128)(2,1)}), bf16[12,2,48,384]{3,2,1,0:T(8,128)(2,1)}) %all-reduce.2.cloned.1.call-update) | async-done | bytes 884752 | tf_op jit(solution)/shard_map/psum | solution.py:438
  672.6 1.0 slice.33
  673.6 0.2 reshape.79
  673.8 0.3 copy.60
  674.0 0.0 copy-done.13
  674.1 0.0 copy-done.12
  674.1 0.0 copy-start
  674.1 0.1 reshape.80
  674.2 1.0 copy-done
  675.2 1.1 slice.35
  676.3 2.1 reshape.82
  678.4 0.7 copy.62
  679.1 0.0 copy-start.5
  679.1 0.0 copy-start.9
  679.1 0.2 convert_element_type.28
  679.4 0.8 copy-done.5
  680.2 0.2 copy-done.9
  680.4 1.1 fusion.2
  681.4 0.0 copy-done.6
  681.5 0.4 copy-done.10
  681.8 0.9 add_multiply_fusion.1
  682.7 0.0 copy-done.8
  682.7 0.6 copy-done.3
  683.3 2.2 fusion.1
  685.5 1.2 add_multiply_fusion
  686.7 0.2 copy-done.1
  (21 shorter events, 0.2 us)
Async XLA Ops:
  7.2 174.4 %all-gather.3.cloned.1.call-start = ((), (), s32[]{:S(2)}) async-start(), calls=%async_computation.2 | async-start | bytes 15040512 | tf_op jit(solution)/shard_map/all_gather | solution.py:394
  8.3 1.3 copy-start.2
  10.7 1.1 copy-start.15
  11.8 513.2 %reduce-scatter.5.cloned.1.call-start = ((), (), s32[]{:S(2)}) async-start(), calls=%async_computation.3 | async-start | bytes 15040512 | tf_op jit(solution)/shard_map/reduce_scatter | solution.py:437
  305.4 0.7 copy-start.11
  305.4 349.8 %copy-start.16 = (f32[2,48]{1,0:T(2,128)S(1)}, f32[2,48]{1,0:T(2,128)}, u32[]{:S(2)}) copy-start(f32[2,48]{1,0:T(2,128)} %param.22) | copy-start | bytes 1156
  305.5 350.3 %copy-start.14 = (f32[2,48]{1,0:T(2,128)S(1)}, f32[2,48]{1,0:T(2,128)}, u32[]{:S(2)}) copy-start(f32[2,48]{1,0:T(2,128)} %param.25) | copy-start | bytes 1156
  305.5 346.5 %reduce-scatter.7.cloned.1.call-start = ((), (), s32[]{:S(2)}) async-start(), calls=%async_computation.5 | async-start | bytes 417792
  307.1 365.5 %all-reduce.2.cloned.1.call-start = ((), (), s32[]{:S(2)}) async-start(), calls=%async_computation.4 | async-start | bytes 1769472 | tf_op jit(solution)/shard_map/psum | solution.py:438
  655.2 18.8 %copy-start.13 = (f32[2,48]{1,0:T(2,128)}, f32[2,48]{1,0:T(2,128)S(1)}, u32[]{:S(2)}) copy-start(f32[2,48]{1,0:T(2,128)S(1)} %psum.15) | copy-start | bytes 1156
  655.8 18.3 %copy-start.12 = (f32[2,48]{1,0:T(2,128)}, f32[2,48]{1,0:T(2,128)S(1)}, u32[]{:S(2)}) copy-start(f32[2,48]{1,0:T(2,128)S(1)} %get-tuple-element.26) | copy-start | bytes 1156
  674.1 1.2 copy-start
  679.1 1.1 copy-start.5
  679.1 1.2 copy-start.9
  680.4 1.1 copy-start.6
  680.4 1.5 copy-start.10
  680.4 2.3 copy-start.8
  681.5 4.0 copy-start.4
  681.5 1.8 copy-start.3
  683.3 2.2 copy-start.7
  685.5 1.4 copy-start.1
Sparse Core Ops, SparseCore 0:
  11.9 169.6 all-gather.2
  305.6 219.4 reduce-scatter.4
  531.0 120.9 reduce-scatter.6
  654.2 18.3 all-reduce.1

commit v2 on v1

v2 whole, which is shorter than its diff:
```python
import functools
import math

import jax
import jax.numpy as jnp
import numpy as np
from jax import lax
from jax.experimental import pallas as pl
from jax.experimental.pallas import tpu as pltpu
from jax.sharding import PartitionSpec as P

HEAD = 64
STEP = 5
WARMUP = 10
EPSILON = 1e-05
MASKED = -1e30
MOMENTUM = 0.5
DECAY = 0.5
PEAK_RATE = 0.1
LANES = 128
BLOCK = 256

f32 = jnp.float32
bf16 = jnp.bfloat16


def nn(left, right):
    return jnp.dot(left, right, preferred_element_type=f32)


def nt(left, right):
    return lax.dot_general(
        left, right, (((1,), (1,)), ((), ())), preferred_element_type=f32
    )


def rotary_tables(row_count):
    half = HEAD // 2
    frequency = np.float32(10000.0) ** (-np.arange(half, dtype=np.float32) / np.float32(half))
    angles = np.arange(row_count, dtype=np.float32)[None, :] * frequency.astype(np.float32)[:, None]
    angles = angles.astype(np.float64)
    split = lambda t: np.ascontiguousarray(
        t.astype(np.float32).reshape(half, row_count // BLOCK, BLOCK).transpose(1, 0, 2)
    )
    return split(np.cos(angles)), split(np.sin(angles))


def rotate_rows(rows, cosine, sine):
    half = HEAD // 2
    first, second = rows[:half], rows[half:]
    return jnp.concatenate(
        [first * cosine - second * sine, second * cosine + first * sine], axis=0
    )


def rms_scale(rows):
    return lax.rsqrt(jnp.mean(rows * rows, axis=-1, keepdims=True) + EPSILON)


class Scratch:
    def __init__(self, names, refs):
        for name, ref in zip(names, refs, strict=True):
            setattr(self, name, ref)


def block_kernel(linked, names, *refs):
    s = Scratch(names, refs)
    row_count, width = s.x.shape
    blocks = row_count // BLOCK
    pairs = width // LANES
    thirds = pairs // 2
    half_width = width // 2
    chunks = s.w.shape[0]
    mlp_chunks = chunks - thirds - 1
    slots = s.g.shape[0]
    last_step = mlp_chunks + 2 * thirds

    def rows_of(i):
        return pl.ds(i * BLOCK, BLOCK)

    def load_w(chunk, half):
        return s.w[chunk, half].reshape(width, half_width)

    def store_g(chunk, half, lanes, value):
        low = value.astype(bf16)
        if linked:
            low = low.reshape(s.g.shape[2:5] + (low.shape[1],))
            s.g[chunk % slots, half, :, :, :, lanes] = low
        else:
            s.g[chunk % slots, half, :, lanes] = low

    def chunk_of(step):
        return jnp.where(step <= mlp_chunks, step, mlp_chunks + (step - mlp_chunks) // 2)

    def is_step(step):
        late = (step > mlp_chunks) & ((step - mlp_chunks) % 2 == 0) & (step <= last_step)
        return (step >= 0) & ((step <= mlp_chunks) | late)

    if linked:
        gather_start, gather_step, reduce_step, gain_sum = links(
            s, chunks, thirds, mlp_chunks, chunk_of, is_step
        )
    else:

        def gather_start():
            pass

        def gather_step(step):
            pass

        def grad_copy(chunk):
            slot = chunk % slots
            return pltpu.make_async_copy(s.g.at[slot], s.g_out.at[chunk], s.g_sem.at[slot])

        def reduce_step(step):
            @pl.when(is_step(step - 1))
            def _():
                grad_copy(chunk_of(step - 1)).wait()

            @pl.when(is_step(step))
            def _():
                grad_copy(chunk_of(step)).start()

    copies = [
        pltpu.make_async_copy(s.x_in, s.x, s.local_sem.at[0]),
        pltpu.make_async_copy(s.cot_in, s.cot, s.local_sem.at[1]),
    ]
    for copy in copies:
        copy.start()

    docs = [s.doc[BLOCK * j] for j in range(blocks)]
    bias = [
        [jnp.where(docs[i] == docs[j], 0.0, MASKED).astype(f32) for j in range(i)] + [0.0]
        for i in range(blocks)
    ]
    causal = lax.broadcasted_iota(jnp.int32, (BLOCK, BLOCK), 0) <= lax.broadcasted_iota(
        jnp.int32, (BLOCK, BLOCK), 1
    )

    gather_start()
    for i in range(blocks):
        place = sum([(docs[j] == docs[i]).astype(jnp.int32) for j in range(i)], jnp.int32(0))
        s.cost[:, rows_of(i)] = s.cos[place]
        s.sint[:, rows_of(i)] = s.sin[place]
    for copy in copies:
        copy.wait()
    gather_step(0)
    for i in range(blocks):
        s.cott[:, rows_of(i)] = s.cot[rows_of(i), :].T
        if i < 2:
            gather_step(i + 1)
    gain_one = s.gain[0:1, :]
    gain_two = s.gain[1:2, :]
    for i in range(blocks):
        stream = s.x[rows_of(i), :].astype(f32)
        normed = (stream * rms_scale(stream) * gain_one).astype(bf16)
        s.n1t[:, rows_of(i)] = normed.T
        s.dn[rows_of(i), :] = jnp.zeros((BLOCK, width), f32)
    gather_step(3)

    def masked_pair(rows, h):
        zero = jnp.zeros((HEAD, BLOCK), bf16)
        parts = [rows[:HEAD], zero] if h == 0 else [zero, rows[HEAD:]]
        return jnp.concatenate(parts, axis=0)

    def scores_of(p, i, h):
        span = (i + 1) * BLOCK
        query = masked_pair(s.qt[p, :, rows_of(i)], h)
        scores = nn(s.k[p, pl.ds(0, span), :], query)
        parts = [scores[j * BLOCK : (j + 1) * BLOCK] for j in range(i + 1)]
        parts[i] = jnp.where(causal, parts[i], MASKED)
        return parts

    def attention_forward(p, carry):
        @pl.when((p == 1) | (p == 2))
        def _():
            gather_step(p + 3)

        @pl.when(p >= 4)
        def _():
            gather_step(p + 2)

        weights_t = load_w(p // 2, p % 2).T
        for i in range(blocks):
            cosine, sine = s.cost[:, rows_of(i)], s.sint[:, rows_of(i)]
            projected = nn(weights_t, s.n1t[:, rows_of(i)])
            for h in range(2):
                lo, hi = h * HEAD, (h + 1) * HEAD
                query = rotate_rows(projected[lo:hi], cosine, sine).astype(bf16)
                s.qt[p, lo:hi, rows_of(i)] = query * bf16(0.125)
                key = rotate_rows(projected[LANES + lo : LANES + hi], cosine, sine)
                s.kt[p, lo:hi, rows_of(i)] = key.astype(bf16)
            s.vt[p, :, rows_of(i)] = projected[2 * LANES :].astype(bf16)
            s.k[p, rows_of(i), :] = s.kt[p, :, rows_of(i)].T
            s.v[p, rows_of(i), :] = s.vt[p, :, rows_of(i)].T
        for i in range(blocks):
            span = (i + 1) * BLOCK
            for h in range(2):
                parts = scores_of(p, i, h)
                tops = [
                    jnp.max(part, axis=0, keepdims=True) + bias[i][j]
                    for j, part in enumerate(parts)
                ]
                top = functools.reduce(jnp.maximum, tops)
                exps = [jnp.exp(part - (top - bias[i][j])) for j, part in enumerate(parts)]
                total = sum([jnp.sum(e, axis=0, keepdims=True) for e in exps])
                exps_low = jnp.concatenate([e.astype(bf16) for e in exps], axis=0)
                heads = pl.ds(h * HEAD, HEAD)
                mixed = nn(s.vt[p, heads, pl.ds(0, span)], exps_low)
                s.mixt[p, heads, rows_of(i)] = (mixed * (1.0 / total)).astype(bf16)
                s.lse[p, h : h + 1, rows_of(i)] = top + jnp.log(total)
        return carry

    lax.fori_loop(0, pairs, attention_forward, 0)

    out_chunk = thirds
    for i in range(blocks):
        mixed = s.mixt[:, :, rows_of(i)].reshape(width, BLOCK).T
        branch = jnp.concatenate(
            [nn(mixed, load_w(out_chunk, half)) for half in range(2)], axis=1
        )
        after = s.x[rows_of(i), :].astype(f32) + branch
        s.y[rows_of(i), :] = after
        s.total[rows_of(i), :] = after
        normed = (after * rms_scale(after) * gain_two).astype(bf16)
        s.n2[rows_of(i), :] = normed
        s.n2t[:, :, rows_of(i)] = normed.T.reshape(pairs, LANES, BLOCK)

    def feed_forward(chunk, carry):
        gather_step(chunk + pairs + 2)
        low = [load_w(thirds + 1 + chunk, half) for half in range(2)]
        w_gu = [w[:, : 2 * LANES] for w in low]
        w_gu_all = jnp.concatenate(w_gu, axis=1)
        w_down = jnp.concatenate([w[:, 2 * LANES :] for w in low], axis=1)
        for i in range(blocks):
            normed = s.n2[rows_of(i), :]
            d_hidden = nn(s.cot[rows_of(i), :], w_down)
            for half in range(2):
                gate_up = nn(normed, w_gu[half])
                gate, up = gate_up[:, :LANES], gate_up[:, LANES:]
                back = d_hidden[:, half * LANES : (half + 1) * LANES]
                sig = jax.nn.sigmoid(gate)
                silu = gate * sig
                s.hid[rows_of(i), pl.ds(half * LANES, LANES)] = (silu * up).astype(bf16)
                s.dgu[rows_of(i), pl.ds(2 * half * LANES, LANES)] = (
                    back * up * (sig + silu * (1.0 - sig))
                ).astype(bf16)
                s.dgu[rows_of(i), pl.ds((2 * half + 1) * LANES, LANES)] = (
                    back * silu
                ).astype(bf16)
            s.total[rows_of(i), :] += nt(s.hid[rows_of(i), :], w_down)
            s.dn[rows_of(i), :] += nt(s.dgu[rows_of(i), :], w_gu_all)
        n2t = s.n2t[...].reshape(width, row_count)
        for half in range(2):
            store_g(
                chunk,
                half,
                pl.ds(0, 2 * LANES),
                nn(n2t, s.dgu[:, pl.ds(2 * half * LANES, 2 * LANES)]),
            )
        grad_down = nn(s.cott[...], s.hid[...])
        for half in range(2):
            store_g(
                chunk,
                half,
                pl.ds(2 * LANES, LANES),
                grad_down[:, half * LANES : (half + 1) * LANES],
            )
        reduce_step(chunk)
        return carry

    lax.fori_loop(0, mlp_chunks, feed_forward, 0)

    gain_grad_two = jnp.zeros((1, width), f32)
    for i in range(blocks):
        after = s.y[rows_of(i), :]
        scale = rms_scale(after)
        unit = after * scale
        d_normed = s.dn[rows_of(i), :]
        d_unit = d_normed * gain_two
        gain_grad_two += jnp.sum(d_normed * unit, axis=0, keepdims=True)
        grad_after = s.cot[rows_of(i), :].astype(f32) + scale * (
            d_unit - unit * jnp.mean(d_unit * unit, axis=-1, keepdims=True)
        )
        s.y[rows_of(i), :] = grad_after
        s.n2[rows_of(i), :] = grad_after.astype(bf16)
        s.cot[rows_of(i), :] = s.total[rows_of(i), :].astype(bf16)
        s.dn[rows_of(i), :] = jnp.zeros((BLOCK, width), f32)
    out_copy = pltpu.make_async_copy(s.cot, s.block_out, s.local_sem.at[0])
    out_copy.start()

    mixt = s.mixt[...].reshape(width, row_count)
    for half in range(2):
        store_g(
            mlp_chunks,
            half,
            pl.ds(0, half_width),
            nn(mixt, s.n2[:, pl.ds(half * half_width, half_width)]),
        )
    reduce_step(mlp_chunks)
    dmt = s.n2t
    w_out = jnp.concatenate([load_w(out_chunk, half) for half in range(2)], axis=1)
    for i in range(blocks):
        d_mixed = nt(w_out, s.n2[rows_of(i), :])
        dmt[:, :, rows_of(i)] = d_mixed.astype(bf16).reshape(pairs, LANES, BLOCK)

    def attention_backward(p, carry):
        s.acc[1] = jnp.zeros((LANES, row_count), f32)
        s.acc[2] = jnp.zeros((LANES, row_count), f32)
        for i in range(blocks):
            span = (i + 1) * BLOCK
            for h in range(2):
                heads = pl.ds(h * HEAD, HEAD)
                parts = scores_of(p, i, h)
                lse = s.lse[p, h : h + 1, rows_of(i)]
                probs = [jnp.exp(part - (lse - bias[i][j])) for j, part in enumerate(parts)]
                probs = jnp.concatenate(probs, axis=0)
                back = masked_pair(dmt[p, :, rows_of(i)], h)
                d_probs = nn(s.v[p, pl.ds(0, span), :], back)
                weighted = probs * d_probs
                inner = jnp.sum(weighted, axis=0, keepdims=True)
                d_scores = (weighted - probs * inner).astype(bf16)
                s.acc[0, heads, rows_of(i)] = nn(s.kt[p, heads, pl.ds(0, span)], d_scores)
                s.acc[1, heads, pl.ds(0, span)] += nt(s.qt[p, heads, rows_of(i)], d_scores)
                s.acc[2, heads, pl.ds(0, span)] += nt(
                    dmt[p, heads, rows_of(i)], probs.astype(bf16)
                )
        for i in range(blocks):
            cosine, sine = s.cost[:, rows_of(i)], -s.sint[:, rows_of(i)]
            pieces = []
            for kind in range(2):
                for h in range(2):
                    piece = s.acc[kind, pl.ds(h * HEAD, HEAD), rows_of(i)]
                    piece = rotate_rows(piece, cosine, sine)
                    pieces.append((piece * 0.125 if kind == 0 else piece).astype(bf16))
            pieces.append(s.acc[2, :, rows_of(i)].astype(bf16))
            s.dgu[rows_of(i), pl.ds(0, 3 * LANES)] = jnp.concatenate(pieces, axis=0).T
        weights = load_w(p // 2, p % 2)
        store_g(
            mlp_chunks + 1 + p // 2,
            p % 2,
            pl.ds(0, half_width),
            nn(s.n1t[...], s.dgu[:, pl.ds(0, 3 * LANES)]),
        )
        reduce_step(mlp_chunks + 1 + p)
        for i in range(blocks):
            s.dn[rows_of(i), :] += nt(s.dgu[rows_of(i), pl.ds(0, 3 * LANES)], weights)
        return carry

    lax.fori_loop(0, pairs, attention_backward, 0)

    reduce_step(last_step + 1)
    gain_grad_one = jnp.zeros((1, width), f32)
    for i in range(blocks):
        stream = s.x[rows_of(i), :].astype(f32)
        scale = rms_scale(stream)
        unit = stream * scale
        d_normed = s.dn[rows_of(i), :]
        d_unit = d_normed * gain_one
        gain_grad_one += jnp.sum(d_normed * unit, axis=0, keepdims=True)
        s.x[rows_of(i), :] = (
            s.y[rows_of(i), :]
            + scale * (d_unit - unit * jnp.mean(d_unit * unit, axis=-1, keepdims=True))
        ).astype(bf16)
    grad_copy_out = pltpu.make_async_copy(s.x, s.input_grad, s.local_sem.at[1])
    grad_copy_out.start()
    gain_grads = jnp.concatenate(
        [gain_grad_one, gain_grad_two, jnp.zeros((6, width), f32)], axis=0
    )
    if linked:
        gain_sum[0](gain_grads)
        reduce_step(last_step + 2)
        gain_sum[1]()
        reduce_step(last_step + 3)
        gain_sum[2]()
        reduce_step(last_step + 4)
        gain_sum[3]()
        reduce_step(last_step + 5)
        s.g_out[...] = s.gout[...]
    else:
        s.gain_out[...] = gain_grads
    out_copy.wait()
    grad_copy_out.wait()


def links(s, chunks, thirds, mlp_chunks, chunk_of, is_step):
    planes = s.w.shape[2]
    me = lax.axis_index("fsdp")
    core = lax.axis_index("rep")
    z, m = me // 4, me % 4
    over_x, over_y, over_both = m + 1 - 2 * (m % 2), (m + 2) % 4, 3 - m
    m1 = (1 - core) * over_x + core * over_y
    m2 = (1 - core) * over_y + core * over_x
    m3 = over_both
    other = 1 - core

    def chip(plane, place):
        return (plane * 4 + place, core)

    sibling = (me, other)

    def far(k):
        return (z + k) % planes

    peers = [chip(far(k), m) for k in range(1, planes)]

    def remote(src, dst, sems, index, device):
        return pltpu.make_async_remote_copy(
            src_ref=src,
            dst_ref=dst,
            send_sem=sems.at[(0,) + index],
            recv_sem=sems.at[(1,) + index],
            device_id=device,
            device_id_type=pl.DeviceIdType.MESH,
        )

    def along_z(chunk, k):
        block = s.w.at[chunk, core, z, m]
        return remote(block, block, s.z_sem, (chunk, k), peers[k])

    def line(chunk, place, index, device):
        block = s.w.at[chunk, core, :, place]
        return remote(block, block, s.line_sem, (chunk, index), device)

    hops = [
        (m, chip(z, m1)),
        (m, chip(z, m2)),
        (m1, chip(z, m2)),
        (m, sibling),
        (m1, sibling),
        (m2, sibling),
        (m3, sibling),
    ]

    def hop(chunk, index):
        return line(chunk, hops[index][0], index, hops[index][1])

    def gain_along_z(k):
        block = s.gt.at[z, m]
        return remote(block, block, s.gain_sem, (k,), peers[k])

    def gain_line(place, index, device):
        block = s.gt.at[:, place]
        return remote(block, block, s.gain_sem, (planes - 1 + index,), device)

    def gain_hop(index):
        return gain_line(hops[index][0], index, hops[index][1])

    width = s.x.shape[1]
    pairs = width // LANES
    shard_rows = s.w.shape[4]
    half_width = s.w.shape[5]
    hidden = s.mlp_in.shape[1] // 3

    def gather_start():
        loads = [
            pltpu.make_async_copy(
                s.attn_in.at[:, pl.ds(k * width, width)],
                s.dn.at[pl.ds(k * shard_rows, shard_rows)],
                s.load_sem.at[k],
            )
            for k in range(4)
        ] + [
            pltpu.make_async_copy(
                s.mlp_in.at[:, pl.ds(k * width, width)],
                s.dn.at[pl.ds((4 + k) * shard_rows, shard_rows)],
                s.load_sem.at[4 + k],
            )
            for k in range(3 * hidden // width)
        ]
        for load in loads:
            load.start()
        barrier = pltpu.get_barrier_semaphore()
        partners = [chip(z, over_x), chip(z, over_y), chip(z, over_both), sibling] + peers
        for partner in partners:
            pl.semaphore_signal(
                barrier, inc=1, device_id=partner, device_id_type=pl.DeviceIdType.MESH
            )
        own = s.gains_in[...].astype(bf16)
        own = jnp.concatenate([own, jnp.zeros((2, LANES - shard_rows), bf16)], axis=1)
        s.gt[z, m] = jnp.concatenate([own, jnp.zeros((14, LANES), bf16)], axis=0)
        for load in loads:
            load.wait()

        def piece(row, lane):
            rows = s.dn[pl.ds(row * shard_rows, shard_rows), pl.ds(lane, LANES)]
            return rows.astype(bf16)

        for third in range(thirds):
            lane = pl.multiple_of((2 * third + core) * LANES, LANES)
            for kind in range(3):
                s.w[third, core, z, m, :, kind * LANES : (kind + 1) * LANES] = piece(kind, lane)
        lane = pl.multiple_of(core * half_width, LANES)
        s.w[thirds, core, z, m] = s.dn[
            pl.ds(3 * shard_rows, shard_rows), pl.ds(lane, half_width)
        ].astype(bf16)
        pl.semaphore_wait(barrier, len(partners))
        for k in range(planes - 1):
            gain_along_z(k).start()
        for chunk in range(thirds + 1):
            for k in range(planes - 1):
                along_z(chunk, k).start()
        for j in range(mlp_chunks):
            for kind in range(3):
                place = kind * hidden + 2 * j * LANES
                row, first = 4 + place // width, place % width
                lane = pl.multiple_of(first + core * LANES, LANES)
                s.w[thirds + 1 + j, core, z, m, :, kind * LANES : (kind + 1) * LANES] = piece(
                    row, lane
                )
            for k in range(planes - 1):
                along_z(thirds + 1 + j, k).start()

    def gather_step(step):
        early = isinstance(step, int) and step < 3
        if early and step == 0:
            for k in range(planes - 1):
                gain_along_z(k).wait()
            gain_hop(0).start()
            gain_hop(1).start()
        if early and step == 1:
            gain_hop(0).wait()
            gain_hop(2).start()
        if early and step == 2:
            gain_hop(1).wait()
            gain_hop(2).wait()
            rows = jnp.zeros((8, width), f32)
            for d in range(planes * 4):
                tile = s.gt[d // 4, d % 4].astype(f32)[:8]
                wide = jnp.concatenate([tile, jnp.zeros((8, width - LANES), f32)], axis=1)
                rows += pltpu.roll(wide, d * shard_rows, 1) if d else wide
            s.gain[...] = rows

        def stage(chunk, todo):
            if isinstance(chunk, int):
                if 0 <= chunk < chunks:
                    todo(chunk)
            else:
                pl.when((chunk >= 0) & (chunk < chunks))(lambda: todo(chunk))

        def ready(chunk):
            for index in range(3, 7):
                hop(chunk, index).wait_recv()
            for k in range(planes - 1):
                along_z(chunk, k).wait_send()
            for index in range(7):
                hop(chunk, index).wait_send()

        def third_hop(chunk):
            hop(chunk, 1).wait_recv()
            hop(chunk, 5).start()
            hop(chunk, 2).wait_recv()
            hop(chunk, 6).start()

        def second_hop(chunk):
            hop(chunk, 0).wait_recv()
            hop(chunk, 2).start()
            hop(chunk, 4).start()

        def first_hop(chunk):
            for k in range(planes - 1):
                along_z(chunk, k).wait_recv()
            for index in (0, 1, 3):
                hop(chunk, index).start()

        stage(step, first_hop)
        stage(step - 1, second_hop)
        stage(step - 2, third_hop)
        stage(step - 3, ready)

    def to_sibling(step):
        chunk = chunk_of(step)
        return remote(
            s.g.at[chunk % 2, other], s.a.at[chunk % 4], s.rs_sem, (step, 0), sibling
        )

    def to_second(step):
        return remote(s.bs, s.b.at[chunk_of(step) % 2], s.rs_sem, (step, 1), chip(z, m2))

    def to_first(step):
        return remote(s.cs, s.c.at[chunk_of(step) % 2], s.rs_sem, (step, 2), chip(z, m1))

    def to_plane(step, k):
        return remote(
            s.ds.at[far(k + 1)],
            s.d.at[chunk_of(step) % 2, k],
            s.rs_sem,
            (step, 3 + k),
            peers[k],
        )

    def half_block(step):
        place = jnp.where(
            step < mlp_chunks,
            thirds + 1 + step,
            jnp.where(step == mlp_chunks, thirds, (step - mlp_chunks) // 2 - 1),
        )
        return s.gout.at[place, core]

    def to_copy(step):
        block = half_block(step)
        return remote(block, block, s.rs_sem, (step, 2 + planes), sibling)

    def reduce_step(step):
        def when(number, todo):
            pl.when(is_step(number))(lambda: todo(number))

        def begin(number):
            to_sibling(number).start()

        def halves(number):
            chunk = chunk_of(number)
            to_sibling(number).wait()

            def both(place):
                return s.g[chunk % 2, core, :, place].astype(f32) + s.a[
                    chunk % 4, :, place
                ].astype(f32)

            s.bs[:, 0] = both(m2).astype(bf16)
            s.bs[:, 1] = both(m3).astype(bf16)
            to_second(number).start()
            s.h[:, 0] = both(m).astype(bf16)
            s.h[:, 1] = both(m1).astype(bf16)

        def quarters(number):
            chunk = chunk_of(number)
            to_second(number).wait()
            s.cs[...] = (s.h[:, 1].astype(f32) + s.b[chunk % 2, :, 1].astype(f32)).astype(bf16)
            to_first(number).start()
            s.kept[...] = s.h[:, 0].astype(f32) + s.b[chunk % 2, :, 0].astype(f32)

        def lines(number):
            chunk = chunk_of(number)
            to_first(number).wait()
            s.kept[...] = s.kept[...] + s.c[chunk % 2].astype(f32)
            s.ds[...] = s.kept[...].astype(bf16)
            for k in range(planes - 1):
                to_plane(number, k).start()
            s.own[...] = s.kept[z]

        def last(number):
            chunk = chunk_of(number)
            total = s.own[...]
            for k in range(planes - 1):
                to_plane(number, k).wait()
                total += s.d[chunk % 2, k].astype(f32)
            half_block(number)[...] = total
            to_copy(number).start()

        def end(number):
            to_copy(number).wait()

        when(step, begin)
        when(step - 5, end)
        when(step - 4, last)
        when(step - 3, lines)
        when(step - 2, quarters)
        when(step - 1, halves)

    def plane_sum():
        block = s.gp.at[m]
        return [
            remote(block, block, s.gsum_sem, (k,), chip(z, place))
            for k, place in enumerate([over_x, over_y, over_both])
        ]

    def line_sum():
        block = s.gz.at[z]
        return [
            remote(block, block, s.gsum_sem, (3 + k,), peers[k]) for k in range(planes - 1)
        ]

    def core_sum():
        return remote(s.gc.at[0], s.gc.at[1], s.gsum_sem, (2 + planes,), sibling)

    def gain_begin(value):
        s.gp[m] = value
        for copy in plane_sum():
            copy.start()

    def gain_lines_sum():
        for copy in plane_sum():
            copy.wait()
        s.gz[z] = (s.gp[0] + s.gp[1]) + (s.gp[2] + s.gp[3])
        for copy in line_sum():
            copy.start()

    def gain_cores():
        for copy in line_sum():
            copy.wait()
        total = s.gz[0]
        for k in range(1, planes):
            total += s.gz[k]
        s.gc[0] = total
        core_sum().start()

    def gain_end():
        core_sum().wait()
        total = s.gc[0] + s.gc[1]
        s.gain_out[...] = pltpu.roll(total, (width - me * shard_rows) % width, 1)[:, :LANES]

    return gather_start, gather_step, reduce_step, (gain_begin, gain_lines_sum, gain_cores, gain_end)


def local(
    tokens,
    doc_ids,
    cotangent,
    attn_weights,
    mlp_weights,
    gains,
    moment_attn,
    moment_mlp,
    moment_gains,
    ema_attn,
    ema_mlp,
    ema_gains,
):
    row_count, width = tokens.shape
    shard_rows = attn_weights.shape[0]
    group = width // shard_rows
    pairs = width // LANES
    hidden = mlp_weights.shape[1] // 3
    half_width = width // 2
    thirds = pairs // 2
    mlp_chunks = hidden // (2 * LANES)
    chunks = thirds + 1 + mlp_chunks

    def pack(attn, mlp):
        qkv = attn[:, : 3 * width].reshape(shard_rows, 3, pairs, LANES).transpose(2, 0, 1, 3)
        out = attn[:, 3 * width :].reshape(shard_rows, 2, half_width).transpose(1, 0, 2)
        ffn = mlp.reshape(shard_rows, 3, 2 * mlp_chunks, LANES).transpose(2, 0, 1, 3)
        return jnp.concatenate(
            [
                qkv.reshape(pairs, shard_rows, half_width),
                out,
                ffn.reshape(2 * mlp_chunks, shard_rows, half_width),
            ],
            axis=0,
        ).reshape(chunks, 2, shard_rows, half_width)

    cos_table, sin_table = rotary_tables(row_count)
    vmem = pl.BlockSpec(memory_space=pltpu.VMEM)
    hbm = pl.BlockSpec(memory_space=pl.ANY)
    smem = pl.BlockSpec(memory_space=pltpu.SMEM)
    linked = shard_rows % 16 == 0 and group % 4 == 0
    planes = group // 4
    inputs = [("doc", smem, doc_ids), ("x_in", hbm, tokens), ("cot_in", hbm, cotangent)]
    inputs += [("cos", vmem, cos_table), ("sin", vmem, sin_table)]
    token_rows = (row_count, width)
    outputs = [
        ("block_out", hbm, jax.ShapeDtypeStruct(token_rows, bf16)),
        ("input_grad", hbm, jax.ShapeDtypeStruct(token_rows, bf16)),
    ]
    by_pair = (pairs, LANES, row_count)
    scratch = [
        ("x", pltpu.VMEM(token_rows, bf16)),
        ("cot", pltpu.VMEM(token_rows, bf16)),
        ("y", pltpu.VMEM(token_rows, f32)),
        ("total", pltpu.VMEM(token_rows, f32)),
        ("dn", pltpu.VMEM(token_rows, f32)),
        ("n1t", pltpu.VMEM((width, row_count), bf16)),
        ("qt", pltpu.VMEM(by_pair, bf16)),
        ("kt", pltpu.VMEM(by_pair, bf16)),
        ("vt", pltpu.VMEM(by_pair, bf16)),
        ("k", pltpu.VMEM((pairs, row_count, LANES), bf16)),
        ("v", pltpu.VMEM((pairs, row_count, LANES), bf16)),
        ("mixt", pltpu.VMEM(by_pair, bf16)),
        ("n2", pltpu.VMEM(token_rows, bf16)),
        ("n2t", pltpu.VMEM(by_pair, bf16)),
        ("cott", pltpu.VMEM((width, row_count), bf16)),
        ("hid", pltpu.VMEM((row_count, 2 * LANES), bf16)),
        ("dgu", pltpu.VMEM((row_count, 4 * LANES), bf16)),
        ("lse", pltpu.VMEM((pairs, 8, row_count), f32)),
        ("cost", pltpu.VMEM((HEAD // 2, row_count), f32)),
        ("sint", pltpu.VMEM((HEAD // 2, row_count), f32)),
        ("acc", pltpu.VMEM((3, LANES, row_count), f32)),
        ("local_sem", pltpu.SemaphoreType.DMA((2,))),
    ]
    if linked:
        lines = (planes, shard_rows, half_width)
        pair_lines = (planes, 2, shard_rows, half_width)
        whole = (planes, 4, shard_rows, half_width)
        gain_rows = (8, width)
        steps = mlp_chunks + 2 * thirds + 1
        inputs += [
            ("attn_in", hbm, attn_weights),
            ("mlp_in", hbm, mlp_weights),
            ("gains_in", vmem, gains),
        ]
        outputs += [
            ("g_out", vmem, jax.ShapeDtypeStruct((chunks, 2, shard_rows, half_width), f32)),
            ("gain_out", vmem, jax.ShapeDtypeStruct((8, LANES), f32)),
        ]
        scratch += [
            ("w", pltpu.VMEM((chunks, 2) + whole, bf16)),
            ("g", pltpu.VMEM((2, 2) + whole, bf16)),
            ("a", pltpu.VMEM((4,) + whole, bf16)),
            ("bs", pltpu.VMEM(pair_lines, bf16)),
            ("b", pltpu.VMEM((2,) + pair_lines, bf16)),
            ("h", pltpu.VMEM(pair_lines, bf16)),
            ("cs", pltpu.VMEM(lines, bf16)),
            ("c", pltpu.VMEM((2,) + lines, bf16)),
            ("kept", pltpu.VMEM(lines, f32)),
            ("ds", pltpu.VMEM(lines, bf16)),
            ("d", pltpu.VMEM((2, planes - 1) + lines[1:], bf16)),
            ("own", pltpu.VMEM(lines[1:], f32)),
            ("gout", pltpu.VMEM((chunks, 2) + lines[1:], f32)),
            ("gt", pltpu.VMEM((planes, 4, 16, LANES), bf16)),
            ("gain", pltpu.VMEM(gain_rows, f32)),
            ("gp", pltpu.VMEM((4,) + gain_rows, f32)),
            ("gz", pltpu.VMEM((planes,) + gain_rows, f32)),
            ("gc", pltpu.VMEM((2,) + gain_rows, f32)),
            ("load_sem", pltpu.SemaphoreType.DMA((4 + 3 * hidden // width,))),
            ("z_sem", pltpu.SemaphoreType.DMA((2, chunks, planes - 1))),
            ("line_sem", pltpu.SemaphoreType.DMA((2, chunks, 7))),
            ("gain_sem", pltpu.SemaphoreType.DMA((2, planes + 2))),
            ("rs_sem", pltpu.SemaphoreType.DMA((2, steps, planes + 3))),
            ("gsum_sem", pltpu.SemaphoreType.DMA((2, planes + 3))),
        ]
        params = pltpu.CompilerParams(
            collective_id=0, has_side_effects=True, vmem_limit_bytes=63 * 2**20
        )
    else:
        packed = pack(attn_weights.astype(bf16), mlp_weights.astype(bf16))
        full = lax.all_gather(packed, "fsdp", axis=2, tiled=True)
        gain_full = lax.all_gather(gains.astype(bf16), "fsdp", axis=1, tiled=True).astype(f32)
        inputs += [("w", vmem, full), ("gain", vmem, gain_full)]
        outputs += [
            ("g_out", hbm, jax.ShapeDtypeStruct((chunks, 2, width, half_width), bf16)),
            ("gain_out", vmem, jax.ShapeDtypeStruct((8, width), f32)),
        ]
        scratch += [
            ("g", pltpu.VMEM((2, 2, width, half_width), bf16)),
            ("g_sem", pltpu.SemaphoreType.DMA((2,))),
        ]
        params = pltpu.CompilerParams(vmem_limit_bytes=63 * 2**20)
    names = [entry[0] for entry in inputs + outputs + scratch]
    block_out, input_grad, part, gain_part = pl.pallas_call(
        functools.partial(block_kernel, linked, names),
        out_shape=[entry[2] for entry in outputs],
        in_specs=[entry[1] for entry in inputs],
        out_specs=[entry[1] for entry in outputs],
        scratch_shapes=[entry[1] for entry in scratch],
        compiler_params=params,
        name="block",
    )(*[entry[2] for entry in inputs])

    if linked:
        grad_gains = gain_part[:2, :shard_rows]
    else:
        part = lax.psum_scatter(part, "fsdp", scatter_dimension=2, tiled=True)
        part = lax.psum(part.astype(bf16), "rep").astype(f32)
        part = jnp.concatenate([part[mlp_chunks + 1 :], part[mlp_chunks:][:1], part[:mlp_chunks]])
        grad_gains = lax.psum_scatter(gain_part[:2], "fsdp", scatter_dimension=1, tiled=True)
        grad_gains = lax.psum(grad_gains, "rep")
    part = part.reshape(2 * chunks, shard_rows, half_width)
    qkv = part[:pairs].reshape(pairs, shard_rows, 3, LANES).transpose(1, 2, 0, 3)
    out = part[pairs : pairs + 2].transpose(1, 0, 2)
    ffn = part[pairs + 2 :].reshape(2 * mlp_chunks, shard_rows, 3, LANES).transpose(1, 2, 0, 3)
    grad_attn = jnp.concatenate(
        [qkv.reshape(shard_rows, 3 * width), out.reshape(shard_rows, width)], axis=1
    )
    grad_mlp = ffn.reshape(shard_rows, 3 * hidden)
    total_tokens = row_count * lax.axis_size("fsdp") * lax.axis_size("rep")
    rate = PEAK_RATE * STEP / (WARMUP * math.sqrt(total_tokens))

    def update(weight, grad, moment, average):
        velocity = MOMENTUM * moment + grad
        weight_new = weight - rate * (grad + MOMENTUM * velocity)
        average_new = DECAY * average + (1.0 - DECAY) * weight_new
        return (weight_new, velocity, average_new, weight_new.astype(bf16))

    kinds = [
        update(attn_weights, grad_attn, moment_attn, ema_attn),
        update(mlp_weights, grad_mlp, moment_mlp, ema_mlp),
        update(gains, grad_gains, moment_gains, ema_gains),
    ]
    return (block_out, input_grad, grad_attn, grad_mlp, grad_gains) + tuple(
        kind[what] for what in range(4) for kind in kinds
    )


def solution(mesh):
    rows = P(("fsdp", "rep"), None)
    shard = P("fsdp", None)
    columns = P(None, "fsdp")
    kinds = (shard, shard, columns)
    return jax.shard_map(
        local,
        mesh=mesh,
        in_specs=(rows, P(("fsdp", "rep")), rows) + kinds * 3,
        out_specs=(rows, rows) + kinds * 5,
        check_vma=False,
    )
```

time: 694 us -> 220 us (0.32)
  waiting for transfers between devices: 488 us -> 0 us
  Pallas kernels: 124 us -> 201 us
  blocking collectives: 44.8 us -> 0 us
  between operations: 14.1 us -> 0.84 us
    reduce_scatter x1 -> x0, waiting for transfers between devices: 218 us -> none  [local(): part = lax.psum_scatter(grads, 'fsdp', scatter_dimension=2, tiled=True)]
    unnamed x5 -> x0, waiting for transfers between devices: 127 us -> none
    all_gather x1 -> x0, waiting for transfers between devices: 127 us -> none  [local(): full = lax.all_gather(packed, 'fsdp', axis=2, tiled=True)]
    pallas_call x1, Pallas kernels: 124 us -> 201 us  [local(): pl.pallas_call(functools.partial(block_kernel, linked, names), out_shape=...]
    all_gather x1 -> x0, blocking collectives: 42.4 us -> none  [local(): lax.all_gather(gains.astype(bf16), 'fsdp', axis=1, tiled=True).astype(f32)]
    psum x1 -> x0, waiting for transfers between devices: 16.3 us -> none  [local(): part = lax.psum(part.astype(bf16), 'rep').astype(f32)]
  transfers between devices with their start and end apart: 4 -> 0, of which waited for: 4 -> 0; matrix products, arithmetic and copies ran while one was open for 1% -> 0% of each run, Pallas kernels for 0% -> 0%
where the time goes in v2:
time: 220 us
  Pallas kernels  201 us (91%)
  local copies, waits for them, and re-layouts  10.8 us (5%)
  other arithmetic  7.05 us (3%)
    pallas_call x1, Pallas kernels, local(): pl.pallas_call(functools.partial(block_kernel, linked, names), out_shape=...  201 us
    unnamed x34, local copies, waits for them, and re-layouts  6.65 us
    convert_element_type x3, other arithmetic, update(): return (weight_new, velocity, average_new, weight_new.astype(bf16))  4.47 us

profile of v2, /device:TPU:0, one launch (start us, length us, event | category | flops | bytes accessed | tf_op | source)
XLA Modules:
  0.0 219.8 jit_solution(17550879459480110664)
XLA Ops:
  0.7 0.0 copy-start.11
  0.7 0.0 copy-start.13
  0.7 0.0 copy-start.14
  0.7 201.0 %block.1 = (bf16[1024,768]{1,0:T(8,128)(2,1)}, bf16[1024,768]{1,0:T(8,128)(2,1)}, f32[12,2,48,384]{3,2,1,0:T(8,128)}, f32[8,128]{1,0:T(8,128)}) custom-call(s32[1024]{0:T(1024)} %refs_0_.1, bf16[1024,768]{1,0:T(8,128)(2,1)} %refs_1_.1, bf16[1024,768]{1,0:T(8,128)(2,1)} %refs_2_.1, f32[4,32,256]{2,1,0:T(8,128)} %constant.6.clone.refs_3_, ...), custom_call_target="tpu_custom_call" | custom-call | tf_op jit(solution)/shard_map/block/pallas_call | solution.py:840
  201.7 0.0 copy-done.11
  201.7 0.0 copy-done.14
  201.7 1.2 fusion
  203.0 0.0 copy-start.12
  203.0 0.0 copy-done.13
  203.0 0.6 add_multiply_fusion.2
  203.6 0.9 slice_bitcast_fusion
  204.5 1.0 slice.17
  205.6 1.4 slice.20
  206.9 0.0 copy-done.12
  206.9 0.2 reshape.55
  207.1 0.3 copy.35
  207.4 0.1 reshape.56
  207.6 0.0 copy-start.4
  207.6 0.5 reshape.58
  208.1 0.0 copy-start.2
  208.1 0.0 copy-start.9
  208.1 0.7 copy.37
  208.8 0.0 copy-done.4
  208.8 0.3 copy-done.2
  209.2 0.2 copy-done.9
  209.3 0.0 copy-start.10
  209.3 0.0 copy-start.8
  209.3 1.1 fusion.2
  210.4 0.0 copy-start.3
  210.4 0.0 copy-start
  210.4 0.0 copy-done.10
  210.4 0.9 add_multiply_fusion.1
  211.3 0.0 copy-done.8
  211.3 0.9 copy-done
  212.2 0.0 copy-start.7
  212.2 2.2 fusion.1
  214.4 0.0 copy-done.3
  214.4 0.0 copy-start.1
  214.4 0.0 copy-done.7
  214.4 0.0 copy-start.6
  214.4 1.1 add_multiply_fusion
  215.5 0.3 copy-done.1
  215.8 0.9 copy-done.6
  216.6 0.0 copy-start.5
  216.6 1.1 copy.45
  217.8 0.8 copy-done.5
  218.6 1.1 copy.46
  (3 shorter events, 0.1 us)
Async XLA Ops:
  0.7 201.1 %copy-start.11 = (f32[2,48]{1,0:T(2,128)S(1)}, f32[2,48]{1,0:T(2,128)}, u32[]{:S(2)}) copy-start(f32[2,48]{1,0:T(2,128)} %refs_7_.1) | copy-start | bytes 1156
  0.7 202.3 %copy-start.13 = (f32[2,48]{1,0:T(2,128)S(1)}, f32[2,48]{1,0:T(2,128)}, u32[]{:S(2)}) copy-start(f32[2,48]{1,0:T(2,128)} %param.25) | copy-start | bytes 1156
  0.7 201.1 %copy-start.14 = (f32[2,48]{1,0:T(2,128)S(1)}, f32[2,48]{1,0:T(2,128)}, u32[]{:S(2)}) copy-start(f32[2,48]{1,0:T(2,128)} %param.22) | copy-start | bytes 1156
  203.0 3.9 %copy-start.12 = (f32[2,48]{1,0:T(2,128)}, f32[2,48]{1,0:T(2,128)S(1)}, u32[]{:S(2)}) copy-start(f32[2,48]{1,0:T(2,128)S(1)} %get-tuple-element.60) | copy-start | bytes 1156
  207.6 1.3 copy-start.4
  208.1 1.1 copy-start.2
  208.1 1.2 copy-start.9
  209.3 1.1 copy-start.10
  209.3 2.0 copy-start.8
  210.4 3.9 %copy-start.3 = (f32[48,3072]{1,0:T(8,128)}, f32[48,3072]{1,0:T(8,128)S(1)}, u32[]{:S(2)}) copy-start(f32[48,3072]{1,0:T(8,128)S(1)} %get-tuple-element.58) | copy-start | bytes 1769476
  210.4 1.8 copy-start
  212.2 2.2 copy-start.7
  214.4 1.4 copy-start.1
  214.4 2.3 %copy-start.6 = (bf16[1024,768]{1,0:T(8,128)(2,1)S(1)}, bf16[1024,768]{1,0:T(8,128)(2,1)}, u32[]{:S(2)}) copy-start(bf16[1024,768]{1,0:T(8,128)(2,1)} %get-tuple-element.53) | copy-start | bytes 4718596
  216.6 2.0 copy-start.5

commit v3 on v2

v3 whole, which is shorter than its diff:
```python
import functools
import math

import jax
import jax.numpy as jnp
import numpy as np
from jax import lax
from jax.experimental import pallas as pl
from jax.experimental.pallas import tpu as pltpu
from jax.sharding import PartitionSpec as P

HEAD = 64
VMEM_BYTES = 67_000_000
STEP = 5
WARMUP = 10
EPSILON = 1e-05
MASKED = -1e30
MOMENTUM = 0.5
DECAY = 0.5
PEAK_RATE = 0.1
LANES = 128
BLOCK = 256
PLAN = {
    ("fwd", 0): [
        ("R", (0, -1, -1, -1, -1, -1)),
        ("S", (-1, -1, 2, -1, 4, -1)),
        ("F", (1, -1, 4, -1, 6, -1)),
        ("T", (-1, -1, 1, -1, -1, 3)),
        ("S", (-1, -1, 3, -1, -1, -1)),
        ("F", (2, -1, 5, -1, -1, -1)),
        ("R", (-1, -1, 1, -1, 2, -1)),
    ],
    ("fwd", 1): [
        ("S", (-1, 1, -1, -1, -1, 5)),
        ("F", (-1, 3, -1, -1, -1, 7)),
        ("T", (-1, -1, -1, 2, -1, -1)),
    ],
    ("wo", 0): [
        ("R", (3,)),
    ],
    ("wo", 1): [
        ("T", (4,)),
    ],
    ("mlp", 0): [
        ("Q", (-1, -1, -1, -1, -1, -1, 0, 1)),
        ("H", (-1, -1, 0, 1, 2, 3, 4, 5)),
        ("S", (6, 7, 8, 9, 10, -1, -1, -1)),
        ("F", (8, 9, -1, -1, -1, -1, -1, -1)),
        ("B", (-1, -1, -1, -1, -1, 0, 2, 3)),
        ("B", (-1, -1, -1, -1, -1, 1, -1, -1)),
        ("T", (-1, -1, -1, -1, -1, -1, -1, 11)),
        ("L", (-1, -1, -1, -1, -1, -1, -1, 0)),
        ("R", (4, 5, 6, 7, 8, 9, 10, 11)),
        ("A", (-1, 0, 1, 2, 3, 4, 5, 6)),
        ("F", (-1, -1, 10, 11, -1, -1, -1, -1)),
        ("S", (-1, -1, -1, -1, -1, 11, -1, -1)),
    ],
    ("mlp", 1): [
        ("T", (5, 6, 7, 8, 9, 10, -1, -1)),
        ("Q", (-1, -1, -1, -1, -1, -1, -1, 2)),
        ("B", (-1, -1, -1, -1, -1, -1, -1, 4)),
    ],
    ("d", 0): [
        ("E", (0,)),
        ("L", (1,)),
        ("H", (6,)),
        ("A", (7,)),
    ],
    ("o", 0): [
        ("X", (0,)),
        ("Q", (3,)),
        ("B", (5,)),
    ],
    ("o", 1): [
        ("L", (2,)),
        ("H", (7,)),
        ("A", (8,)),
    ],
    ("bwd", 0): [
        ("E", (1, -1, -1, -1, -1, -1)),
        ("X", (-1, -1, -1, 4, -1, 6)),
    ],
    ("bwd", 1): [
        ("X", (1, 2, 3, -1, 5, 7)),
        ("E", (-1, 3, 4, 5, 6, -1)),
        ("L", (3, 4, 5, -1, -1, 9)),
        ("Q", (4, -1, -1, 8, 9, -1)),
        ("H", (8, -1, 9, -1, 10, -1)),
        ("B", (6, -1, -1, -1, 10, -1)),
    ],
    ("bwd", 2): [
        ("E", (2, -1, -1, -1, 7, -1)),
        ("L", (-1, -1, 6, 7, 8, -1)),
        ("Q", (5, 6, 7, -1, -1, 10)),
        ("A", (-1, 9, -1, 10, -1, 11)),
        ("B", (7, 8, 9, -1, -1, -1)),
    ],
    ("tail", 0): [
        ("E", (8,)),
    ],
    ("tail", 1): [
    ],
    ("tail", 2): [
        ("X", (8,)),
        ("L", (10,)),
        ("H", (11,)),
        ("B", (11,)),
    ],
    ("tail", 3): [
        ("E", (9,)),
    ],
    ("end", 0): [
        ("X", (9,)),
        ("E", (10,)),
        ("Q", (11,)),
        ("X", (10,)),
        ("L", (11,)),
        ("E", (11,)),
        ("X", (11,)),
    ],
}
HELD = 4

f32 = jnp.float32
bf16 = jnp.bfloat16


def nn(left, right):
    return jnp.dot(left, right, preferred_element_type=f32)


def nt(left, right):
    return lax.dot_general(
        left, right, (((1,), (1,)), ((), ())), preferred_element_type=f32
    )


def in_turn(items, stages):
    values = {}
    for turn in range(len(items) + len(stages) - 1):
        for number, stage in enumerate(stages):
            index = turn - number
            if 0 <= index < len(items):
                values[index] = stage(items[index], *values.get(index, ()))


def rotary_tables(row_count):
    half = HEAD // 2
    frequency = np.float32(10000.0) ** (-np.arange(half, dtype=np.float32) / np.float32(half))
    angles = np.arange(row_count, dtype=np.float32)[None, :] * frequency.astype(np.float32)[:, None]
    angles = angles.astype(np.float64)
    tables = np.stack([np.cos(angles), np.sin(angles)]).astype(np.float32)
    tables = tables.reshape(2, half, row_count // BLOCK, BLOCK).transpose(0, 2, 1, 3)
    return np.ascontiguousarray(tables.reshape(-1, BLOCK))


def rotate_rows(rows, cosine, sine):
    half = HEAD // 2
    first, second = rows[:half], rows[half:]
    return jnp.concatenate(
        [first * cosine - second * sine, second * cosine + first * sine], axis=0
    )


def rms_scale(rows):
    return lax.rsqrt(jnp.mean(rows * rows, axis=-1, keepdims=True) + EPSILON)


class Scratch:
    def __init__(self, names, refs):
        for name, ref in zip(names, refs, strict=True):
            setattr(self, name, ref)


def block_kernel(linked, names, *refs):
    s = Scratch(names, refs)
    row_count, width = s.x.shape
    blocks = row_count // BLOCK
    pairs = width // LANES
    thirds = pairs // 2
    half_width = width // 2
    chunks = s.w.shape[0]
    mlp_chunks = chunks - thirds - 1
    slots = s.g.shape[0]

    def rows_of(i):
        return pl.ds(i * BLOCK, BLOCK)

    def store_pairs(i, value):
        for p in range(pairs):
            s.n2[p, rows_of(i), :] = value[:, p * LANES : (p + 1) * LANES]

    def load_pairs(i):
        return jnp.concatenate([s.n2[p, rows_of(i), :] for p in range(pairs)], axis=1)

    def sums_at(kind, first, count, j):
        return (pl.ds(j * LANES + first, count), pl.ds(kind * BLOCK, BLOCK))

    def load_w(chunk, half):
        return s.w[chunk, half].reshape(width, half_width)

    def store_g(chunk, half, lanes, value):
        low = value.astype(bf16)
        if linked:
            low = low.reshape(s.g.shape[2:5] + (low.shape[1],))
            s.g[chunk % slots, half, :, :, :, lanes] = low
        else:
            s.g[chunk % slots, half, :, lanes] = low

    if linked:
        gather_start, actions, gain_steps = links(s, chunks, thirds, mlp_chunks)
    else:


        def grad_copy(chunk):
            slot = chunk % slots
            return pltpu.make_async_copy(s.g.at[slot], s.g_out.at[chunk], s.g_sem.at[slot])

        actions = {"A": lambda chunk: grad_copy(chunk).start()}
        actions["H"] = lambda chunk: grad_copy(chunk).wait()

    def events(loop, place, index=0):
        for kind, table in PLAN[loop, place]:
            if kind not in actions:
                continue
            if isinstance(index, int):
                if table[index] >= 0:
                    actions[kind](table[index])
                continue
            used = [i for i, entry in enumerate(table) if entry >= 0]
            shift = table[used[0]] - used[0]
            in_line = all(table[i] == i + shift for i in used)
            in_line = in_line and used == list(range(used[0], used[-1] + 1))
            if in_line:
                chunk = index + shift
            else:
                chunk = jnp.int32(table[used[0]])
                for i in used[1:]:
                    chunk = jnp.where(index == i, table[i], chunk)
            if len(used) == len(table):
                actions[kind](chunk)
                continue
            if in_line:
                now = (index >= used[0]) & (index <= used[-1])
            else:
                now = functools.reduce(lambda u, v: u | v, [index == i for i in used])
            pl.when(now)(functools.partial(actions[kind], chunk))

    copies = [
        pltpu.make_async_copy(s.x_in, s.x, s.local_sem.at[0]),
        pltpu.make_async_copy(s.cot_in, s.cot, s.local_sem.at[1]),
    ]
    tables = s.total.at[pl.ds(0, HEAD * blocks), pl.ds(0, BLOCK)]
    copies.append(pltpu.make_async_copy(s.tables, tables, s.local_sem.at[2]))
    for copy in copies:
        copy.start()

    docs = [s.doc[BLOCK * j] for j in range(blocks)]
    bias = [
        [jnp.where(docs[i] == docs[j], 0.0, MASKED).astype(f32) for j in range(i)] + [0.0]
        for i in range(blocks)
    ]
    causal = lax.broadcasted_iota(jnp.int32, (BLOCK, BLOCK), 0) <= lax.broadcasted_iota(
        jnp.int32, (BLOCK, BLOCK), 1
    )

    if linked:
        gather_start[0]()
    copies.pop().wait()
    for i in range(blocks):
        place = sum([(docs[j] == docs[i]).astype(jnp.int32) for j in range(i)], jnp.int32(0))
        for index, table in enumerate([s.cost, s.sint]):
            chosen = None
            for t in range(i + 1):
                first = (index * blocks + t) * (HEAD // 2)
                part = s.total[pl.ds(first, HEAD // 2), pl.ds(0, BLOCK)]
                chosen = part if t == 0 else jnp.where(place == t, part, chosen)
            table[:, rows_of(i)] = chosen
    if linked:
        gather_start[1]()
    for copy in copies:
        copy.wait()
    if linked:
        gather_start[2]()
    if linked:
        gather_start[3]()
    gain_one = s.gain[0:1, :]
    gain_two = s.gain[1:2, :]
    for i in range(blocks):
        stream = s.x[rows_of(i), :].astype(f32)
        normed = (stream * rms_scale(stream) * gain_one).astype(bf16)
        s.n1t[:, rows_of(i)] = normed.T
        s.dn[rows_of(i), :] = jnp.zeros((BLOCK, width), f32)

    def masked_pair(rows, h):
        zero = jnp.zeros((HEAD, BLOCK), bf16)
        parts = [rows[:HEAD], zero] if h == 0 else [zero, rows[HEAD:]]
        return jnp.concatenate(parts, axis=0)

    def scores_of(p, i, h):
        span = (i + 1) * BLOCK
        query = masked_pair(s.qt[p, :, rows_of(i)], h)
        scores = nn(s.k[p, pl.ds(0, span), :], query)
        parts = [scores[j * BLOCK : (j + 1) * BLOCK] for j in range(i + 1)]
        parts[i] = jnp.where(causal, parts[i], MASKED)
        return parts

    bodies = [(i, h) for i in range(blocks) for h in range(2)]

    def attention_forward(p, carry):
        events("fwd", 0, p)
        weights_t = load_w(p // 2, p % 2).T
        for i in range(blocks):
            cosine, sine = s.cost[:, rows_of(i)], s.sint[:, rows_of(i)]
            projected = nn(weights_t, s.n1t[:, rows_of(i)])
            for h in range(2):
                lo, hi = h * HEAD, (h + 1) * HEAD
                query = rotate_rows(projected[lo:hi], cosine, sine).astype(bf16)
                s.qt[p, lo:hi, rows_of(i)] = query * bf16(0.125)
                key = rotate_rows(projected[LANES + lo : LANES + hi], cosine, sine)
                s.kt[p, lo:hi, rows_of(i)] = key.astype(bf16)
            s.vt[p, :, rows_of(i)] = projected[2 * LANES :].astype(bf16)
            s.k[p, rows_of(i), :] = s.kt[p, :, rows_of(i)].T
            s.v[p, rows_of(i), :] = s.vt[p, :, rows_of(i)].T
        events("fwd", 1, p)

        def shares(n, parts):
            i, h = n
            tops = [
                jnp.max(part, axis=0, keepdims=True) + bias[i][j]
                for j, part in enumerate(parts)
            ]
            top = functools.reduce(jnp.maximum, tops)
            exps = [jnp.exp(part - (top - bias[i][j])) for j, part in enumerate(parts)]
            total = sum([jnp.sum(e, axis=0, keepdims=True) for e in exps])
            s.lse[p // 2, pl.ds(2 * (p % 2) + h, 1), rows_of(i)] = top + jnp.log(total)
            return jnp.concatenate([e.astype(bf16) for e in exps], axis=0), 1.0 / total

        def mix(n, exps_low, inverse):
            i, h = n
            heads = pl.ds(h * HEAD, HEAD)
            mixed = nn(s.vt[p, heads, pl.ds(0, (i + 1) * BLOCK)], exps_low)
            s.mixt[p, heads, rows_of(i)] = (mixed * inverse).astype(bf16)

        in_turn(bodies, [lambda n: (scores_of(p, *n),), shares, mix])
        return carry

    lax.fori_loop(0, pairs, attention_forward, 0)

    out_chunk = thirds
    for i in range(blocks):
        if i % 2 == 0:
            events("wo", i // 2)
        mixed = s.mixt[:, :, rows_of(i)].reshape(width, BLOCK).T
        branch = jnp.concatenate(
            [nn(mixed, load_w(out_chunk, half)) for half in range(2)], axis=1
        )
        after = s.x[rows_of(i), :].astype(f32) + branch
        s.y[rows_of(i), :] = after
        s.total[rows_of(i), :] = after
        normed = (after * rms_scale(after) * gain_two).astype(bf16)
        store_pairs(i, normed)
        s.n2t[:, :, rows_of(i)] = normed.T.reshape(pairs, LANES, BLOCK)

    tiles = [pl.ds(t * BLOCK, BLOCK) for t in range(width // BLOCK)]
    for i in range(blocks):
        for tile in tiles:
            s.x[rows_of(i), tile] = s.cot[rows_of(i), tile].T

    def feed_forward(chunk, carry):
        events("mlp", 0, chunk)
        low = [load_w(thirds + 1 + chunk, half) for half in range(2)]
        w_gu = [w[:, : 2 * LANES] for w in low]
        w_gu_all = jnp.concatenate(w_gu, axis=1)
        w_down = jnp.concatenate([w[:, 2 * LANES :] for w in low], axis=1)

        def products(i):
            normed = load_pairs(i)
            d_hidden = nn(s.cot[rows_of(i), :], w_down)
            return d_hidden, [nn(normed, w) for w in w_gu]

        def slopes(i, d_hidden, gate_ups):
            for half, gate_up in enumerate(gate_ups):
                gate, up = gate_up[:, :LANES], gate_up[:, LANES:]
                back = d_hidden[:, half * LANES : (half + 1) * LANES]
                sig = jax.nn.sigmoid(gate)
                silu = gate * sig
                s.hid[rows_of(i), pl.ds(half * LANES, LANES)] = (silu * up).astype(bf16)
                s.dgu[rows_of(i), pl.ds(2 * half * LANES, LANES)] = (
                    back * up * (sig + silu * (1.0 - sig))
                ).astype(bf16)
                s.dgu[rows_of(i), pl.ds((2 * half + 1) * LANES, LANES)] = (
                    back * silu
                ).astype(bf16)
            return ()

        def sums(i):
            s.total[rows_of(i), :] += nt(s.hid[rows_of(i), :], w_down)
            s.dn[rows_of(i), :] += nt(s.dgu[rows_of(i), :], w_gu_all)

        in_turn(list(range(blocks)), [products, slopes, sums])
        events("mlp", 1, chunk)
        n2t = s.n2t[...].reshape(width, row_count)
        for half in range(2):
            store_g(
                chunk,
                half,
                pl.ds(0, 2 * LANES),
                nn(n2t, s.dgu[:, pl.ds(2 * half * LANES, 2 * LANES)]),
            )
        grad_down = jnp.concatenate(
            [
                nn(
                    jnp.concatenate([s.x[rows_of(i), tile] for i in range(blocks)], axis=1),
                    s.hid[...],
                )
                for tile in tiles
            ],
            axis=0,
        )
        for half in range(2):
            store_g(
                chunk,
                half,
                pl.ds(2 * LANES, LANES),
                grad_down[:, half * LANES : (half + 1) * LANES],
            )
        return carry

    lax.fori_loop(0, mlp_chunks, feed_forward, 0)

    events("d", 0)
    x_copy = pltpu.make_async_copy(s.x_in, s.x, s.local_sem.at[1])
    x_copy.start()

    gain_grad_two = jnp.zeros((1, width), f32)
    for i in range(blocks):
        after = s.y[rows_of(i), :]
        scale = rms_scale(after)
        unit = after * scale
        d_normed = s.dn[rows_of(i), :]
        d_unit = d_normed * gain_two
        gain_grad_two += jnp.sum(d_normed * unit, axis=0, keepdims=True)
        grad_after = s.cot[rows_of(i), :].astype(f32) + scale * (
            d_unit - unit * jnp.mean(d_unit * unit, axis=-1, keepdims=True)
        )
        s.y[rows_of(i), :] = grad_after
        store_pairs(i, grad_after.astype(bf16))
        s.cot[rows_of(i), :] = s.total[rows_of(i), :].astype(bf16)
    out_copy = pltpu.make_async_copy(s.cot, s.block_out, s.local_sem.at[0])
    out_copy.start()

    events("o", 0)
    mixt = s.mixt[...].reshape(width, row_count)
    for half in range(2):
        store_g(
            mlp_chunks,
            half,
            pl.ds(0, half_width),
            nn(mixt, jnp.concatenate([s.n2[p] for p in range(half * thirds, (half + 1) * thirds)], axis=1)),
        )
    events("o", 1)
    dmt = s.n2t
    w_out = jnp.concatenate([load_w(out_chunk, half) for half in range(2)], axis=1)
    for i in range(blocks):
        d_mixed = nt(w_out, load_pairs(i))
        dmt[:, :, rows_of(i)] = d_mixed.astype(bf16).reshape(pairs, LANES, BLOCK)

    def attention_backward(p, carry):
        events("bwd", 0, p)
        for j in range(blocks):
            for kind in (1, 2):
                s.total[sums_at(kind, 0, LANES, j)] = jnp.zeros((LANES, BLOCK), f32)
        def begin(n):
            i, h = n
            back = masked_pair(dmt[p, :, rows_of(i)], h)
            return scores_of(p, i, h), nn(s.v[p, pl.ds(0, (i + 1) * BLOCK), :], back)

        def middle(n, parts, d_probs):
            i, h = n
            lse = s.lse[p // 2, pl.ds(2 * (p % 2) + h, 1), rows_of(i)]
            probs = [jnp.exp(part - (lse - bias[i][j])) for j, part in enumerate(parts)]
            probs = jnp.concatenate(probs, axis=0)
            weighted = probs * d_probs
            inner = jnp.sum(weighted, axis=0, keepdims=True)
            return (weighted - probs * inner).astype(bf16), probs.astype(bf16)

        def finish(n, d_scores, probs_low):
            i, h = n
            heads, keys = pl.ds(h * HEAD, HEAD), pl.ds(0, (i + 1) * BLOCK)
            s.total[sums_at(0, h * HEAD, HEAD, i)] = nn(s.kt[p, heads, keys], d_scores)
            d_keys = nt(s.qt[p, heads, rows_of(i)], d_scores)
            d_values = nt(dmt[p, heads, rows_of(i)], probs_low)
            for j in range(i + 1):
                span = slice(j * BLOCK, (j + 1) * BLOCK)
                s.total[sums_at(1, h * HEAD, HEAD, j)] += d_keys[:, span]
                s.total[sums_at(2, h * HEAD, HEAD, j)] += d_values[:, span]

        in_turn(bodies, [begin, middle, finish])
        events("bwd", 1, p)
        for i in range(blocks):
            cosine, sine = s.cost[:, rows_of(i)], -s.sint[:, rows_of(i)]
            pieces = []
            for kind in range(2):
                for h in range(2):
                    piece = s.total[sums_at(kind, h * HEAD, HEAD, i)]
                    piece = rotate_rows(piece, cosine, sine)
                    pieces.append((piece * 0.125 if kind == 0 else piece).astype(bf16))
            s.k[p, rows_of(i), :] = jnp.concatenate(pieces[:2], axis=0).T
            s.v[p, rows_of(i), :] = jnp.concatenate(pieces[2:], axis=0).T
            s.n2[p, rows_of(i), :] = s.total[sums_at(2, 0, LANES, i)].astype(bf16).T
        d_qkv = jnp.concatenate([s.k[p], s.v[p], s.n2[p]], axis=1)
        store_g(
            mlp_chunks + 1 + p // 2, p % 2, pl.ds(0, half_width), nn(s.n1t[...], d_qkv)
        )
        events("bwd", 2, p)
        return carry

    lax.fori_loop(0, pairs, attention_backward, 0)

    x_copy.wait()
    w_qkv_t = jnp.concatenate([load_w(p // 2, p % 2).T for p in range(pairs)], axis=0)
    gain_grad_one = jnp.zeros((1, width), f32)
    for i in range(blocks):
        events("tail", i)
        d_qkv = [
            ref[p, rows_of(i), :] for p in range(pairs) for ref in (s.k, s.v, s.n2)
        ]
        d_normed = nn(jnp.concatenate(d_qkv, axis=1), w_qkv_t)
        stream = s.x[rows_of(i), :].astype(f32)
        scale = rms_scale(stream)
        unit = stream * scale
        d_unit = d_normed * gain_one
        gain_grad_one += jnp.sum(d_normed * unit, axis=0, keepdims=True)
        s.x[rows_of(i), :] = (
            s.y[rows_of(i), :]
            + scale * (d_unit - unit * jnp.mean(d_unit * unit, axis=-1, keepdims=True))
        ).astype(bf16)
    grad_copy_out = pltpu.make_async_copy(s.x, s.input_grad, s.local_sem.at[1])
    grad_copy_out.start()
    gain_grads = jnp.concatenate(
        [gain_grad_one, gain_grad_two, jnp.zeros((6, width), f32)], axis=0
    )
    if linked:
        gain_steps[0](gain_grads)
        for kind, table in PLAN["end", 0]:
            actions[kind](table[0])
            if table[0] == chunks - 1 and kind in "LEX":
                gain_steps["LEX".index(kind) + 1]()
        gain_steps[4]()
    else:
        events("end", 0)
        s.gain_out[...] = gain_grads
    out_copy.wait()
    grad_copy_out.wait()


def links(s, chunks, thirds, mlp_chunks):
    planes = s.w.shape[2]
    me = lax.axis_index("fsdp")
    core = lax.axis_index("rep")
    z, m = me // 4, me % 4
    over_x, over_y, over_both = m + 1 - 2 * (m % 2), (m + 2) % 4, 3 - m
    m1 = (1 - core) * over_x + core * over_y
    m2 = (1 - core) * over_y + core * over_x
    m3 = over_both
    other = 1 - core

    def chip(plane, place):
        return (plane * 4 + place, core)

    sibling = (me, other)

    def far(k):
        return (z + k) % planes

    peers = [chip(far(k), m) for k in range(1, planes)]

    def remote(src, dst, sems, index, device):
        return pltpu.make_async_remote_copy(
            src_ref=src,
            dst_ref=dst,
            send_sem=sems.at[(0,) + index],
            recv_sem=sems.at[(1,) + index],
            device_id=device,
            device_id_type=pl.DeviceIdType.MESH,
        )

    def along_z(chunk, k):
        block = s.w.at[chunk, core, z, m]
        return remote(block, block, s.z_sem, (chunk, k), peers[k])

    def line(chunk, place, index, device):
        block = s.w.at[chunk, core, :, place]
        return remote(block, block, s.line_sem, (chunk, index), device)

    hops = [
        (m, chip(z, m1)),
        (m, chip(z, m2)),
        (m1, chip(z, m2)),
        (m, sibling),
        (m1, sibling),
        (m2, sibling),
        (m3, sibling),
    ]

    def hop(chunk, index):
        return line(chunk, hops[index][0], index, hops[index][1])

    def gain_along_z(k):
        block = s.gt.at[z, m]
        return remote(block, block, s.gain_sem, (k,), peers[k])

    def gain_line(place, index, device):
        block = s.gt.at[:, place]
        return remote(block, block, s.gain_sem, (planes - 1 + index,), device)

    def gain_hop(index):
        return gain_line(hops[index][0], index, hops[index][1])

    width = s.x.shape[1]
    pairs = width // LANES
    shard_rows = s.w.shape[4]
    half_width = s.w.shape[5]
    hidden = s.mlp_in.shape[1] // 3

    def gather_start():
        loads = [
            pltpu.make_async_copy(
                s.attn_in.at[:, pl.ds(k * width, width)],
                s.dn.at[pl.ds(k * shard_rows, shard_rows)],
                s.load_sem.at[k],
            )
            for k in range(4)
        ] + [
            pltpu.make_async_copy(
                s.mlp_in.at[:, pl.ds(k * width, width)],
                s.dn.at[pl.ds((4 + k) * shard_rows, shard_rows)],
                s.load_sem.at[4 + k],
            )
            for k in range(3 * hidden // width)
        ]
        for load in loads:
            load.start()
        barrier = pltpu.get_barrier_semaphore()
        partners = [chip(z, over_x), chip(z, over_y), chip(z, over_both), sibling] + peers
        for partner in partners:
            pl.semaphore_signal(
                barrier, inc=1, device_id=partner, device_id_type=pl.DeviceIdType.MESH
            )
        own = s.gains_in[...].astype(bf16)
        own = jnp.concatenate([own, jnp.zeros((2, LANES - shard_rows), bf16)], axis=1)
        s.gt[z, m] = jnp.concatenate([own, jnp.zeros((14, LANES), bf16)], axis=0)
        for load in loads:
            load.wait()
        for third in range(thirds):
            lane = pl.multiple_of((2 * third + core) * LANES, LANES)
            for kind in range(3):
                s.w[third, core, z, m, :, kind * LANES : (kind + 1) * LANES] = piece(kind, lane)
        lane = pl.multiple_of(core * half_width, LANES)
        s.w[thirds, core, z, m] = s.dn[
            pl.ds(3 * shard_rows, shard_rows), pl.ds(lane, half_width)
        ].astype(bf16)
        pl.semaphore_wait(barrier, len(partners))
        for k in range(planes - 1):
            along_z(0, k).start()
        for k in range(planes - 1):
            gain_along_z(k).start()
        for chunk in range(1, thirds + 1):
            for k in range(planes - 1):
                along_z(chunk, k).start()

    def piece(row, lane):
        rows = s.dn[pl.ds(row * shard_rows, shard_rows), pl.ds(lane, LANES)]
        return rows.astype(bf16)

    def gather_feed_forward():
        for j in range(mlp_chunks):
            for kind in range(3):
                place = kind * hidden + 2 * j * LANES
                row, first = 4 + place // width, place % width
                lane = pl.multiple_of(first + core * LANES, LANES)
                s.w[thirds + 1 + j, core, z, m, :, kind * LANES : (kind + 1) * LANES] = piece(
                    row, lane
                )
            for k in range(planes - 1):
                along_z(thirds + 1 + j, k).start()

    def gather_one():
        first_hop(0)
        for k in range(planes - 1):
            gain_along_z(k).wait()
        gain_hop(0).start()
        gain_hop(1).start()
        gather_feed_forward()

    def gather_two():
        second_hop(0)
        gain_hop(0).wait()
        gain_hop(2).start()

    def gather_three():
        third_hop(0)
        gain_hop(1).wait()
        gain_hop(2).wait()
        rows = jnp.zeros((8, width), f32)
        for d in range(planes * 4):
            tile = s.gt[d // 4, d % 4].astype(f32)[:8]
            wide = jnp.concatenate([tile, jnp.zeros((8, width - LANES), f32)], axis=1)
            rows += pltpu.roll(wide, d * shard_rows, 1) if d else wide
        s.gain[...] = rows

    def ready(chunk):
        for index in range(3, 7):
            hop(chunk, index).wait_recv()
        for k in range(planes - 1):
            along_z(chunk, k).wait_send()
        for index in range(7):
            hop(chunk, index).wait_send()

    def third_hop(chunk):
        hop(chunk, 1).wait_recv()
        hop(chunk, 5).start()
        hop(chunk, 2).wait_recv()
        hop(chunk, 6).start()

    def second_hop(chunk):
        hop(chunk, 0).wait_recv()
        hop(chunk, 2).start()
        hop(chunk, 4).start()

    def first_hop(chunk):
        for k in range(planes - 1):
            along_z(chunk, k).wait_recv()
        for index in (0, 1, 3):
            hop(chunk, index).start()

    def to_sibling(chunk):
        return remote(
            s.g.at[chunk % 2, other], s.a.at[chunk % 2], s.rs_sem, (chunk, 0), sibling
        )

    def to_second(chunk):
        return remote(
            s.h.at[chunk % held, :, pl.ds(2, 2)],
            s.b.at[chunk % 4],
            s.rs_sem,
            (chunk, 1),
            chip(z, m2),
        )

    def to_first(chunk):
        return remote(s.cs.at[chunk % 2], s.c.at[chunk % 4], s.rs_sem, (chunk, 2), chip(z, m1))

    def to_plane(chunk, k):
        return remote(
            s.ds.at[chunk % 2, far(k + 1)],
            s.d.at[chunk % 4, k],
            s.rs_sem,
            (chunk, 3 + k),
            peers[k],
        )

    def place_of(chunk):
        return jnp.where(
            chunk < mlp_chunks,
            thirds + 1 + chunk,
            jnp.where(chunk == mlp_chunks, thirds, chunk - mlp_chunks - 1),
        )

    def half_block(chunk):
        return s.gout.at[chunk % 6, core]

    def to_copy(chunk):
        block = half_block(chunk)
        return remote(block, block, s.rs_sem, (chunk, 2 + planes), sibling)

    def leave(chunk):
        place = place_of(chunk)
        return pltpu.make_async_copy(s.gout.at[chunk % 6], s.g_out.at[place], s.leave_sem.at[chunk])

    held = s.h.shape[0]

    def send_half(chunk):
        to_sibling(chunk).start()

    def add_half(chunk):
        to_sibling(chunk).wait()
        for index, place in enumerate([m, m1, m2, m3]):
            s.h[chunk % held, :, index] = (
                s.g[chunk % 2, core, :, place].astype(f32)
                + s.a[chunk % 2, :, place].astype(f32)
            ).astype(bf16)

    def halves(chunk):
        to_second(chunk).start()

    def quarters(chunk):
        to_second(chunk).wait()
        even = chunk % 2
        s.cs[even] = (
            s.h[chunk % held, :, 1].astype(f32) + s.b[chunk % 4, :, 1].astype(f32)
        ).astype(bf16)
        to_first(chunk).start()
        s.kept[even] = s.h[chunk % held, :, 0].astype(f32) + s.b[chunk % 4, :, 0].astype(f32)

    def lines(chunk):
        to_first(chunk).wait()
        even = chunk % 2
        s.kept[even] = s.kept[even] + s.c[chunk % 4].astype(f32)
        s.ds[even] = s.kept[even].astype(bf16)
        s.own[even] = s.kept[even, z]
        for k in range(planes - 1):
            to_plane(chunk, k).start()

    def last(chunk):
        total = s.own[chunk % 2]
        for k in range(planes - 1):
            to_plane(chunk, k).wait()
            total += s.d[chunk % 4, k].astype(f32)
        half_block(chunk)[...] = total
        to_copy(chunk).start()

    def end(chunk):
        to_copy(chunk).wait()
        leave(chunk).start()
        if isinstance(chunk, int):
            if chunk >= 2:
                leave(chunk - 2).wait()
        else:
            pl.when(chunk >= 2)(lambda: leave(chunk - 2).wait())

    actions = {"F": first_hop, "S": second_hop, "T": third_hop, "R": ready}
    actions.update({"A": send_half, "H": add_half, "B": halves, "Q": quarters})
    actions.update({"L": lines, "E": last, "X": end})

    def plane_sum():
        block = s.gp.at[m]
        return [
            remote(block, block, s.gsum_sem, (k,), chip(z, place))
            for k, place in enumerate([over_x, over_y, over_both])
        ]

    def line_sum():
        block = s.gz.at[z]
        return [
            remote(block, block, s.gsum_sem, (3 + k,), peers[k]) for k in range(planes - 1)
        ]

    def core_sum():
        return remote(s.gc.at[0], s.gc.at[1], s.gsum_sem, (2 + planes,), sibling)

    def gain_begin(value):
        s.gp[m] = value
        for copy in plane_sum():
            copy.start()

    def gain_lines_sum():
        for copy in plane_sum():
            copy.wait()
        s.gz[z] = (s.gp[0] + s.gp[1]) + (s.gp[2] + s.gp[3])
        for copy in line_sum():
            copy.start()

    def gain_cores():
        for copy in line_sum():
            copy.wait()
        total = s.gz[0]
        for k in range(1, planes):
            total += s.gz[k]
        s.gc[0] = total
        core_sum().start()

    def gain_end():
        core_sum().wait()
        total = s.gc[0] + s.gc[1]
        s.gain_out[...] = pltpu.roll(total, (width - me * shard_rows) % width, 1)[:, :LANES]

    def gain_out():
        for chunk in range(chunks - 2, chunks):
            leave(chunk).wait()

    start = (gather_start, gather_one, gather_two, gather_three)
    return start, actions, (gain_begin, gain_lines_sum, gain_cores, gain_end, gain_out)


def update_kernel(rate, names, *refs):
    s = Scratch(names, refs)
    width = s.attn_w.shape[1] // 4
    hidden = s.mlp_w.shape[1] // 3
    pairs = width // LANES
    thirds = pairs // 2
    half_width = width // 2
    whats = ["grad", "next", "velocity", "average", "copy"]

    def rule(weight, grad, moment, average):
        velocity = MOMENTUM * moment + grad
        weight_new = weight - rate * (grad + MOMENTUM * velocity)
        average_new = DECAY * average + (1.0 - DECAY) * weight_new
        return grad, weight_new, velocity, average_new, weight_new.astype(bf16)

    attn_blocks = [
        (kind * width + pair * LANES, LANES, (pair // 2, pair % 2), kind * LANES)
        for kind in range(3)
        for pair in range(pairs)
    ] + [(3 * width + half * half_width, half_width, (thirds, half), 0) for half in range(2)]
    pieces = [("attn", 0, 4 * width, attn_blocks)] + [
        (
            "mlp",
            kind * hidden,
            hidden,
            [
                (kind * hidden + b * LANES, LANES, (thirds + 1 + b // 2, b % 2), kind * LANES)
                for b in range(hidden // LANES)
            ],
        )
        for kind in range(3)
    ]

    def loads(index):
        kind, first, count, _ = pieces[index]
        span = pl.ds(first, count)
        return [
            pltpu.make_async_copy(
                getattr(s, f"{kind}_{what}").at[:, span],
                getattr(s, f"{kind}_{what}_here").at[:, span],
                s.in_sem.at[index, k],
            )
            for k, what in enumerate(["w", "m", "e"])
        ]

    def stores(index):
        kind, first, count, _ = pieces[index]
        span = pl.ds(first, count)
        return [
            pltpu.make_async_copy(
                getattr(s, f"{kind}_{what}_here").at[:, span],
                getattr(s, f"{kind}_{what}").at[:, span],
                s.out_sem.at[index, k],
            )
            for k, what in enumerate(whats)
        ]

    enter = [
        pltpu.make_async_copy(s.out_in, s.pass_here.at[0], s.pass_sem.at[0]),
        pltpu.make_async_copy(s.grad_in, s.pass_here.at[1], s.pass_sem.at[1]),
    ]
    leave = [
        pltpu.make_async_copy(s.pass_here.at[0], s.block_out, s.pass_sem.at[4]),
        pltpu.make_async_copy(s.pass_here.at[1], s.input_grad, s.pass_sem.at[5]),
    ]
    grads = [
        pltpu.make_async_copy(
            s.g.at[pl.ds(0, thirds + 1)], s.g_here.at[pl.ds(0, thirds + 1)], s.pass_sem.at[2]
        ),
        pltpu.make_async_copy(
            s.g.at[pl.ds(thirds + 1, s.g.shape[0] - thirds - 1)],
            s.g_here.at[pl.ds(thirds + 1, s.g.shape[0] - thirds - 1)],
            s.pass_sem.at[3],
        ),
    ]
    grads[0].start()
    for load in loads(0):
        load.start()
    grads[1].start()
    for index in range(1, len(pieces)):
        for load in loads(index):
            load.start()
    for copy in enter:
        copy.start()
    shard_rows = s.attn_w.shape[0]
    results = rule(s.gains_w[...], s.gain_part[:2, :shard_rows], s.gains_m[...], s.gains_e[...])
    for what, result in zip(whats, results, strict=True):
        getattr(s, f"gains_{what}")[...] = result
    for index, (kind, _, _, blocks) in enumerate(pieces):
        if index < 2:
            grads[index].wait()
        for load in loads(index):
            load.wait()
        for first, count, chunk, lane in blocks:
            span = slice(first, first + count)
            results = rule(
                getattr(s, f"{kind}_w_here")[:, span],
                s.g_here[chunk[0], chunk[1], :, lane : lane + count],
                getattr(s, f"{kind}_m_here")[:, span],
                getattr(s, f"{kind}_e_here")[:, span],
            )
            for what, result in zip(whats, results, strict=True):
                getattr(s, f"{kind}_{what}_here")[:, span] = result
        for store in stores(index):
            store.start()
    for copy_in, copy_out in zip(enter, leave, strict=True):
        copy_in.wait()
        copy_out.start()
    for index in range(len(pieces)):
        for store in stores(index):
            store.wait()
    for copy in leave:
        copy.wait()


def local(
    tokens,
    doc_ids,
    cotangent,
    attn_weights,
    mlp_weights,
    gains,
    moment_attn,
    moment_mlp,
    moment_gains,
    ema_attn,
    ema_mlp,
    ema_gains,
):
    row_count, width = tokens.shape
    shard_rows = attn_weights.shape[0]
    group = width // shard_rows
    pairs = width // LANES
    hidden = mlp_weights.shape[1] // 3
    half_width = width // 2
    thirds = pairs // 2
    mlp_chunks = hidden // (2 * LANES)
    chunks = thirds + 1 + mlp_chunks

    def pack(attn, mlp):
        qkv = attn[:, : 3 * width].reshape(shard_rows, 3, pairs, LANES).transpose(2, 0, 1, 3)
        out = attn[:, 3 * width :].reshape(shard_rows, 2, half_width).transpose(1, 0, 2)
        ffn = mlp.reshape(shard_rows, 3, 2 * mlp_chunks, LANES).transpose(2, 0, 1, 3)
        return jnp.concatenate(
            [
                qkv.reshape(pairs, shard_rows, half_width),
                out,
                ffn.reshape(2 * mlp_chunks, shard_rows, half_width),
            ],
            axis=0,
        ).reshape(chunks, 2, shard_rows, half_width)

    vmem = pl.BlockSpec(memory_space=pltpu.VMEM)
    hbm = pl.BlockSpec(memory_space=pl.ANY)
    smem = pl.BlockSpec(memory_space=pltpu.SMEM)
    linked = shard_rows % 16 == 0 and group % 4 == 0
    planes = group // 4
    inputs = [("doc", smem, doc_ids), ("x_in", hbm, tokens), ("cot_in", hbm, cotangent)]
    inputs += [("tables", hbm, rotary_tables(row_count))]
    token_rows = (row_count, width)
    outputs = [
        ("block_out", hbm, jax.ShapeDtypeStruct(token_rows, bf16)),
        ("input_grad", hbm, jax.ShapeDtypeStruct(token_rows, bf16)),
    ]
    by_pair = (pairs, LANES, row_count)
    scratch = [
        ("x", pltpu.VMEM(token_rows, bf16)),
        ("cot", pltpu.VMEM(token_rows, bf16)),
        ("y", pltpu.VMEM(token_rows, f32)),
        ("total", pltpu.VMEM(token_rows, f32)),
        ("dn", pltpu.VMEM(token_rows, f32)),
        ("n1t", pltpu.VMEM((width, row_count), bf16)),
        ("qt", pltpu.VMEM(by_pair, bf16)),
        ("kt", pltpu.VMEM(by_pair, bf16)),
        ("vt", pltpu.VMEM(by_pair, bf16)),
        ("k", pltpu.VMEM((pairs, row_count, LANES), bf16)),
        ("v", pltpu.VMEM((pairs, row_count, LANES), bf16)),
        ("mixt", pltpu.VMEM(by_pair, bf16)),
        ("n2", pltpu.VMEM((pairs, row_count, LANES), bf16)),
        ("n2t", pltpu.VMEM(by_pair, bf16)),
        ("hid", pltpu.VMEM((row_count, 2 * LANES), bf16)),
        ("dgu", pltpu.VMEM((row_count, 4 * LANES), bf16)),
        ("lse", pltpu.VMEM((pairs // 2, 8, row_count), f32)),
        ("cost", pltpu.VMEM((HEAD // 2, row_count), f32)),
        ("sint", pltpu.VMEM((HEAD // 2, row_count), f32)),
        ("local_sem", pltpu.SemaphoreType.DMA((3,))),
    ]
    if linked:
        lines = (planes, shard_rows, half_width)
        pair_lines = (planes, 2, shard_rows, half_width)
        whole = (planes, 4, shard_rows, half_width)
        gain_rows = (8, width)
        inputs += [
            ("attn_in", hbm, attn_weights),
            ("mlp_in", hbm, mlp_weights),
            ("gains_in", vmem, gains),
        ]
        outputs += [
            ("g_out", hbm, jax.ShapeDtypeStruct((chunks, 2, shard_rows, half_width), f32)),
            ("gain_out", vmem, jax.ShapeDtypeStruct((8, LANES), f32)),
        ]
        scratch += [
            ("w", pltpu.VMEM((chunks, 2) + whole, bf16)),
            ("g", pltpu.VMEM((2, 2) + whole, bf16)),
            ("a", pltpu.VMEM((2,) + whole, bf16)),
            ("h", pltpu.VMEM((HELD,) + whole, bf16)),
            ("b", pltpu.VMEM((4,) + pair_lines, bf16)),
            ("cs", pltpu.VMEM((2,) + lines, bf16)),
            ("c", pltpu.VMEM((4,) + lines, bf16)),
            ("kept", pltpu.VMEM((2,) + lines, f32)),
            ("ds", pltpu.VMEM((2,) + lines, bf16)),
            ("d", pltpu.VMEM((4, planes - 1) + lines[1:], bf16)),
            ("own", pltpu.VMEM((2,) + lines[1:], f32)),
            ("gout", pltpu.VMEM((6, 2) + lines[1:], f32)),
            ("gt", pltpu.VMEM((planes, 4, 16, LANES), bf16)),
            ("gain", pltpu.VMEM(gain_rows, f32)),
            ("gp", pltpu.VMEM((4,) + gain_rows, f32)),
            ("gz", pltpu.VMEM((planes,) + gain_rows, f32)),
            ("gc", pltpu.VMEM((2,) + gain_rows, f32)),
            ("load_sem", pltpu.SemaphoreType.DMA((4 + 3 * hidden // width,))),
            ("z_sem", pltpu.SemaphoreType.DMA((2, chunks, planes - 1))),
            ("line_sem", pltpu.SemaphoreType.DMA((2, chunks, 7))),
            ("gain_sem", pltpu.SemaphoreType.DMA((2, planes + 2))),
            ("rs_sem", pltpu.SemaphoreType.DMA((2, chunks, planes + 3))),
            ("leave_sem", pltpu.SemaphoreType.DMA((chunks,))),
            ("gsum_sem", pltpu.SemaphoreType.DMA((2, planes + 3))),
        ]
        params = pltpu.CompilerParams(
            collective_id=0, has_side_effects=True, vmem_limit_bytes=VMEM_BYTES
        )
    else:
        packed = pack(attn_weights.astype(bf16), mlp_weights.astype(bf16))
        full = lax.all_gather(packed, "fsdp", axis=2, tiled=True)
        gain_full = lax.all_gather(gains.astype(bf16), "fsdp", axis=1, tiled=True).astype(f32)
        inputs += [("w", vmem, full), ("gain", vmem, gain_full)]
        outputs += [
            ("g_out", hbm, jax.ShapeDtypeStruct((chunks, 2, width, half_width), bf16)),
            ("gain_out", vmem, jax.ShapeDtypeStruct((8, width), f32)),
        ]
        scratch += [
            ("g", pltpu.VMEM((2, 2, width, half_width), bf16)),
            ("g_sem", pltpu.SemaphoreType.DMA((2,))),
        ]
        params = pltpu.CompilerParams(vmem_limit_bytes=63 * 2**20)
    names = [entry[0] for entry in inputs + outputs + scratch]
    block_out, input_grad, part, gain_part = pl.pallas_call(
        functools.partial(block_kernel, linked, names),
        out_shape=[entry[2] for entry in outputs],
        in_specs=[entry[1] for entry in inputs],
        out_specs=[entry[1] for entry in outputs],
        scratch_shapes=[entry[1] for entry in scratch],
        compiler_params=params,
        name="block",
    )(*[entry[2] for entry in inputs])

    if not linked:
        part = lax.psum_scatter(part, "fsdp", scatter_dimension=2, tiled=True)
        part = lax.psum(part, "rep").astype(f32)
        part = jnp.concatenate([part[mlp_chunks + 1 :], part[mlp_chunks:][:1], part[:mlp_chunks]])
        gain_part = lax.psum_scatter(gain_part[:2], "fsdp", scatter_dimension=1, tiled=True)
        gain_part = lax.psum(gain_part, "rep")

    total_tokens = row_count * lax.axis_size("fsdp") * lax.axis_size("rep")
    rate = PEAK_RATE * STEP / (WARMUP * math.sqrt(total_tokens))

    sources = {
        "w": (attn_weights, mlp_weights, gains),
        "m": (moment_attn, moment_mlp, moment_gains),
        "e": (ema_attn, ema_mlp, ema_gains),
    }
    kinds = ["attn", "mlp", "gains"]
    whats = ["grad", "next", "velocity", "average", "copy"]
    inputs = [("out_in", hbm, block_out), ("grad_in", hbm, input_grad), ("g", hbm, part)]
    inputs += [("gain_part", vmem, gain_part)]
    outputs = [("block_out", hbm, block_out), ("input_grad", hbm, input_grad)]
    scratch = []
    for what, arrays in sources.items():
        for kind, array in zip(kinds, arrays, strict=True):
            inputs.append((f"{kind}_{what}", vmem if kind == "gains" else hbm, array))
            if kind != "gains":
                scratch.append((f"{kind}_{what}_here", pltpu.VMEM(array.shape, f32)))
    for what in whats:
        for kind, array in zip(kinds, sources["w"], strict=True):
            dtype = bf16 if what == "copy" else f32
            place = vmem if kind == "gains" else hbm
            outputs.append(
                (f"{kind}_{what}", place, jax.ShapeDtypeStruct(array.shape, dtype))
            )
            if kind != "gains":
                scratch.append((f"{kind}_{what}_here", pltpu.VMEM(array.shape, dtype)))
    scratch += [
        ("g_here", pltpu.VMEM(part.shape, f32)),
        ("in_sem", pltpu.SemaphoreType.DMA((4, 3))),
        ("out_sem", pltpu.SemaphoreType.DMA((4, 5))),
        ("pass_here", pltpu.VMEM((2,) + block_out.shape, bf16)),
        ("pass_sem", pltpu.SemaphoreType.DMA((6,))),
    ]
    names = [entry[0] for entry in inputs + outputs + scratch]
    return pl.pallas_call(
        functools.partial(update_kernel, rate, names),
        out_shape=[jax.ShapeDtypeStruct(entry[2].shape, entry[2].dtype) for entry in outputs],
        in_specs=[entry[1] for entry in inputs],
        out_specs=[entry[1] for entry in outputs],
        scratch_shapes=[entry[1] for entry in scratch],
        compiler_params=pltpu.CompilerParams(vmem_limit_bytes=63 * 2**20),
        name="update",
    )(*[entry[2] for entry in inputs])


def solution(mesh):
    rows = P(("fsdp", "rep"), None)
    shard = P("fsdp", None)
    columns = P(None, "fsdp")
    kinds = (shard, shard, columns)
    return jax.shard_map(
        local,
        mesh=mesh,
        in_specs=(rows, P(("fsdp", "rep")), rows) + kinds * 3,
        out_specs=(rows, rows) + kinds * 5,
        check_vma=False,
    )
```

time: 220 us -> 169 us (0.77)
  Pallas kernels: 201 us -> 168 us
  local copies, waits for them, and re-layouts: 10.8 us -> 0 us
  other arithmetic: 7.05 us -> 0 us
    pallas_call x1, Pallas kernels: 201 us -> 159 us  [local(): pl.pallas_call(functools.partial(block_kernel, linked, names), out_shape=...]
    pallas_call x0 -> x1, Pallas kernels: none -> 8.53 us  [local(): pl.pallas_call(functools.partial(update_kernel, rate, names), out_shape=[...]
    unnamed x34 -> x0, local copies, waits for them, and re-layouts: 6.65 us -> none
    convert_element_type x3 -> x0, other arithmetic: 4.47 us -> none  [update(): return (weight_new, velocity, average_new, weight_new.astype(bf16))]
    add x3 -> x0, other arithmetic: 2.58 us -> none  [update(): average_new = DECAY * average + (1.0 - DECAY) * weight_new]
    slice x2 -> x0, local copies, waits for them, and re-layouts: 2.39 us -> none  [the longest x1 1.35 us: local(): part[pairs + 2:].reshape(2 * mlp_chunks, shard_rows, 3, LANES)]
where the time goes in v3:
time: 169 us
  Pallas kernels  168 us (99%)
    pallas_call x1, Pallas kernels, local(): pl.pallas_call(functools.partial(block_kernel, linked, names), out_shape=...  159 us
    pallas_call x1, Pallas kernels, local(): pl.pallas_call(functools.partial(update_kernel, rate, names), out_shape=[...  8.53 us

profile of v3, /device:TPU:0, one launch (start us, length us, event | category | flops | bytes accessed | tf_op | source)
XLA Modules:
  0.0 168.7 jit_solution(14939969764021102667)
XLA Ops:
  0.7 159.3 %block.1 = (bf16[1024,768]{1,0:T(8,128)(2,1)}, bf16[1024,768]{1,0:T(8,128)(2,1)}, f32[12,2,48,384]{3,2,1,0:T(8,128)}, f32[8,128]{1,0:T(8,128)}) custom-call(s32[1024]{0:T(1024)} %refs_0_.1, bf16[1024,768]{1,0:T(8,128)(2,1)} %refs_1_.1, bf16[1024,768]{1,0:T(8,128)(2,1)} %refs_2_.1, f32[256,256]{1,0:T(8,128)} %constant.2.clone.refs_3_, f32[48,3072]{1,0:T(8,128)} %refs_4_.3, ...), custom_call_target="tpu_custom_call" | custom-call | tf_op jit(solution)/shard_map/block/pallas_call | solution.py:1132
  160.0 8.5 %update.1 = (bf16[1024,768]{1,0:T(8,128)(2,1)}, bf16[1024,768]{1,0:T(8,128)(2,1)}, f32[48,3072]{1,0:T(8,128)}, f32[48,6144]{1,0:T(8,128)}, f32[2,48]{1,0:T(2,128...) custom-call(bf16[1024,768]{1,0:T(8,128)(2,1)} %get-tuple-element.21., ...), custom_call_target="tpu_custom_call" | custom-call | tf_op jit(solution)/shard_map/update/pallas_call | solution.py:1185

commit v4 on v3

--- a/solution.py
+++ b/solution.py
@@ -21,105 +21,126 @@
 LANES = 128
 BLOCK = 256
 PLAN = {
+    ("pre", 0): [
+        ("F", (1,)),
+        ("F", (2,)),
+    ],
     ("fwd", 0): [
-        ("R", (0, -1, -1, -1, -1, -1)),
-        ("S", (-1, -1, 2, -1, 4, -1)),
-        ("F", (1, -1, 4, -1, 6, -1)),
-        ("T", (-1, -1, 1, -1, -1, 3)),
-        ("S", (-1, -1, 3, -1, -1, -1)),
-        ("F", (2, -1, 5, -1, -1, -1)),
-        ("R", (-1, -1, 1, -1, 2, -1)),
+        ("S", (1, -1, 4)),
+        ("F", (3, 5, 7)),
+        ("T", (-1, 1, -1)),
+        ("S", (-1, 3, -1)),
+        ("R", (0, 1, 2)),
+        ("F", (-1, 6, -1)),
     ],
     ("fwd", 1): [
-        ("S", (-1, 1, -1, -1, -1, 5)),
-        ("F", (-1, 3, -1, -1, -1, 7)),
-        ("T", (-1, -1, -1, 2, -1, -1)),
+        ("S", (2, -1, 5)),
+        ("F", (4, -1, -1)),
+        ("f", (-1, -1, 8)),
+    ],
+    ("fwd", 2): [
+        ("T", (-1, 2, 3)),
     ],
     ("wo", 0): [
+        ("S", (6,)),
+        ("f", (9,)),
         ("R", (3,)),
     ],
     ("wo", 1): [
-        ("T", (4,)),
     ],
     ("mlp", 0): [
-        ("Q", (-1, -1, -1, -1, -1, -1, 0, 1)),
-        ("H", (-1, -1, 0, 1, 2, 3, 4, 5)),
-        ("S", (6, 7, 8, 9, 10, -1, -1, -1)),
-        ("F", (8, 9, -1, -1, -1, -1, -1, -1)),
-        ("B", (-1, -1, -1, -1, -1, 0, 2, 3)),
-        ("B", (-1, -1, -1, -1, -1, 1, -1, -1)),
-        ("T", (-1, -1, -1, -1, -1, -1, -1, 11)),
+        ("T", (4, -1, -1, 8, -1, -1, 11, -1)),
+        ("S", (7, -1, -1, -1, -1, -1, -1, -1)),
+        ("s", (-1, 8, -1, 11, -1, -1, -1, -1)),
+        ("f", (10, 11, -1, -1, -1, -1, -1, -1)),
+        ("R", (4, 5, 6, -1, -1, -1, 10, -1)),
+        ("T", (-1, -1, 7, -1, -1, -1, -1, -1)),
+        ("H", (-1, -1, -1, 1, 2, -1, -1, -1)),
+        ("R", (-1, -1, -1, -1, 9, -1, -1, -1)),
+        ("Q", (-1, -1, -1, -1, -1, 0, -1, -1)),
         ("L", (-1, -1, -1, -1, -1, -1, -1, 0)),
-        ("R", (4, 5, 6, 7, 8, 9, 10, 11)),
         ("A", (-1, 0, 1, 2, 3, 4, 5, 6)),
-        ("F", (-1, -1, 10, 11, -1, -1, -1, -1)),
-        ("S", (-1, -1, -1, -1, -1, 11, -1, -1)),
+        ("B", (-1, -1, -1, 1, -1, 2, -1, -1)),
     ],
     ("mlp", 1): [
-        ("T", (5, 6, 7, 8, 9, 10, -1, -1)),
-        ("Q", (-1, -1, -1, -1, -1, -1, -1, 2)),
-        ("B", (-1, -1, -1, -1, -1, -1, -1, 4)),
+        ("T", (5, 6, -1, 9, -1, 10, -1, -1)),
+        ("s", (-1, 9, 10, -1, -1, -1, -1, -1)),
+        ("R", (-1, -1, 7, 8, -1, -1, 11, -1)),
+        ("Q", (-1, -1, -1, -1, -1, -1, 1, -1)),
+        ("H", (-1, 0, -1, -1, 3, 4, 5, -1)),
+        ("B", (-1, 0, -1, -1, -1, -1, 3, -1)),
     ],
     ("d", 0): [
-        ("E", (0,)),
+        ("Q", (2,)),
+        ("H", (6,)),
         ("L", (1,)),
-        ("H", (6,)),
         ("A", (7,)),
+        ("B", (4,)),
     ],
     ("o", 0): [
-        ("X", (0,)),
+    ],
+    ("o", 1): [
         ("Q", (3,)),
-        ("B", (5,)),
-    ],
-    ("o", 1): [
-        ("L", (2,)),
         ("H", (7,)),
         ("A", (8,)),
+        ("B", (5,)),
     ],
     ("bwd", 0): [
-        ("E", (1, -1, -1, -1, -1, -1)),
-        ("X", (-1, -1, -1, 4, -1, 6)),
+        ("E", (0, -1, -1)),
+        ("L", (2, -1, -1)),
     ],
     ("bwd", 1): [
-        ("X", (1, 2, 3, -1, 5, 7)),
-        ("E", (-1, 3, 4, 5, 6, -1)),
-        ("L", (3, 4, 5, -1, -1, 9)),
-        ("Q", (4, -1, -1, 8, 9, -1)),
-        ("H", (8, -1, 9, -1, 10, -1)),
-        ("B", (6, -1, -1, -1, 10, -1)),
+        ("E", (-1, -1, 4)),
+        ("L", (-1, 4, 6)),
+        ("H", (-1, 9, 10)),
     ],
     ("bwd", 2): [
-        ("E", (2, -1, -1, -1, 7, -1)),
-        ("L", (-1, -1, 6, 7, 8, -1)),
-        ("Q", (5, 6, 7, -1, -1, 10)),
-        ("A", (-1, 9, -1, 10, -1, 11)),
-        ("B", (7, 8, 9, -1, -1, -1)),
+        ("E", (1, -1, -1)),
+        ("Q", (4, -1, 8)),
+        ("H", (8, -1, -1)),
+        ("B", (6, -1, 10)),
+    ],
+    ("bwd", 3): [
+        ("E", (-1, 3, 5)),
+        ("L", (3, 5, 7)),
+        ("Q", (-1, 6, -1)),
+        ("B", (-1, 8, -1)),
+    ],
+    ("bwd", 4): [
+    ],
+    ("bwd", 5): [
+        ("E", (2, -1, -1)),
+        ("Q", (5, 7, 9)),
+        ("A", (9, 10, 11)),
+        ("B", (7, 9, -1)),
     ],
     ("tail", 0): [
-        ("E", (8,)),
     ],
     ("tail", 1): [
-    ],
-    ("tail", 2): [
-        ("X", (8,)),
-        ("L", (10,)),
+        ("E", (6,)),
+        ("L", (8,)),
         ("H", (11,)),
         ("B", (11,)),
     ],
+    ("tail", 2): [
+        ("Q", (10,)),
+    ],
     ("tail", 3): [
+        ("E", (7,)),
+        ("L", (9,)),
+    ],
+    ("end", 0): [
+        ("Q", (11,)),
+        ("E", (8,)),
+        ("L", (10,)),
         ("E", (9,)),
-    ],
-    ("end", 0): [
-        ("X", (9,)),
+        ("L", (11,)),
         ("E", (10,)),
-        ("Q", (11,)),
-        ("X", (10,)),
-        ("L", (11,)),
         ("E", (11,)),
-        ("X", (11,)),
     ],
 }
 HELD = 4
+LATE = 8
 
 f32 = jnp.float32
 bf16 = jnp.bfloat16
@@ -135,9 +156,11 @@
     )
 
 
-def in_turn(items, stages):
+def in_turn(items, stages, breaks=None):
     values = {}
     for turn in range(len(items) + len(stages) - 1):
+        if breaks and turn in breaks:
+            breaks[turn]()
         for number, stage in enumerate(stages):
             index = turn - number
             if 0 <= index < len(items):
@@ -196,14 +219,26 @@
     def sums_at(kind, first, count, j):
         return (pl.ds(j * LANES + first, count), pl.ds(kind * BLOCK, BLOCK))
 
+    places = [[0, 1, 2, 3], [0, 2, 1, 3]]
+
     def load_w(chunk, half):
-        return s.w[chunk, half].reshape(width, half_width)
+        if not linked:
+            return s.w[chunk, half]
+        if half == 0:
+            return s.w[chunk, 0].reshape(width, half_width)
+        parts = [s.w[chunk, 1, z, place] for z in range(s.w.shape[2]) for place in places[1]]
+        return jnp.concatenate(parts, axis=0)
 
     def store_g(chunk, half, lanes, value):
         low = value.astype(bf16)
-        if linked:
+        if linked and half == 0:
             low = low.reshape(s.g.shape[2:5] + (low.shape[1],))
-            s.g[chunk % slots, half, :, :, :, lanes] = low
+            s.g[chunk % slots, 0, :, :, :, lanes] = low
+        elif linked:
+            low = low.reshape((-1,) + s.g.shape[4:5] + (low.shape[1],))
+            for z in range(s.g.shape[2]):
+                for index, place in enumerate(places[1]):
+                    s.g[chunk % slots, 1, z, place, :, lanes] = low[4 * z + index]
         else:
             s.g[chunk % slots, half, :, lanes] = low
 
@@ -282,6 +317,7 @@
         copy.wait()
     if linked:
         gather_start[2]()
+        events("pre", 0)
     if linked:
         gather_start[3]()
     gain_one = s.gain[0:1, :]
@@ -305,11 +341,16 @@
         parts[i] = jnp.where(causal, parts[i], MASKED)
         return parts
 
-    bodies = [(i, h) for i in range(blocks) for h in range(2)]
-
-    def attention_forward(p, carry):
-        events("fwd", 0, p)
-        weights_t = load_w(p // 2, p % 2).T
+    mixed_order = [i for j in range(blocks // 2) for i in (blocks - 1 - j, j)]
+    bodies = [(q, i, h) for q in range(2) for h in range(2) for i in mixed_order]
+    half_way = 2 * blocks
+
+    def lse_at(p, i, h):
+        return (p // 2, pl.ds(2 * (p % 2) + h, 1), rows_of(i))
+
+    def project(third, q):
+        p = 2 * third + q
+        weights_t = load_w(third, q).T
         for i in range(blocks):
             cosine, sine = s.cost[:, rows_of(i)], s.sint[:, rows_of(i)]
             projected = nn(weights_t, s.n1t[:, rows_of(i)])
@@ -322,10 +363,20 @@
             s.vt[p, :, rows_of(i)] = projected[2 * LANES :].astype(bf16)
             s.k[p, rows_of(i), :] = s.kt[p, :, rows_of(i)].T
             s.v[p, rows_of(i), :] = s.vt[p, :, rows_of(i)].T
-        events("fwd", 1, p)
+
+    def attention_forward(third, carry):
+        events("fwd", 0, third)
+        project(third, 0)
+        project(third, 1)
+        events("fwd", 1, third)
+
+        def scores(n):
+            q, i, h = n
+            return (scores_of(2 * third + q, i, h),)
 
         def shares(n, parts):
-            i, h = n
+            q, i, h = n
+            p = 2 * third + q
             tops = [
                 jnp.max(part, axis=0, keepdims=True) + bias[i][j]
                 for j, part in enumerate(parts)
@@ -333,19 +384,24 @@
             top = functools.reduce(jnp.maximum, tops)
             exps = [jnp.exp(part - (top - bias[i][j])) for j, part in enumerate(parts)]
             total = sum([jnp.sum(e, axis=0, keepdims=True) for e in exps])
-            s.lse[p // 2, pl.ds(2 * (p % 2) + h, 1), rows_of(i)] = top + jnp.log(total)
+            s.lse[lse_at(p, i, h)] = top + jnp.log(total)
             return jnp.concatenate([e.astype(bf16) for e in exps], axis=0), 1.0 / total
 
         def mix(n, exps_low, inverse):
-            i, h = n
+            q, i, h = n
+            p = 2 * third + q
             heads = pl.ds(h * HEAD, HEAD)
             mixed = nn(s.vt[p, heads, pl.ds(0, (i + 1) * BLOCK)], exps_low)
             s.mixt[p, heads, rows_of(i)] = (mixed * inverse).astype(bf16)
 
-        in_turn(bodies, [lambda n: (scores_of(p, *n),), shares, mix])
+        in_turn(
+            bodies,
+            [scores, shares, mix],
+            {half_way: lambda: events("fwd", 2, third)},
+        )
         return carry
 
-    lax.fori_loop(0, pairs, attention_forward, 0)
+    lax.fori_loop(0, thirds, attention_forward, 0)
 
     out_chunk = thirds
     for i in range(blocks):
@@ -466,19 +522,33 @@
         d_mixed = nt(w_out, load_pairs(i))
         dmt[:, :, rows_of(i)] = d_mixed.astype(bf16).reshape(pairs, LANES, BLOCK)
 
-    def attention_backward(p, carry):
-        events("bwd", 0, p)
-        for j in range(blocks):
+    def turn_back(p, q, i):
+        cosine, sine = s.cost[:, rows_of(i)], -s.sint[:, rows_of(i)]
+        pieces = []
+        for kind in range(2):
+            for h in range(2):
+                piece = s.total[sums_at(kind, h * HEAD, HEAD, q * blocks + i)]
+                piece = rotate_rows(piece, cosine, sine)
+                pieces.append((piece * 0.125 if kind == 0 else piece).astype(bf16))
+        s.k[p, rows_of(i), :] = jnp.concatenate(pieces[:2], axis=0).T
+        s.v[p, rows_of(i), :] = jnp.concatenate(pieces[2:], axis=0).T
+        s.n2[p, rows_of(i), :] = s.total[sums_at(2, 0, LANES, q * blocks + i)].astype(bf16).T
+
+    def attention_backward(third, carry):
+        events("bwd", 0, third)
+        for j in range(2 * blocks):
             for kind in (1, 2):
                 s.total[sums_at(kind, 0, LANES, j)] = jnp.zeros((LANES, BLOCK), f32)
+
         def begin(n):
-            i, h = n
+            q, i, h = n
+            p = 2 * third + q
             back = masked_pair(dmt[p, :, rows_of(i)], h)
             return scores_of(p, i, h), nn(s.v[p, pl.ds(0, (i + 1) * BLOCK), :], back)
 
         def middle(n, parts, d_probs):
-            i, h = n
-            lse = s.lse[p // 2, pl.ds(2 * (p % 2) + h, 1), rows_of(i)]
+            q, i, h = n
+            lse = s.lse[lse_at(2 * third + q, i, h)]
             probs = [jnp.exp(part - (lse - bias[i][j])) for j, part in enumerate(parts)]
             probs = jnp.concatenate(probs, axis=0)
             weighted = probs * d_probs
@@ -486,37 +556,44 @@
             return (weighted - probs * inner).astype(bf16), probs.astype(bf16)
 
         def finish(n, d_scores, probs_low):
-            i, h = n
+            q, i, h = n
+            p = 2 * third + q
             heads, keys = pl.ds(h * HEAD, HEAD), pl.ds(0, (i + 1) * BLOCK)
-            s.total[sums_at(0, h * HEAD, HEAD, i)] = nn(s.kt[p, heads, keys], d_scores)
+            s.total[sums_at(0, h * HEAD, HEAD, q * blocks + i)] = nn(
+                s.kt[p, heads, keys], d_scores
+            )
             d_keys = nt(s.qt[p, heads, rows_of(i)], d_scores)
             d_values = nt(dmt[p, heads, rows_of(i)], probs_low)
             for j in range(i + 1):
                 span = slice(j * BLOCK, (j + 1) * BLOCK)
-                s.total[sums_at(1, h * HEAD, HEAD, j)] += d_keys[:, span]
-                s.total[sums_at(2, h * HEAD, HEAD, j)] += d_values[:, span]
-
-        in_turn(bodies, [begin, middle, finish])
-        events("bwd", 1, p)
+                s.total[sums_at(1, h * HEAD, HEAD, q * blocks + j)] += d_keys[:, span]
+                s.total[sums_at(2, h * HEAD, HEAD, q * blocks + j)] += d_values[:, span]
+            number = bodies.index(n) - half_way
+            if 0 <= number < blocks:
+                turn_back(2 * third, 0, number)
+
+        in_turn(
+            bodies,
+            [begin, middle, finish],
+            {
+                half_way // 2 + 2: lambda: events("bwd", 1, third),
+                half_way + 2: lambda: events("bwd", 2, third),
+                half_way + half_way // 2 + 2: lambda: events("bwd", 3, third),
+            },
+        )
+        events("bwd", 4, third)
         for i in range(blocks):
-            cosine, sine = s.cost[:, rows_of(i)], -s.sint[:, rows_of(i)]
-            pieces = []
-            for kind in range(2):
-                for h in range(2):
-                    piece = s.total[sums_at(kind, h * HEAD, HEAD, i)]
-                    piece = rotate_rows(piece, cosine, sine)
-                    pieces.append((piece * 0.125 if kind == 0 else piece).astype(bf16))
-            s.k[p, rows_of(i), :] = jnp.concatenate(pieces[:2], axis=0).T
-            s.v[p, rows_of(i), :] = jnp.concatenate(pieces[2:], axis=0).T
-            s.n2[p, rows_of(i), :] = s.total[sums_at(2, 0, LANES, i)].astype(bf16).T
-        d_qkv = jnp.concatenate([s.k[p], s.v[p], s.n2[p]], axis=1)
-        store_g(
-            mlp_chunks + 1 + p // 2, p % 2, pl.ds(0, half_width), nn(s.n1t[...], d_qkv)
-        )
-        events("bwd", 2, p)
+            turn_back(2 * third + 1, 1, i)
+        for q in range(2):
+            p = 2 * third + q
+            d_qkv = jnp.concatenate([s.k[p], s.v[p], s.n2[p]], axis=1)
+            store_g(
+                mlp_chunks + 1 + third, q, pl.ds(0, half_width), nn(s.n1t[...], d_qkv)
+            )
+        events("bwd", 5, third)
         return carry
 
-    lax.fori_loop(0, pairs, attention_backward, 0)
+    lax.fori_loop(0, thirds, attention_backward, 0)
 
     x_copy.wait()
     w_qkv_t = jnp.concatenate([load_w(p // 2, p % 2).T for p in range(pairs)], axis=0)
@@ -543,10 +620,13 @@
     )
     if linked:
         gain_steps[0](gain_grads)
+        left = list(gain_steps[1:4])
         for kind, table in PLAN["end", 0]:
             actions[kind](table[0])
-            if table[0] == chunks - 1 and kind in "LEX":
-                gain_steps["LEX".index(kind) + 1]()
+            if kind in "QLE" and left:
+                left.pop(0)()
+        for step in left:
+            step()
         gain_steps[4]()
     else:
         events("end", 0)
@@ -563,8 +643,10 @@
     over_x, over_y, over_both = m + 1 - 2 * (m % 2), (m + 2) % 4, 3 - m
     m1 = (1 - core) * over_x + core * over_y
     m2 = (1 - core) * over_y + core * over_x
-    m3 = over_both
     other = 1 - core
+    low = (1 - core) * (m % 2) + core * (m // 2)
+    high = (1 - core) * (m // 2) + core * (m % 2)
+    place = 2 * high + low
 
     def chip(plane, place):
         return (plane * 4 + place, core)
@@ -575,116 +657,150 @@
         return (z + k) % planes
 
     peers = [chip(far(k), m) for k in range(1, planes)]
-
-    def remote(src, dst, sems, index, device):
+    first, second = chip(z, m1), chip(z, m2)
+
+    def remote(src, dst, send_sem, recv_sem, device):
         return pltpu.make_async_remote_copy(
             src_ref=src,
             dst_ref=dst,
-            send_sem=sems.at[(0,) + index],
-            recv_sem=sems.at[(1,) + index],
+            send_sem=send_sem,
+            recv_sem=recv_sem,
             device_id=device,
             device_id_type=pl.DeviceIdType.MESH,
         )
 
     def along_z(chunk, k):
-        block = s.w.at[chunk, core, z, m]
-        return remote(block, block, s.z_sem, (chunk, k), peers[k])
-
-    def line(chunk, place, index, device):
-        block = s.w.at[chunk, core, :, place]
-        return remote(block, block, s.line_sem, (chunk, index), device)
-
-    hops = [
-        (m, chip(z, m1)),
-        (m, chip(z, m2)),
-        (m1, chip(z, m2)),
-        (m, sibling),
-        (m1, sibling),
-        (m2, sibling),
-        (m3, sibling),
-    ]
+        block = s.w.at[chunk, core, z, place]
+        return remote(block, block, s.sent_sem.at[0], s.hop_sem.at[chunk, 0], peers[k])
+
+    def along_z_here(chunk):
+        blocks = s.w.at[chunk, core, pl.ds(0, planes - 1), place]
+        return remote(blocks, blocks, s.sent_sem.at[0], s.hop_sem.at[chunk, 0], peers[0])
 
     def hop(chunk, index):
-        return line(chunk, hops[index][0], index, hops[index][1])
+        if index == 1:
+            blocks, device = s.w.at[chunk, core, :, place], first
+        elif index == 2:
+            blocks, device = s.w.at[chunk, core, :, pl.ds(2 * high, 2)], second
+        else:
+            blocks, device = s.w.at[chunk, core], sibling
+        return remote(blocks, blocks, s.sent_sem.at[index], s.hop_sem.at[chunk, index], device)
+
+    def alone(chunk):
+        block = s.w.at[chunk, core, z, place]
+        return remote(block, block, s.sent_sem.at[5], s.hop_sem.at[chunk, 1], first)
+
+    def along_z_again(chunk, k):
+        block = s.w.at[chunk, core, z, place + 1 - 2 * low]
+        return remote(block, block, s.sent_sem.at[4], s.hop_sem.at[chunk, 4], peers[k])
+
+    def along_z_again_here(chunk):
+        blocks = s.w.at[chunk, core, pl.ds(0, planes - 1), place]
+        return remote(blocks, blocks, s.sent_sem.at[4], s.hop_sem.at[chunk, 4], peers[0])
+
+    def gather_end():
+        late = pl.ds(LATE, chunks - LATE)
+        blocks = s.w.at[late, core, pl.ds(0, planes - 1), place]
+        remote(blocks, blocks, s.sent_sem.at[4], s.hop_sem.at[0, 4], peers[0]).wait_send()
+        blocks = s.w.at[late, core, z, place]
+        remote(blocks, blocks, s.sent_sem.at[5], s.hop_sem.at[0, 1], first).wait_send()
+        blocks = s.w.at[:, core, pl.ds(0, planes - 1), place]
+        remote(blocks, blocks, s.sent_sem.at[0], s.hop_sem.at[0, 0], peers[0]).wait_send()
+        blocks = s.w.at[pl.ds(0, LATE), core, :, place]
+        remote(blocks, blocks, s.sent_sem.at[1], s.hop_sem.at[0, 1], first).wait_send()
+        blocks = s.w.at[:, core, :, pl.ds(2 * high, 2)]
+        remote(blocks, blocks, s.sent_sem.at[2], s.hop_sem.at[0, 2], second).wait_send()
+        blocks = s.w.at[:, core]
+        remote(blocks, blocks, s.sent_sem.at[3], s.hop_sem.at[0, 3], sibling).wait_send()
 
     def gain_along_z(k):
         block = s.gt.at[z, m]
-        return remote(block, block, s.gain_sem, (k,), peers[k])
-
-    def gain_line(place, index, device):
-        block = s.gt.at[:, place]
-        return remote(block, block, s.gain_sem, (planes - 1 + index,), device)
+        return remote(block, block, s.gain_sem.at[0, k], s.gain_sem.at[1, k], peers[k])
 
     def gain_hop(index):
-        return gain_line(hops[index][0], index, hops[index][1])
+        blocks = s.gt.at[:, [m, m, m1][index]]
+        device = [first, second, second][index]
+        k = planes - 1 + index
+        return remote(blocks, blocks, s.gain_sem.at[0, k], s.gain_sem.at[1, k], device)
 
     width = s.x.shape[1]
     pairs = width // LANES
     shard_rows = s.w.shape[4]
     half_width = s.w.shape[5]
     hidden = s.mlp_in.shape[1] // 3
+    loads = [
+        functools.partial(
+            pltpu.make_async_copy,
+            s.attn_in.at[:, pl.ds(k * width, width)],
+            s.dn.at[pl.ds(k * shard_rows, shard_rows)],
+            s.load_sem.at[k],
+        )
+        for k in range(4)
+    ] + [
+        functools.partial(
+            pltpu.make_async_copy,
+            s.mlp_in.at[:, pl.ds(k * width, width)],
+            s.dn.at[pl.ds((4 + k) * shard_rows, shard_rows)],
+            s.load_sem.at[4 + k],
+        )
+        for k in range(3 * hidden // width)
+    ]
+
+    def piece(row, lane):
+        rows = s.dn[pl.ds(row * shard_rows, shard_rows), pl.ds(lane, LANES)]
+        return rows.astype(bf16)
+
+    def round_third(third):
+        lane = pl.multiple_of((2 * third + core) * LANES, LANES)
+        for kind in range(3):
+            s.w[third, core, z, place, :, kind * LANES : (kind + 1) * LANES] = piece(kind, lane)
 
     def gather_start():
-        loads = [
-            pltpu.make_async_copy(
-                s.attn_in.at[:, pl.ds(k * width, width)],
-                s.dn.at[pl.ds(k * shard_rows, shard_rows)],
-                s.load_sem.at[k],
-            )
-            for k in range(4)
-        ] + [
-            pltpu.make_async_copy(
-                s.mlp_in.at[:, pl.ds(k * width, width)],
-                s.dn.at[pl.ds((4 + k) * shard_rows, shard_rows)],
-                s.load_sem.at[4 + k],
-            )
-            for k in range(3 * hidden // width)
-        ]
-        for load in loads:
-            load.start()
         barrier = pltpu.get_barrier_semaphore()
         partners = [chip(z, over_x), chip(z, over_y), chip(z, over_both), sibling] + peers
         for partner in partners:
             pl.semaphore_signal(
                 barrier, inc=1, device_id=partner, device_id_type=pl.DeviceIdType.MESH
             )
+        for load in loads:
+            load().start()
         own = s.gains_in[...].astype(bf16)
         own = jnp.concatenate([own, jnp.zeros((2, LANES - shard_rows), bf16)], axis=1)
         s.gt[z, m] = jnp.concatenate([own, jnp.zeros((14, LANES), bf16)], axis=0)
-        for load in loads:
-            load.wait()
-        for third in range(thirds):
-            lane = pl.multiple_of((2 * third + core) * LANES, LANES)
-            for kind in range(3):
-                s.w[third, core, z, m, :, kind * LANES : (kind + 1) * LANES] = piece(kind, lane)
-        lane = pl.multiple_of(core * half_width, LANES)
-        s.w[thirds, core, z, m] = s.dn[
-            pl.ds(3 * shard_rows, shard_rows), pl.ds(lane, half_width)
-        ].astype(bf16)
+        for load in loads[:3]:
+            load().wait()
+        round_third(0)
         pl.semaphore_wait(barrier, len(partners))
         for k in range(planes - 1):
             along_z(0, k).start()
         for k in range(planes - 1):
             gain_along_z(k).start()
+        loads[3]().wait()
+        for third in range(1, thirds):
+            round_third(third)
+        lane = pl.multiple_of(core * half_width, LANES)
+        s.w[thirds, core, z, place] = s.dn[
+            pl.ds(3 * shard_rows, shard_rows), pl.ds(lane, half_width)
+        ].astype(bf16)
         for chunk in range(1, thirds + 1):
             for k in range(planes - 1):
                 along_z(chunk, k).start()
 
-    def piece(row, lane):
-        rows = s.dn[pl.ds(row * shard_rows, shard_rows), pl.ds(lane, LANES)]
-        return rows.astype(bf16)
-
     def gather_feed_forward():
+        for load in loads[4:]:
+            load().wait()
         for j in range(mlp_chunks):
             for kind in range(3):
-                place = kind * hidden + 2 * j * LANES
-                row, first = 4 + place // width, place % width
-                lane = pl.multiple_of(first + core * LANES, LANES)
-                s.w[thirds + 1 + j, core, z, m, :, kind * LANES : (kind + 1) * LANES] = piece(
-                    row, lane
+                column = kind * hidden + 2 * j * LANES
+                row, begin = 4 + column // width, column % width
+                lane = pl.multiple_of(begin + core * LANES, LANES)
+                s.w[thirds + 1 + j, core, z, place, :, kind * LANES : (kind + 1) * LANES] = (
+                    piece(row, lane)
                 )
             for k in range(planes - 1):
                 along_z(thirds + 1 + j, k).start()
+            if thirds + 1 + j >= LATE:
+                alone(thirds + 1 + j).start()
 
     def gather_one():
         first_hop(0)
@@ -700,7 +816,6 @@
         gain_hop(2).start()
 
     def gather_three():
-        third_hop(0)
         gain_hop(1).wait()
         gain_hop(2).wait()
         rows = jnp.zeros((8, width), f32)
@@ -709,56 +824,78 @@
             wide = jnp.concatenate([tile, jnp.zeros((8, width - LANES), f32)], axis=1)
             rows += pltpu.roll(wide, d * shard_rows, 1) if d else wide
         s.gain[...] = rows
+        third_hop(0)
+
+    def first_hop(chunk):
+        along_z_here(chunk).wait_recv()
+        hop(chunk, 1).start()
+
+    def first_hop_late(chunk):
+        alone(chunk).wait_recv()
+        for k in range(planes - 1):
+            along_z_again(chunk, k).start()
+
+    def second_hop_late(chunk):
+        along_z_here(chunk).wait_recv()
+        along_z_again_here(chunk).wait_recv()
+        hop(chunk, 2).start()
+
+    def second_hop(chunk):
+        hop(chunk, 1).wait_recv()
+        hop(chunk, 2).start()
+
+    def third_hop(chunk):
+        hop(chunk, 2).wait_recv()
+        hop(chunk, 3).start()
 
     def ready(chunk):
-        for index in range(3, 7):
-            hop(chunk, index).wait_recv()
-        for k in range(planes - 1):
-            along_z(chunk, k).wait_send()
-        for index in range(7):
-            hop(chunk, index).wait_send()
-
-    def third_hop(chunk):
-        hop(chunk, 1).wait_recv()
-        hop(chunk, 5).start()
-        hop(chunk, 2).wait_recv()
-        hop(chunk, 6).start()
-
-    def second_hop(chunk):
-        hop(chunk, 0).wait_recv()
-        hop(chunk, 2).start()
-        hop(chunk, 4).start()
-
-    def first_hop(chunk):
-        for k in range(planes - 1):
-            along_z(chunk, k).wait_recv()
-        for index in (0, 1, 3):
-            hop(chunk, index).start()
+        hop(chunk, 3).wait_recv()
+
+    held = s.h.shape[0]
 
     def to_sibling(chunk):
         return remote(
-            s.g.at[chunk % 2, other], s.a.at[chunk % 2], s.rs_sem, (chunk, 0), sibling
+            s.g.at[chunk % 2, other],
+            s.a.at[chunk % 2],
+            s.rs_sem.at[chunk, 0, 0],
+            s.rs_sem.at[chunk, 0, 1],
+            sibling,
         )
 
     def to_second(chunk):
         return remote(
-            s.h.at[chunk % held, :, pl.ds(2, 2)],
+            s.h.at[chunk % held, :, pl.ds(2 - 2 * high, 2)],
             s.b.at[chunk % 4],
-            s.rs_sem,
-            (chunk, 1),
-            chip(z, m2),
+            s.rs_sem.at[chunk, 1, 0],
+            s.rs_sem.at[chunk, 1, 1],
+            second,
         )
 
     def to_first(chunk):
-        return remote(s.cs.at[chunk % 2], s.c.at[chunk % 4], s.rs_sem, (chunk, 2), chip(z, m1))
+        return remote(
+            s.cs.at[chunk % 2],
+            s.c.at[chunk % 4],
+            s.rs_sem.at[chunk, 2, 0],
+            s.rs_sem.at[chunk, 2, 1],
+            first,
+        )
 
     def to_plane(chunk, k):
         return remote(
             s.ds.at[chunk % 2, far(k + 1)],
             s.d.at[chunk % 4, k],
-            s.rs_sem,
-            (chunk, 3 + k),
+            s.rs_sem.at[chunk, 3, 0],
+            s.rs_sem.at[chunk, 3, 1],
             peers[k],
+        )
+
+    def to_planes(chunk):
+        return remote(
+            s.ds.at[chunk % 2, pl.ds(0, planes - 1)],
+            s.d.at[chunk % 4],
+            s.rs_sem.at[chunk, 3, 0],
+            s.rs_sem.at[chunk, 3, 1],
+            peers[0],
         )
 
     def place_of(chunk):
@@ -768,29 +905,33 @@
             jnp.where(chunk == mlp_chunks, thirds, chunk - mlp_chunks - 1),
         )
 
-    def half_block(chunk):
-        return s.gout.at[chunk % 6, core]
-
     def to_copy(chunk):
-        block = half_block(chunk)
-        return remote(block, block, s.rs_sem, (chunk, 2 + planes), sibling)
+        done = s.g_out.at[place_of(chunk), core]
+        sems = s.end_sem.at[chunk, 0], s.end_sem.at[0, 2]
+        return remote(s.gout.at[chunk % 6], done, *sems, sibling)
 
     def leave(chunk):
-        place = place_of(chunk)
-        return pltpu.make_async_copy(s.gout.at[chunk % 6], s.g_out.at[place], s.leave_sem.at[chunk])
-
-    held = s.h.shape[0]
+        done = s.g_out.at[place_of(chunk), core]
+        return pltpu.make_async_copy(s.gout.at[chunk % 6], done, s.end_sem.at[chunk, 1])
+
+    def left(chunk):
+        to_copy(chunk).wait_send()
+        leave(chunk).wait()
+
+    def reduce_end():
+        done = s.g_out.at[:, core]
+        remote(done, done, s.end_sem.at[0, 0], s.end_sem.at[0, 2], sibling).wait_recv()
+        for chunk in range(chunks - 6, chunks):
+            left(chunk)
 
     def send_half(chunk):
         to_sibling(chunk).start()
 
     def add_half(chunk):
         to_sibling(chunk).wait()
-        for index, place in enumerate([m, m1, m2, m3]):
-            s.h[chunk % held, :, index] = (
-                s.g[chunk % 2, core, :, place].astype(f32)
-                + s.a[chunk % 2, :, place].astype(f32)
-            ).astype(bf16)
+        s.h[chunk % held] = (
+            s.g[chunk % 2, core].astype(f32) + s.a[chunk % 2].astype(f32)
+        ).astype(bf16)
 
     def halves(chunk):
         to_second(chunk).start()
@@ -799,56 +940,58 @@
         to_second(chunk).wait()
         even = chunk % 2
         s.cs[even] = (
-            s.h[chunk % held, :, 1].astype(f32) + s.b[chunk % 4, :, 1].astype(f32)
+            s.h[chunk % held, :, 2 * high + 1 - low].astype(f32)
+            + s.b[chunk % 4, :, 1 - low].astype(f32)
         ).astype(bf16)
         to_first(chunk).start()
-        s.kept[even] = s.h[chunk % held, :, 0].astype(f32) + s.b[chunk % 4, :, 0].astype(f32)
+        s.kept[even] = (
+            s.h[chunk % held, :, place].astype(f32) + s.b[chunk % 4, :, low].astype(f32)
+        ).astype(bf16)
 
     def lines(chunk):
         to_first(chunk).wait()
         even = chunk % 2
-        s.kept[even] = s.kept[even] + s.c[chunk % 4].astype(f32)
-        s.ds[even] = s.kept[even].astype(bf16)
-        s.own[even] = s.kept[even, z]
+        s.ds[even] = (s.kept[even].astype(f32) + s.c[chunk % 4].astype(f32)).astype(bf16)
         for k in range(planes - 1):
             to_plane(chunk, k).start()
+        s.own[even] = s.kept[even, z].astype(f32) + s.c[chunk % 4, z].astype(f32)
 
     def last(chunk):
+        to_planes(chunk).wait()
         total = s.own[chunk % 2]
         for k in range(planes - 1):
-            to_plane(chunk, k).wait()
             total += s.d[chunk % 4, k].astype(f32)
-        half_block(chunk)[...] = total
+        if isinstance(chunk, int):
+            if chunk >= 6:
+                left(chunk - 6)
+        else:
+            pl.when(chunk >= 6)(lambda: left(chunk - 6))
+        s.gout[chunk % 6] = total
         to_copy(chunk).start()
-
-    def end(chunk):
-        to_copy(chunk).wait()
         leave(chunk).start()
-        if isinstance(chunk, int):
-            if chunk >= 2:
-                leave(chunk - 2).wait()
-        else:
-            pl.when(chunk >= 2)(lambda: leave(chunk - 2).wait())
 
     actions = {"F": first_hop, "S": second_hop, "T": third_hop, "R": ready}
     actions.update({"A": send_half, "H": add_half, "B": halves, "Q": quarters})
-    actions.update({"L": lines, "E": last, "X": end})
+    actions.update({"L": lines, "E": last, "f": first_hop_late, "s": second_hop_late})
 
     def plane_sum():
         block = s.gp.at[m]
         return [
-            remote(block, block, s.gsum_sem, (k,), chip(z, place))
-            for k, place in enumerate([over_x, over_y, over_both])
+            remote(block, block, s.gsum_sem.at[0, k], s.gsum_sem.at[1, k], chip(z, at))
+            for k, at in enumerate([over_x, over_y, over_both])
         ]
 
     def line_sum():
         block = s.gz.at[z]
         return [
-            remote(block, block, s.gsum_sem, (3 + k,), peers[k]) for k in range(planes - 1)
+            remote(block, block, s.gsum_sem.at[0, 3 + k], s.gsum_sem.at[1, 3 + k], peers[k])
+            for k in range(planes - 1)
         ]
 
     def core_sum():
-        return remote(s.gc.at[0], s.gc.at[1], s.gsum_sem, (2 + planes,), sibling)
+        k = planes + 2
+        sems = s.gsum_sem
+        return remote(s.gc.at[0], s.gc.at[1], sems.at[0, k], sems.at[1, k], sibling)
 
     def gain_begin(value):
         s.gp[m] = value
@@ -877,8 +1020,8 @@
         s.gain_out[...] = pltpu.roll(total, (width - me * shard_rows) % width, 1)[:, :LANES]
 
     def gain_out():
-        for chunk in range(chunks - 2, chunks):
-            leave(chunk).wait()
+        gather_end()
+        reduce_end()
 
     start = (gather_start, gather_one, gather_two, gather_three)
     return start, actions, (gain_begin, gain_lines_sum, gain_cores, gain_end, gain_out)
@@ -1093,22 +1236,22 @@
             ("b", pltpu.VMEM((4,) + pair_lines, bf16)),
             ("cs", pltpu.VMEM((2,) + lines, bf16)),
             ("c", pltpu.VMEM((4,) + lines, bf16)),
-            ("kept", pltpu.VMEM((2,) + lines, f32)),
+            ("kept", pltpu.VMEM((2,) + lines, bf16)),
             ("ds", pltpu.VMEM((2,) + lines, bf16)),
             ("d", pltpu.VMEM((4, planes - 1) + lines[1:], bf16)),
             ("own", pltpu.VMEM((2,) + lines[1:], f32)),
-            ("gout", pltpu.VMEM((6, 2) + lines[1:], f32)),
+            ("gout", pltpu.VMEM((6,) + lines[1:], f32)),
             ("gt", pltpu.VMEM((planes, 4, 16, LANES), bf16)),
             ("gain", pltpu.VMEM(gain_rows, f32)),
             ("gp", pltpu.VMEM((4,) + gain_rows, f32)),
             ("gz", pltpu.VMEM((planes,) + gain_rows, f32)),
             ("gc", pltpu.VMEM((2,) + gain_rows, f32)),
             ("load_sem", pltpu.SemaphoreType.DMA((4 + 3 * hidden // width,))),
-            ("z_sem", pltpu.SemaphoreType.DMA((2, chunks, planes - 1))),
-            ("line_sem", pltpu.SemaphoreType.DMA((2, chunks, 7))),
+            ("hop_sem", pltpu.SemaphoreType.DMA((chunks, 5))),
+            ("sent_sem", pltpu.SemaphoreType.DMA((6,))),
             ("gain_sem", pltpu.SemaphoreType.DMA((2, planes + 2))),
-            ("rs_sem", pltpu.SemaphoreType.DMA((2, chunks, planes + 3))),
-            ("leave_sem", pltpu.SemaphoreType.DMA((chunks,))),
+            ("rs_sem", pltpu.SemaphoreType.DMA((chunks, 4, 2))),
+            ("end_sem", pltpu.SemaphoreType.DMA((chunks, 3))),
             ("gsum_sem", pltpu.SemaphoreType.DMA((2, planes + 3))),
         ]
         params = pltpu.CompilerParams(

time: 169 us -> 163 us (0.964)
  Pallas kernels: 168 us -> 162 us
    pallas_call x1, Pallas kernels: 159 us -> 153 us  [local(): pl.pallas_call(functools.partial(block_kernel, linked, names), out_shape=...]
where the time goes in v4:
time: 163 us
  Pallas kernels  162 us (99%)
    pallas_call x1, Pallas kernels, local(): pl.pallas_call(functools.partial(block_kernel, linked, names), out_shape=...  153 us
    pallas_call x1, Pallas kernels, local(): pl.pallas_call(functools.partial(update_kernel, rate, names), out_shape=[...  8.53 us

profile of v4, /device:TPU:0, one launch (start us, length us, event | category | flops | bytes accessed | tf_op | source)
XLA Modules:
  0.0 162.6 jit_solution(17456062213154525558)
XLA Ops:
  0.7 153.2 %block.1 = (bf16[1024,768]{1,0:T(8,128)(2,1)}, bf16[1024,768]{1,0:T(8,128)(2,1)}, f32[12,2,48,384]{3,2,1,0:T(8,128)}, f32[8,128]{1,0:T(8,128)}) custom-call(s32[1024]{0:T(1024)} %refs_0_.1, bf16[1024,768]{1,0:T(8,128)(2,1)} %refs_1_.1, bf16[1024,768]{1,0:T(8,128)(2,1)} %refs_2_.1, f32[256,256]{1,0:T(8,128)} %constant.2.clone.refs_3_, f32[48,3072]{1,0:T(8,128)} %refs_4_.3, ...), custom_call_target="tpu_custom_call" | custom-call | tf_op jit(solution)/shard_map/block/pallas_call | solution.py:1275
  153.9 8.5 %update.1 = (bf16[1024,768]{1,0:T(8,128)(2,1)}, bf16[1024,768]{1,0:T(8,128)(2,1)}, f32[48,3072]{1,0:T(8,128)}, f32[48,6144]{1,0:T(8,128)}, f32[2,48]{1,0:T(2,128...) custom-call(bf16[1024,768]{1,0:T(8,128)(2,1)} %get-tuple-element.21., ...), custom_call_target="tpu_custom_call" | custom-call | tf_op jit(solution)/shard_map/update/pallas_call | solution.py:1328

commit v5 on v4

--- a/solution.py
+++ b/solution.py
@@ -21,63 +21,68 @@
 LANES = 128
 BLOCK = 256
 PLAN = {
+    ("pre", 1): [
+        ("F", (1,)),
+    ],
     ("pre", 0): [
-        ("F", (1,)),
         ("F", (2,)),
+        ("S", (1,)),
+        ("F", (3,)),
     ],
     ("fwd", 0): [
-        ("S", (1, -1, 4)),
-        ("F", (3, 5, 7)),
-        ("T", (-1, 1, -1)),
-        ("S", (-1, 3, -1)),
-        ("R", (0, 1, 2)),
+        ("S", (2, 3, 5)),
+        ("R", (0, 1, -1)),
+        ("F", (4, -1, 7)),
+        ("f", (-1, -1, 8)),
+        ("f", (-1, -1, 9)),
+        ("f", (-1, -1, 10)),
+        ("R", (-1, -1, 2)),
+    ],
+    ("fwd", 1): [
         ("F", (-1, 6, -1)),
     ],
-    ("fwd", 1): [
-        ("S", (2, -1, 5)),
-        ("F", (4, -1, -1)),
-        ("f", (-1, -1, 8)),
-    ],
     ("fwd", 2): [
-        ("T", (-1, 2, 3)),
+        ("T", (1, 2, 3)),
+        ("F", (5, -1, -1)),
+        ("S", (-1, 4, -1)),
     ],
     ("wo", 0): [
         ("S", (6,)),
-        ("f", (9,)),
+        ("f", (11,)),
         ("R", (3,)),
     ],
     ("wo", 1): [
     ],
     ("mlp", 0): [
-        ("T", (4, -1, -1, 8, -1, -1, 11, -1)),
-        ("S", (7, -1, -1, -1, -1, -1, -1, -1)),
-        ("s", (-1, 8, -1, 11, -1, -1, -1, -1)),
-        ("f", (10, 11, -1, -1, -1, -1, -1, -1)),
-        ("R", (4, 5, 6, -1, -1, -1, 10, -1)),
-        ("T", (-1, -1, 7, -1, -1, -1, -1, -1)),
-        ("H", (-1, -1, -1, 1, 2, -1, -1, -1)),
-        ("R", (-1, -1, -1, -1, 9, -1, -1, -1)),
-        ("Q", (-1, -1, -1, -1, -1, 0, -1, -1)),
+        ("s", (-1, -1, 9, -1, -1, -1, -1, -1)),
+        ("T", (4, -1, 7, 8, -1, -1, -1, -1)),
+        ("R", (4, 5, 6, -1, -1, -1, -1, -1)),
+        ("s", (-1, 8, -1, -1, -1, -1, -1, -1)),
+        ("Q", (-1, -1, -1, -1, -1, -1, 0, -1)),
+        ("H", (-1, -1, -1, 1, 2, -1, 4, -1)),
         ("L", (-1, -1, -1, -1, -1, -1, -1, 0)),
         ("A", (-1, 0, 1, 2, 3, 4, 5, 6)),
-        ("B", (-1, -1, -1, 1, -1, 2, -1, -1)),
+        ("B", (-1, -1, -1, -1, -1, -1, 2, -1)),
+        ("R", (-1, -1, -1, -1, -1, 10, 11, -1)),
     ],
     ("mlp", 1): [
-        ("T", (5, 6, -1, 9, -1, 10, -1, -1)),
-        ("s", (-1, 9, 10, -1, -1, -1, -1, -1)),
-        ("R", (-1, -1, 7, 8, -1, -1, 11, -1)),
+        ("T", (5, 6, -1, 9, 10, 11, -1, -1)),
+        ("S", (7, -1, -1, -1, -1, -1, -1, -1)),
         ("Q", (-1, -1, -1, -1, -1, -1, 1, -1)),
-        ("H", (-1, 0, -1, -1, 3, 4, 5, -1)),
-        ("B", (-1, 0, -1, -1, -1, -1, 3, -1)),
+        ("H", (-1, 0, -1, -1, 3, -1, 5, -1)),
+        ("s", (-1, -1, 10, 11, -1, -1, -1, -1)),
+        ("B", (-1, -1, -1, 0, -1, -1, 3, -1)),
+        ("B", (-1, -1, -1, 1, -1, -1, -1, -1)),
+        ("R", (-1, -1, 7, 8, 9, -1, -1, -1)),
     ],
     ("d", 0): [
         ("Q", (2,)),
         ("H", (6,)),
-        ("L", (1,)),
         ("A", (7,)),
         ("B", (4,)),
     ],
     ("o", 0): [
+        ("L", (1,)),
     ],
     ("o", 1): [
         ("Q", (3,)),
@@ -95,15 +100,13 @@
         ("H", (-1, 9, 10)),
     ],
     ("bwd", 2): [
-        ("E", (1, -1, -1)),
-        ("Q", (4, -1, 8)),
+        ("Q", (4, 6, 8)),
         ("H", (8, -1, -1)),
         ("B", (6, -1, 10)),
     ],
     ("bwd", 3): [
-        ("E", (-1, 3, 5)),
+        ("E", (1, 3, 5)),
         ("L", (3, 5, 7)),
-        ("Q", (-1, 6, -1)),
         ("B", (-1, 8, -1)),
     ],
     ("bwd", 4): [
@@ -287,9 +290,13 @@
     ]
     tables = s.total.at[pl.ds(0, HEAD * blocks), pl.ds(0, BLOCK)]
     copies.append(pltpu.make_async_copy(s.tables, tables, s.local_sem.at[2]))
+    copies.append(pltpu.make_async_copy(s.doc_in, s.doc, s.local_sem.at[3]))
+    if linked:
+        gather_start[0]()
     for copy in copies:
         copy.start()
 
+    copies.pop().wait()
     docs = [s.doc[BLOCK * j] for j in range(blocks)]
     bias = [
         [jnp.where(docs[i] == docs[j], 0.0, MASKED).astype(f32) for j in range(i)] + [0.0]
@@ -299,8 +306,6 @@
         jnp.int32, (BLOCK, BLOCK), 1
     )
 
-    if linked:
-        gather_start[0]()
     copies.pop().wait()
     for i in range(blocks):
         place = sum([(docs[j] == docs[i]).astype(jnp.int32) for j in range(i)], jnp.int32(0))
@@ -313,6 +318,7 @@
             table[:, rows_of(i)] = chosen
     if linked:
         gather_start[1]()
+        events("pre", 1)
     for copy in copies:
         copy.wait()
     if linked:
@@ -341,8 +347,7 @@
         parts[i] = jnp.where(causal, parts[i], MASKED)
         return parts
 
-    mixed_order = [i for j in range(blocks // 2) for i in (blocks - 1 - j, j)]
-    bodies = [(q, i, h) for q in range(2) for h in range(2) for i in mixed_order]
+    bodies = [(q, i, h) for q in range(2) for i in range(blocks) for h in range(2)]
     half_way = 2 * blocks
 
     def lse_at(p, i, h):
@@ -623,7 +628,7 @@
         left = list(gain_steps[1:4])
         for kind, table in PLAN["end", 0]:
             actions[kind](table[0])
-            if kind in "QLE" and left:
+            if table[0] == chunks - 1 and kind in "QLE" and left:
                 left.pop(0)()
         for step in left:
             step()
@@ -764,6 +769,9 @@
             )
         for load in loads:
             load().start()
+        gains_copy = pltpu.make_async_copy(s.gains_hbm, s.gains_in, s.gains_sem.at[0])
+        gains_copy.start()
+        gains_copy.wait()
         own = s.gains_in[...].astype(bf16)
         own = jnp.concatenate([own, jnp.zeros((2, LANES - shard_rows), bf16)], axis=1)
         s.gt[z, m] = jnp.concatenate([own, jnp.zeros((14, LANES), bf16)], axis=0)
@@ -1017,11 +1025,13 @@
     def gain_end():
         core_sum().wait()
         total = s.gc[0] + s.gc[1]
-        s.gain_out[...] = pltpu.roll(total, (width - me * shard_rows) % width, 1)[:, :LANES]
+        s.gains_end[...] = pltpu.roll(total, (width - me * shard_rows) % width, 1)[:, :LANES]
+        pltpu.make_async_copy(s.gains_end, s.gain_out, s.gains_sem.at[1]).start()
 
     def gain_out():
         gather_end()
         reduce_end()
+        pltpu.make_async_copy(s.gains_end, s.gain_out, s.gains_sem.at[1]).wait()
 
     start = (gather_start, gather_one, gather_two, gather_three)
     return start, actions, (gain_begin, gain_lines_sum, gain_cores, gain_end, gain_out)
@@ -1102,19 +1112,44 @@
             s.pass_sem.at[3],
         ),
     ]
+    enter[0].start()
     grads[0].start()
     for load in loads(0):
         load.start()
+    enter[1].start()
     grads[1].start()
     for index in range(1, len(pieces)):
         for load in loads(index):
             load.start()
-    for copy in enter:
+    small_in = [
+        pltpu.make_async_copy(
+            getattr(s, f"gains_{what}"), getattr(s, f"gains_{what}_here"), s.in_sem.at[4, k]
+        )
+        for k, what in enumerate(["w", "m", "e"])
+    ] + [pltpu.make_async_copy(s.gain_part_in, s.gain_part, s.in_sem.at[4, 3])]
+    small_out = [
+        pltpu.make_async_copy(
+            getattr(s, f"gains_{what}_here"), getattr(s, f"gains_{what}"), s.out_sem.at[4, k]
+        )
+        for k, what in enumerate(whats)
+    ]
+    for copy in small_in:
         copy.start()
+    enter[0].wait()
+    leave[0].start()
+    for copy in small_in:
+        copy.wait()
     shard_rows = s.attn_w.shape[0]
-    results = rule(s.gains_w[...], s.gain_part[:2, :shard_rows], s.gains_m[...], s.gains_e[...])
+    results = rule(
+        s.gains_w_here[...],
+        s.gain_part[:2, :shard_rows],
+        s.gains_m_here[...],
+        s.gains_e_here[...],
+    )
     for what, result in zip(whats, results, strict=True):
-        getattr(s, f"gains_{what}")[...] = result
+        getattr(s, f"gains_{what}_here")[...] = result
+    for copy in small_out:
+        copy.start()
     for index, (kind, _, _, blocks) in enumerate(pieces):
         if index < 2:
             grads[index].wait()
@@ -1132,13 +1167,13 @@
                 getattr(s, f"{kind}_{what}_here")[:, span] = result
         for store in stores(index):
             store.start()
-    for copy_in, copy_out in zip(enter, leave, strict=True):
-        copy_in.wait()
-        copy_out.start()
+        if index == 0:
+            enter[1].wait()
+            leave[1].start()
     for index in range(len(pieces)):
         for store in stores(index):
             store.wait()
-    for copy in leave:
+    for copy in leave + small_out:
         copy.wait()
 
 
@@ -1181,10 +1216,9 @@
 
     vmem = pl.BlockSpec(memory_space=pltpu.VMEM)
     hbm = pl.BlockSpec(memory_space=pl.ANY)
-    smem = pl.BlockSpec(memory_space=pltpu.SMEM)
     linked = shard_rows % 16 == 0 and group % 4 == 0
     planes = group // 4
-    inputs = [("doc", smem, doc_ids), ("x_in", hbm, tokens), ("cot_in", hbm, cotangent)]
+    inputs = [("doc_in", hbm, doc_ids), ("x_in", hbm, tokens), ("cot_in", hbm, cotangent)]
     inputs += [("tables", hbm, rotary_tables(row_count))]
     token_rows = (row_count, width)
     outputs = [
@@ -1212,7 +1246,8 @@
         ("lse", pltpu.VMEM((pairs // 2, 8, row_count), f32)),
         ("cost", pltpu.VMEM((HEAD // 2, row_count), f32)),
         ("sint", pltpu.VMEM((HEAD // 2, row_count), f32)),
-        ("local_sem", pltpu.SemaphoreType.DMA((3,))),
+        ("local_sem", pltpu.SemaphoreType.DMA((4,))),
+        ("doc", pltpu.SMEM(doc_ids.shape, jnp.int32)),
     ]
     if linked:
         lines = (planes, shard_rows, half_width)
@@ -1222,11 +1257,11 @@
         inputs += [
             ("attn_in", hbm, attn_weights),
             ("mlp_in", hbm, mlp_weights),
-            ("gains_in", vmem, gains),
+            ("gains_hbm", hbm, gains),
         ]
         outputs += [
             ("g_out", hbm, jax.ShapeDtypeStruct((chunks, 2, shard_rows, half_width), f32)),
-            ("gain_out", vmem, jax.ShapeDtypeStruct((8, LANES), f32)),
+            ("gain_out", hbm, jax.ShapeDtypeStruct((8, LANES), f32)),
         ]
         scratch += [
             ("w", pltpu.VMEM((chunks, 2) + whole, bf16)),
@@ -1241,6 +1276,9 @@
             ("d", pltpu.VMEM((4, planes - 1) + lines[1:], bf16)),
             ("own", pltpu.VMEM((2,) + lines[1:], f32)),
             ("gout", pltpu.VMEM((6,) + lines[1:], f32)),
+            ("gains_in", pltpu.VMEM(gains.shape, f32)),
+            ("gains_end", pltpu.VMEM((8, LANES), f32)),
+            ("gains_sem", pltpu.SemaphoreType.DMA((2,))),
             ("gt", pltpu.VMEM((planes, 4, 16, LANES), bf16)),
             ("gain", pltpu.VMEM(gain_rows, f32)),
             ("gp", pltpu.VMEM((4,) + gain_rows, f32)),
@@ -1288,6 +1326,7 @@
         part = jnp.concatenate([part[mlp_chunks + 1 :], part[mlp_chunks:][:1], part[:mlp_chunks]])
         gain_part = lax.psum_scatter(gain_part[:2], "fsdp", scatter_dimension=1, tiled=True)
         gain_part = lax.psum(gain_part, "rep")
+        gain_part = jnp.pad(gain_part, ((0, 6), (0, LANES - shard_rows)))
 
     total_tokens = row_count * lax.axis_size("fsdp") * lax.axis_size("rep")
     rate = PEAK_RATE * STEP / (WARMUP * math.sqrt(total_tokens))
@@ -1300,27 +1339,23 @@
     kinds = ["attn", "mlp", "gains"]
     whats = ["grad", "next", "velocity", "average", "copy"]
     inputs = [("out_in", hbm, block_out), ("grad_in", hbm, input_grad), ("g", hbm, part)]
-    inputs += [("gain_part", vmem, gain_part)]
+    inputs += [("gain_part_in", hbm, gain_part)]
     outputs = [("block_out", hbm, block_out), ("input_grad", hbm, input_grad)]
     scratch = []
     for what, arrays in sources.items():
         for kind, array in zip(kinds, arrays, strict=True):
-            inputs.append((f"{kind}_{what}", vmem if kind == "gains" else hbm, array))
-            if kind != "gains":
-                scratch.append((f"{kind}_{what}_here", pltpu.VMEM(array.shape, f32)))
+            inputs.append((f"{kind}_{what}", hbm, array))
+            scratch.append((f"{kind}_{what}_here", pltpu.VMEM(array.shape, f32)))
     for what in whats:
         for kind, array in zip(kinds, sources["w"], strict=True):
             dtype = bf16 if what == "copy" else f32
-            place = vmem if kind == "gains" else hbm
-            outputs.append(
-                (f"{kind}_{what}", place, jax.ShapeDtypeStruct(array.shape, dtype))
-            )
-            if kind != "gains":
-                scratch.append((f"{kind}_{what}_here", pltpu.VMEM(array.shape, dtype)))
+            outputs.append((f"{kind}_{what}", hbm, jax.ShapeDtypeStruct(array.shape, dtype)))
+            scratch.append((f"{kind}_{what}_here", pltpu.VMEM(array.shape, dtype)))
     scratch += [
         ("g_here", pltpu.VMEM(part.shape, f32)),
-        ("in_sem", pltpu.SemaphoreType.DMA((4, 3))),
-        ("out_sem", pltpu.SemaphoreType.DMA((4, 5))),
+        ("gain_part", pltpu.VMEM(gain_part.shape, f32)),
+        ("in_sem", pltpu.SemaphoreType.DMA((5, 4))),
+        ("out_sem", pltpu.SemaphoreType.DMA((5, 5))),
         ("pass_here", pltpu.VMEM((2,) + block_out.shape, bf16)),
         ("pass_sem", pltpu.SemaphoreType.DMA((6,))),
     ]

time: 163 us -> 155 us (0.951)
  Pallas kernels: 162 us -> 154 us
    pallas_call x1, Pallas kernels: 153 us -> 146 us  [local(): pl.pallas_call(functools.partial(block_kernel, linked, names), out_shape=...]
where the time goes in v5:
time: 155 us
  Pallas kernels  154 us (99%)
    pallas_call x1, Pallas kernels, local(): pl.pallas_call(functools.partial(block_kernel, linked, names), out_shape=...  146 us
    pallas_call x1, Pallas kernels, local(): pl.pallas_call(functools.partial(update_kernel, rate, names), out_shape=[...  7.88 us

profile of v5, /device:TPU:0, one launch (start us, length us, event | category | flops | bytes accessed | tf_op | source)
XLA Modules:
  0.0 154.9 jit_solution(3190863624828594154)
XLA Ops:
  0.7 146.1 %block.1 = (bf16[1024,768]{1,0:T(8,128)(2,1)}, bf16[1024,768]{1,0:T(8,128)(2,1)}, f32[12,2,48,384]{3,2,1,0:T(8,128)}, f32[8,128]{1,0:T(8,128)}) custom-call(s32[1024]{0:T(1024)} %refs_0_.1, bf16[1024,768]{1,0:T(8,128)(2,1)} %refs_1_.1, bf16[1024,768]{1,0:T(8,128)(2,1)} %refs_2_.1, f32[256,256]{1,0:T(8,128)} %constant.2.clone.refs_3_, f32[48,3072]{1,0:T(8,128)} %refs_4_.3, ...), custom_call_target="tpu_custom_call" | custom-call | tf_op jit(solution)/shard_map/block/pallas_call | solution.py:1313
  146.8 7.9 %update.1 = (bf16[1024,768]{1,0:T(8,128)(2,1)}, bf16[1024,768]{1,0:T(8,128)(2,1)}, f32[48,3072]{1,0:T(8,128)}, f32[48,6144]{1,0:T(8,128)}, f32[2,48]{1,0:T(2,128...) custom-call(bf16[1024,768]{1,0:T(8,128)(2,1)} %get-tuple-element.21., ...), custom_call_target="tpu_custom_call" | custom-call | tf_op jit(solution)/shard_map/update/pallas_call | solution.py:1363

commit v6 on v5

--- a/solution.py
+++ b/solution.py
@@ -1321,8 +1321,8 @@
     )(*[entry[2] for entry in inputs])
 
     if not linked:
-        part = lax.psum_scatter(part, "fsdp", scatter_dimension=2, tiled=True)
-        part = lax.psum(part, "rep").astype(f32)
+        part = lax.psum_scatter(part.astype(f32), "fsdp", scatter_dimension=2, tiled=True)
+        part = lax.psum(part.astype(bf16), "rep").astype(f32)
         part = jnp.concatenate([part[mlp_chunks + 1 :], part[mlp_chunks:][:1], part[:mlp_chunks]])
         gain_part = lax.psum_scatter(gain_part[:2], "fsdp", scatter_dimension=1, tiled=True)
         gain_part = lax.psum(gain_part, "rep")

time: 155 us -> 155 us (level)
  no operation moved by 1% of the time
where the time goes in v6:
time: 155 us
  Pallas kernels  154 us (99%)
    pallas_call x1, Pallas kernels, local(): pl.pallas_call(functools.partial(block_kernel, linked, names), out_shape=...  146 us
    pallas_call x1, Pallas kernels, local(): pl.pallas_call(functools.partial(update_kernel, rate, names), out_shape=[...  7.88 us

profile of v6, /device:TPU:0, one launch (start us, length us, event | category | flops | bytes accessed | tf_op | source)
XLA Modules:
  0.0 154.9 jit_solution(3190863624828594154)
XLA Ops:
  0.7 146.1 %block.1 = (bf16[1024,768]{1,0:T(8,128)(2,1)}, bf16[1024,768]{1,0:T(8,128)(2,1)}, f32[12,2,48,384]{3,2,1,0:T(8,128)}, f32[8,128]{1,0:T(8,128)}) custom-call(s32[1024]{0:T(1024)} %refs_0_.1, bf16[1024,768]{1,0:T(8,128)(2,1)} %refs_1_.1, bf16[1024,768]{1,0:T(8,128)(2,1)} %refs_2_.1, f32[256,256]{1,0:T(8,128)} %constant.2.clone.refs_3_, f32[48,3072]{1,0:T(8,128)} %refs_4_.3, ...), custom_call_target="tpu_custom_call" | custom-call | tf_op jit(solution)/shard_map/block/pallas_call | solution.py:1313
  146.8 7.9 %update.1 = (bf16[1024,768]{1,0:T(8,128)(2,1)}, bf16[1024,768]{1,0:T(8,128)(2,1)}, f32[48,3072]{1,0:T(8,128)}, f32[48,6144]{1,0:T(8,128)}, f32[2,48]{1,0:T(2,128...) custom-call(bf16[1024,768]{1,0:T(8,128)(2,1)} %get-tuple-element.21., ...), custom_call_target="tpu_custom_call" | custom-call | tf_op jit(solution)/shard_map/update/pallas_call | solution.py:1363
